TPU v7x, 32 devices: a whole 2x2x4 slice. The times are simulated.
32 devices in a mesh: blk: 8 (over z, y), az: 4 (over x, core).
Axes of the slice: x: 2, y: 2, z: 4, core: 2. Of those that a mesh axis runs over, the one named last changes fastest.
Arguments:
- lower_part: float32 [8, 512, 512], P('blk', None, 'az'), may hold values from -0.02 to 0.02
- diag_part: float32 [8, 512, 512], P('blk', None, 'az'), may hold values from -0.02 to 0.02
- upper_part: float32 [8, 512, 512], P('blk', None, 'az'), may hold values from -0.02 to 0.02
- right_side: float32 [8, 512, 512], P('blk', None, 'az'), may hold values from -6 to 6
- extra: float32 [4096, 512], P('blk', 'az'), may hold values from -6 to 6
- owners: int32 [4096, 1], P('blk'), may hold values from 0 to 7; in each aligned block of 512 rows (0 to 511, 512 to 1023, ...) at most 128 rows name the same one
- rows_in: int32 [4096], P('blk'), may hold values from 0 to 511
- counts: int32 [8], P('blk'), may hold values from 384 to 512, as said below
Outputs:
- solution: float32 [8, 512, 512], P('blk', None, 'az')
Inputs may be any that keep to these rules, and one draw needn't show every extreme that they name: `owners`: within the 512 entries of one subdomain no block row is named more than 128 times; some subdomain names some block row exactly 128 times. `counts`: A subdomain's entries at positions below its count are live, the others are ignored; some subdomain has all 512 entries live.
All inputs are finite; a program needn't handle non-finite values.
Results may differ from a plain program's by a relative error of at most 0.00013.
Values sent between devices are 32-bit elements; how exact they have to be, the bound alone decides.
No kernel may reach another device: no remote copies, remote signals or barrier semaphores. Data moves between devices by JAX's collectives and lax.ppermute only.
A program may use at most 64 MiB of HBM per device.

v0:
```python
import jax
import jax.numpy as jnp
from jax import lax
from jax.sharding import PartitionSpec as P

coupling = 0.42


def passed_along(value, axis, steps):
    count = lax.axis_size(axis)
    pairs = [(source, (source + steps) % count) for source in range(count)]
    return lax.ppermute(value, axis, pairs)


def product(left, right):
    return jnp.dot(left, right, precision=lax.Precision.HIGHEST, preferred_element_type=jnp.float32)


def inverse_apply(diag_full, values):
    first_pass = 2.0 * values - product(diag_full, values)
    second_pass = 2.0 * values - product(diag_full, first_pass)
    return 2.0 * second_pass - product(diag_full, second_pass)


def deliver(extra, owners, rows_in, counts, block_order):
    cycle_size = lax.axis_size("blk")
    entries = owners.shape[0]
    slot_count = 2 * entries // cycle_size
    owner_ids = owners[:, 0]
    position = lax.iota(jnp.int32, entries)
    live_mask = position < counts[0]
    earlier_same = (
        (owner_ids[:, None] == owner_ids[None, :])
        & live_mask[None, :]
        & (position[None, :] < position[:, None])
    )
    slot_rank = jnp.sum(earlier_same.astype(jnp.int32), axis=1)
    target = jnp.where(live_mask, owner_ids * slot_count + slot_rank, cycle_size * slot_count)
    local_width = extra.shape[1]
    send_values = (
        jnp.zeros((cycle_size * slot_count, local_width), jnp.float32)
        .at[target]
        .set(extra, mode="drop")
    )
    row_marks = (
        jnp.full((cycle_size * slot_count,), -1.0, jnp.float32)
        .at[target]
        .set(rows_in.astype(jnp.float32), mode="drop")
    )
    got_values, got_marks = (
        lax.all_to_all(
            send_values.reshape(cycle_size, slot_count, local_width),
            "blk",
            split_axis=0,
            concat_axis=0,
            tiled=True,
        ),
        lax.all_to_all(
            row_marks.reshape(cycle_size, slot_count),
            "blk",
            split_axis=0,
            concat_axis=0,
            tiled=True,
        ),
    )
    got_values = got_values.reshape(cycle_size * slot_count, local_width)
    got_marks = got_marks.reshape(cycle_size * slot_count)
    row_grid = lax.broadcasted_iota(jnp.int32, (block_order, cycle_size * slot_count), 0).astype(
        jnp.float32
    )
    onehot = (row_grid == got_marks[None, :]).astype(jnp.float32)
    return product(onehot, got_values)


def on_device(lower_part, diag_part, upper_part, right_side, extra, owners, rows_in, counts):
    block_order = diag_part.shape[1]
    local_cols = diag_part.shape[2]
    cycle_size = lax.axis_size("blk")
    levels = min(4, 3 + cycle_size // 16)
    col_start = lax.axis_index("az") * local_cols
    row_grid = lax.broadcasted_iota(jnp.int32, (block_order, local_cols), 0)
    col_grid = lax.broadcasted_iota(jnp.int32, (block_order, local_cols), 1) + col_start
    eye_cols = (row_grid == col_grid).astype(jnp.float32)
    lower_block = lower_part[0] - coupling * eye_cols
    upper_block = upper_part[0] - coupling * eye_cols
    diag_block = diag_part[0] + eye_cols
    right_block = right_side[0] + deliver(extra, owners, rows_in, counts, block_order)
    stride = 1
    for level_index in range(levels):
        diag_full, lower_full, upper_full = (
            lax.all_gather(diag_block, "az", axis=1, tiled=True),
            lax.all_gather(lower_block, "az", axis=1, tiled=True),
            lax.all_gather(upper_block, "az", axis=1, tiled=True),
        )
        stacked = inverse_apply(
            diag_full, jnp.concatenate([lower_block, upper_block, right_block], axis=1)
        )
        from_lower = passed_along(stacked, "blk", stride)
        from_upper = passed_along(stacked, "blk", -stride)
        got_lower = product(lower_full, from_lower)
        got_upper = product(upper_full, from_upper)
        diag_block = (
            diag_block - got_lower[:, local_cols : 2 * local_cols] - got_upper[:, :local_cols]
        )
        right_block = right_block - got_lower[:, 2 * local_cols :] - got_upper[:, 2 * local_cols :]
        lower_block = -got_lower[:, :local_cols]
        upper_block = -got_upper[:, local_cols : 2 * local_cols]
        stride = stride * 2
    diag_full = lax.all_gather(diag_block, "az", axis=1, tiled=True)
    return inverse_apply(diag_full, right_block)[None]


def solution(mesh):
    placed = (
        P("blk", None, "az"),
        P("blk", None, "az"),
        P("blk", None, "az"),
        P("blk", None, "az"),
        P("blk", "az"),
        P("blk", None),
        P("blk"),
        P("blk"),
    )
    return jax.shard_map(
        on_device, mesh=mesh, in_specs=placed, out_specs=P("blk", None, "az"), check_vma=False
    )
```

profile of v0, /device:TPU:0, one launch (start us, length us, event | category | flops | bytes accessed | tf_op | source)
XLA Modules:
  0.0 251.4 jit_solution(17753921826284468014)
XLA Ops:
  11.7 3.0 %scatter_custom_fusion = f32[1024]{0:T(1024)} fusion(s32[512]{0:T(512)S(1)} %bitcast.57, f32[512]{0:T(512)S(1)} %convert_element_type.16, f32[]{:T(128)} %constant.8.clone.1), kind=kCustom, calls=%fused_computation.51 | custom fusion | bytes 4100 | tf_op jit(solution)/shard_map/scatter | solution.py:48
  14.7 7.3 %all-to-all-start = ((f32[8,1,128]{2,1,0:T(1,128)}), f32[8,1,128]{2,1,0:T(1,128)S(1)}, u32[]{:S(2)}, u32[]{:S(2)}) async-start(f32[8,1,128]{2,1,0:T(1,128)} %bitcast.5), calls=%async_computation | async-start | bytes 8192 | tf_op jit(solution)/shard_map/all_to_all | solution.py:58
  22.0 2.9 %scatter_custom_fusion.1 = f32[1024,128]{1,0:T(8,128)} fusion(s32[512]{0:T(512)S(1)} %bitcast.58, f32[512,128]{1,0:T(8,128)} %param.12, f32[]{:T(128)} %constant.12.clone.1), kind=kCustom, calls=%fused_computation.46 | custom fusion | bytes 524800 | tf_op jit(solution)/shard_map/scatter | solution.py:43
  24.9 3.6 %all-to-all-done = f32[8,1,128]{2,1,0:T(1,128)S(1)} async-done(((f32[8,1,128]{2,1,0:T(1,128)}), f32[8,1,128]{2,1,0:T(1,128)S(1)}, u32[]{:S(2)}, u32[]{:S(2)}) %all-to-all-start) | async-done | bytes 4128 | tf_op jit(solution)/shard_map/all_to_all | solution.py:58
  28.5 3.5 %all-to-all-start.1 = ((f32[8,128,128]{2,1,0:T(8,128)}), f32[8,128,128]{2,1,0:T(8,128)S(1)}, u32[]{:S(2)}, u32[]{:S(2)}) async-start(f32[8,128,128]{2,1,0:T(8,128)} %bitcast.7), calls=%async_computation.1 | async-start | bytes 1048576 | tf_op jit(solution)/shard_map/all_to_all | solution.py:51
  32.9 12.3 %all-to-all-done.1 = f32[8,128,128]{2,1,0:T(8,128)S(1)} async-done(((f32[8,128,128]{2,1,0:T(8,128)}), f32[8,128,128]{2,1,0:T(8,128)S(1)}, u32[]{:S(2)}, u32[]{:S(2)}) %all-to-all-start.1) | async-done | bytes 524320 | tf_op jit(solution)/shard_map/all_to_all | solution.py:51
  46.6 2.8 %convolution_subtract_fusion.8 = f32[512,384]{0,1:T(8,128)S(1)} fusion(f32[512,512]{0,1:T(8,128)} %all-gather.13.cloned.1.call-done, f32[512,128]{0,1:T(8,128)S(1)} %fusion.2, f32[512,128]{0,1:T(8,128)S(1)} %copy-done.8, f32[512,128]{0,1:T(8,128)S(1)} %copy-done.9), kind=kOutput, calls=%fused_computation.12 | convolution fusion | flops 1209139200 | bytes 2621440 | tf_op jit(solution)/shard_map/dot_general | solution.py:16
  52.4 1.5 collective-permute-start
  53.9 3.3 %collective-permute-start.1 = (f32[512,384]{0,1:T(8,128)S(1)}, f32[512,384]{0,1:T(8,128)S(1)}, u32[]{:S(2)}, u32[]{:S(2)}) collective-permute-start(f32[512,384]{0,1:T(8,128)S(1)} %convolution_subtract_fusion.6), channel_id=1, source_target_pairs={{0,28},{4,0},{8,4},{12,8},{16,12},{20,16},{24,20},{28,24},{1,29},{... | collective-permute-start | bytes 2359304 | tf_op jit(solution)/shard_map/ppermute | solution.py:12
  57.2 28.6 %collective-permute-done = f32[512,384]{0,1:T(8,128)} collective-permute-done((f32[512,384]{0,1:T(8,128)S(1)}, f32[512,384]{0,1:T(8,128)}, u32[]{:S(2)}, u32[]{:S(2)}) %collective-permute-start) | collective-permute-done | bytes 786464 | tf_op jit(solution)/shard_map/ppermute | solution.py:12
  85.8 2.9 %fusion.16 = f32[512,384]{0,1:T(8,128)S(1)} fusion(f32[512,512]{0,1:T(8,128)} %all-gather.11.cloned.1.call-done, f32[512,384]{0,1:T(8,128)} %collective-permute-done), kind=kOutput, calls=%fused_computation.58 | convolution fusion | flops 1207959552 | bytes 2621440 | tf_op jit(solution)/shard_map/dot_general | solution.py:16
  88.7 2.7 %fusion.17 = f32[512,384]{0,1:T(8,128)S(1)} fusion(f32[512,512]{0,1:T(8,128)} %all-gather.15.cloned.1.call-done, f32[512,384]{0,1:T(8,128)S(1)} %collective-permute-done.1), kind=kOutput, calls=%fused_computation.59 | convolution fusion | flops 1207959552 | bytes 2621440 | tf_op jit(solution)/shard_map/dot_general | solution.py:16
  93.7 17.0 %all-gather.19.cloned.1.call-done = f32[512,512]{0,1:T(8,128)} async-done(((f32[512,128]{0,1:T(8,128)}), f32[512,512]{0,1:T(8,128)}) %all-gather.19.cloned.1.call-update) | async-done | bytes 1048592 | tf_op jit(solution)/shard_map/all_gather | solution.py:91
  110.7 2.8 %convolution_subtract_fusion.5 = f32[512,384]{0,1:T(8,128)S(1)} fusion(f32[512,512]{0,1:T(8,128)} %all-gather.19.cloned.1.call-done, f32[512,128]{0,1:T(8,128)S(1)} %get-tuple-element.7, f32[512,128]{0,1:T(8,128)S(1)} %copy-done.4, f32[512,128]{0,1:T(8,128)S(1)} %copy-done.6), kind=kOutput, calls=%fused_computation.9 | convolution fusion | flops 1209139200 | bytes 2621440 | tf_op jit(solution)/shard_map/dot_general | solution.py:16
  113.5 1.5 convolution_subtract_fusion.4
  116.5 1.5 collective-permute-start.2
  118.1 2.3 collective-permute-start.3
  120.4 8.5 %all-gather.17.cloned.1.call-done = f32[512,512]{0,1:T(8,128)} async-done(((f32[512,128]{0,1:T(8,128)}), f32[512,512]{0,1:T(8,128)}) %all-gather.17.cloned.1.call-update) | async-done | bytes 1048592 | tf_op jit(solution)/shard_map/all_gather | solution.py:92
  128.8 10.0 %collective-permute-done.2 = f32[512,384]{0,1:T(8,128)} collective-permute-done((f32[512,384]{0,1:T(8,128)S(1)}, f32[512,384]{0,1:T(8,128)}, u32[]{:S(2)}, u32[]{:S(2)}) %collective-permute-start.2) | collective-permute-done | bytes 786464 | tf_op jit(solution)/shard_map/ppermute | solution.py:12
  138.9 2.9 %fusion.18 = f32[512,384]{0,1:T(8,128)S(1)} fusion(f32[512,512]{0,1:T(8,128)} %all-gather.17.cloned.1.call-done, f32[512,384]{0,1:T(8,128)} %collective-permute-done.2), kind=kOutput, calls=%fused_computation.60 | convolution fusion | flops 1207959552 | bytes 2621440 | tf_op jit(solution)/shard_map/dot_general | solution.py:16
  141.8 5.2 %all-gather.21.cloned.1.call-done = f32[512,512]{0,1:T(8,128)} async-done(((f32[512,128]{0,1:T(8,128)}), f32[512,512]{0,1:T(8,128)}) %all-gather.21.cloned.1.call-update) | async-done | bytes 1048592 | tf_op jit(solution)/shard_map/all_gather | solution.py:93
  147.0 7.3 %collective-permute-done.3 = f32[512,384]{0,1:T(8,128)S(1)} collective-permute-done((f32[512,384]{0,1:T(8,128)S(1)}, f32[512,384]{0,1:T(8,128)S(1)}, u32[]{:S(2)}, u32[]{:S(2)}) %collective-permute-start.3) | collective-permute-done | bytes 786464 | tf_op jit(solution)/shard_map/ppermute | solution.py:12
  154.3 2.7 %fusion.19 = f32[512,384]{0,1:T(8,128)S(1)} fusion(f32[512,512]{0,1:T(8,128)} %all-gather.21.cloned.1.call-done, f32[512,384]{0,1:T(8,128)S(1)} %collective-permute-done.3), kind=kOutput, calls=%fused_computation.61 | convolution fusion | flops 1207959552 | bytes 2621440 | tf_op jit(solution)/shard_map/dot_general | solution.py:16
  159.8 13.9 %all-gather.25.cloned.1.call-done = f32[512,512]{0,1:T(8,128)} async-done(((f32[512,128]{0,1:T(8,128)}), f32[512,512]{0,1:T(8,128)}) %all-gather.25.cloned.1.call-update) | async-done | bytes 1048592 | tf_op jit(solution)/shard_map/all_gather | solution.py:91
  173.7 2.8 %convolution_subtract_fusion.2 = f32[512,384]{0,1:T(8,128)S(1)} fusion(f32[512,512]{0,1:T(8,128)} %all-gather.25.cloned.1.call-done, f32[512,128]{0,1:T(8,128)S(1)} %get-tuple-element.5, f32[512,128]{0,1:T(8,128)S(1)} %copy-done.5, f32[512,128]{0,1:T(8,128)S(1)} %copy-done.7), kind=kOutput, calls=%fused_computation.6 | convolution fusion | flops 1209139200 | bytes 2621440 | tf_op jit(solution)/shard_map/dot_general | solution.py:16
  179.6 2.5 collective-permute-start.4
  182.0 10.0 %all-gather.23.cloned.1.call-done = f32[512,512]{0,1:T(8,128)} async-done(((f32[512,128]{0,1:T(8,128)}), f32[512,512]{0,1:T(8,128)}) %all-gather.23.cloned.1.call-update) | async-done | bytes 1048592 | tf_op jit(solution)/shard_map/all_gather | solution.py:92
  192.0 25.0 %collective-permute-done.4 = f32[512,384]{0,1:T(8,128)S(1)} collective-permute-done((f32[512,384]{0,1:T(8,128)S(1)}, f32[512,384]{0,1:T(8,128)S(1)}, u32[]{:S(2)}, u32[]{:S(2)}) %collective-permute-start.4) | collective-permute-done | bytes 786464 | tf_op jit(solution)/shard_map/ppermute | solution.py:12
  217.1 2.7 %fusion.20 = f32[512,384]{0,1:T(8,128)S(1)} fusion(f32[512,512]{0,1:T(8,128)} %all-gather.23.cloned.1.call-done, f32[512,384]{0,1:T(8,128)S(1)} %collective-permute-done.4), kind=kOutput, calls=%fused_computation.62 | convolution fusion | flops 1207959552 | bytes 2621440 | tf_op jit(solution)/shard_map/dot_general | solution.py:16
  219.8 2.7 %fusion.21 = f32[512,384]{0,1:T(8,128)S(1)} fusion(f32[512,512]{0,1:T(8,128)} %all-gather.27.cloned.1.call-done, f32[512,384]{0,1:T(8,128)S(1)} %collective-permute-done.4), kind=kOutput, calls=%fused_computation.63 | convolution fusion | flops 1207959552 | bytes 2621440 | tf_op jit(solution)/shard_map/dot_general | solution.py:16
  223.3 16.9 %all-gather.29.cloned.1.call-done = f32[512,512]{0,1:T(8,128)} async-done(((f32[512,128]{0,1:T(8,128)}), f32[512,512]{0,1:T(8,128)}) %all-gather.29.cloned.1.call-update) | async-done | bytes 1048592 | tf_op jit(solution)/shard_map/all_gather | solution.py:109
  240.2 2.0 convolution_subtract_fusion.11
  (82 shorter events, 22.1 us)
Async XLA Ops:
  6.5 40.0 %all-gather.13.cloned.1.call-start = ((), (), s32[]{:S(2)}) async-start(), calls=%async_computation.3 | async-start | bytes 1310720 | tf_op jit(solution)/shard_map/all_gather | solution.py:91
  8.9 2.5 copy-start.16
  8.9 2.5 copy-start.15
  10.0 47.2 %all-gather.11.cloned.1.call-start = ((), (), s32[]{:S(2)}) async-start(), calls=%async_computation.2 | async-start | bytes 1310720 | tf_op jit(solution)/shard_map/all_gather | solution.py:92
  10.0 22.7 %copy-start.14 = (f32[1,512,128]{2,1,0:T(8,128)S(1)}, f32[1,512,128]{2,1,0:T(8,128)}, u32[]{:S(2)}) copy-start(f32[1,512,128]{2,1,0:T(8,128)} %param.11) | copy-start | bytes 786436
  14.7 13.7 %all-to-all-start = ((f32[8,1,128]{2,1,0:T(1,128)}), f32[8,1,128]{2,1,0:T(1,128)S(1)}, u32[]{:S(2)}, u32[]{:S(2)}) async-start(f32[8,1,128]{2,1,0:T(1,128)} %bitcast.5), calls=%async_computation | async-start | bytes 8192 | tf_op jit(solution)/shard_map/all_to_all | solution.py:58
  28.5 16.7 %all-to-all-start.1 = ((f32[8,128,128]{2,1,0:T(8,128)}), f32[8,128,128]{2,1,0:T(8,128)S(1)}, u32[]{:S(2)}, u32[]{:S(2)}) async-start(f32[8,128,128]{2,1,0:T(8,128)} %bitcast.7), calls=%async_computation.1 | async-start | bytes 1048576 | tf_op jit(solution)/shard_map/all_to_all | solution.py:51
  32.0 14.6 %copy-start.8 = (f32[512,128]{0,1:T(8,128)S(1)}, f32[512,128]{0,1:T(8,128)}, u32[]{:S(2)}) copy-start(f32[512,128]{0,1:T(8,128)} %get-tuple-element.14) | copy-start | bytes 786436
  32.0 14.6 %copy-start.9 = (f32[512,128]{0,1:T(8,128)S(1)}, f32[512,128]{0,1:T(8,128)}, u32[]{:S(2)}) copy-start(f32[512,128]{0,1:T(8,128)} %get-tuple-element.13) | copy-start | bytes 786436
  32.0 56.7 %all-gather.15.cloned.1.call-start = ((), (), s32[]{:S(2)}) async-start(), calls=%async_computation.4 | async-start | bytes 1310720 | tf_op jit(solution)/shard_map/all_gather | solution.py:93
  32.7 77.9 %all-gather.19.cloned.1.call-start = ((), (), s32[]{:S(2)}) async-start(), calls=%async_computation.6 | async-start | bytes 1310720 | tf_op jit(solution)/shard_map/all_gather | solution.py:91
  46.5 2.8 %copy-start = (f32[512,512]{0,1:T(8,128)S(1)}, f32[512,512]{0,1:T(8,128)}, u32[]{:S(2)}) copy-start(f32[512,512]{0,1:T(8,128)} %all-gather.13.cloned.1.call-done) | copy-start | bytes 3145732
  52.4 33.4 %collective-permute-start = (f32[512,384]{0,1:T(8,128)S(1)}, f32[512,384]{0,1:T(8,128)}, u32[]{:S(2)}, u32[]{:S(2)}) collective-permute-start(f32[512,384]{0,1:T(8,128)S(1)} %convolution_subtract_fusion.6), channel_id=1, source_target_pairs={{0,4},{4,8},{8,12},{12,16},{16,20},{20,24},{24,28},{28,0},{1,5},{5... | collective-permute-start | bytes 2359304 | tf_op jit(solution)/shard_map/ppermute | solution.py:12
  53.9 34.8 %collective-permute-start.1 = (f32[512,384]{0,1:T(8,128)S(1)}, f32[512,384]{0,1:T(8,128)S(1)}, u32[]{:S(2)}, u32[]{:S(2)}) collective-permute-start(f32[512,384]{0,1:T(8,128)S(1)} %convolution_subtract_fusion.6), channel_id=1, source_target_pairs={{0,28},{4,0},{8,4},{12,8},{16,12},{20,16},{24,20},{28,24},{1,29},{... | collective-permute-start | bytes 2359304 | tf_op jit(solution)/shard_map/ppermute | solution.py:12
  88.7 2.8 %copy-start.11 = (f32[512,128]{0,1:T(8,128)S(1)}, f32[512,128]{0,1:T(8,128)}, u32[]{:S(2)}) copy-start(f32[512,128]{0,1:T(8,128)} %get-tuple-element.15) | copy-start | bytes 786436
  92.5 18.2 %copy-start.4 = (f32[512,128]{0,1:T(8,128)S(1)}, f32[512,128]{0,1:T(8,128)}, u32[]{:S(2)}) copy-start(f32[512,128]{0,1:T(8,128)} %get-tuple-element.12) | copy-start | bytes 786436
  92.5 18.2 %copy-start.6 = (f32[512,128]{0,1:T(8,128)S(1)}, f32[512,128]{0,1:T(8,128)}, u32[]{:S(2)}) copy-start(f32[512,128]{0,1:T(8,128)} %get-tuple-element.11) | copy-start | bytes 786436
  92.5 36.3 %all-gather.17.cloned.1.call-start = ((), (), s32[]{:S(2)}) async-start(), calls=%async_computation.5 | async-start | bytes 1310720 | tf_op jit(solution)/shard_map/all_gather | solution.py:92
  93.1 53.9 %all-gather.21.cloned.1.call-start = ((), (), s32[]{:S(2)}) async-start(), calls=%async_computation.7 | async-start | bytes 1310720 | tf_op jit(solution)/shard_map/all_gather | solution.py:93
  93.7 80.0 %all-gather.25.cloned.1.call-start = ((), (), s32[]{:S(2)}) async-start(), calls=%async_computation.9 | async-start | bytes 1310720 | tf_op jit(solution)/shard_map/all_gather | solution.py:91
  110.7 2.8 %copy-start.1 = (f32[512,512]{0,1:T(8,128)S(1)}, f32[512,512]{0,1:T(8,128)}, u32[]{:S(2)}) copy-start(f32[512,512]{0,1:T(8,128)} %all-gather.19.cloned.1.call-done) | copy-start | bytes 3145732
  116.5 22.4 %collective-permute-start.2 = (f32[512,384]{0,1:T(8,128)S(1)}, f32[512,384]{0,1:T(8,128)}, u32[]{:S(2)}, u32[]{:S(2)}) collective-permute-start(f32[512,384]{0,1:T(8,128)S(1)} %convolution_subtract_fusion.3), channel_id=1, source_target_pairs={{0,8},{4,12},{8,16},{12,20},{16,24},{20,28},{24,0},{28,4},{1,9},{5... | collective-permute-start | bytes 2359304 | tf_op jit(solution)/shard_map/ppermute | solution.py:12
  118.1 36.3 %collective-permute-start.3 = (f32[512,384]{0,1:T(8,128)S(1)}, f32[512,384]{0,1:T(8,128)S(1)}, u32[]{:S(2)}, u32[]{:S(2)}) collective-permute-start(f32[512,384]{0,1:T(8,128)S(1)} %convolution_subtract_fusion.3), channel_id=1, source_target_pairs={{0,24},{4,28},{8,0},{12,4},{16,8},{20,12},{24,16},{28,20},{1,25},{... | collective-permute-start | bytes 2359304 | tf_op jit(solution)/shard_map/ppermute | solution.py:12
  141.8 15.2 %copy-start.10 = (f32[512,128]{0,1:T(8,128)S(1)}, f32[512,128]{0,1:T(8,128)}, u32[]{:S(2)}) copy-start(f32[512,128]{0,1:T(8,128)} %get-tuple-element.8) | copy-start | bytes 786436
  158.0 15.7 %copy-start.5 = (f32[512,128]{0,1:T(8,128)S(1)}, f32[512,128]{0,1:T(8,128)}, u32[]{:S(2)}) copy-start(f32[512,128]{0,1:T(8,128)} %get-tuple-element.10) | copy-start | bytes 786436
  158.0 15.7 %copy-start.7 = (f32[512,128]{0,1:T(8,128)S(1)}, f32[512,128]{0,1:T(8,128)}, u32[]{:S(2)}) copy-start(f32[512,128]{0,1:T(8,128)} %get-tuple-element.9) | copy-start | bytes 786436
  158.0 34.0 %all-gather.23.cloned.1.call-start = ((), (), s32[]{:S(2)}) async-start(), calls=%async_computation.8 | async-start | bytes 1310720 | tf_op jit(solution)/shard_map/all_gather | solution.py:92
  158.8 61.0 %all-gather.27.cloned.1.call-start = ((), (), s32[]{:S(2)}) async-start(), calls=%async_computation.10 | async-start | bytes 1310720 | tf_op jit(solution)/shard_map/all_gather | solution.py:93
  159.5 80.7 %all-gather.29.cloned.1.call-start = ((), (), s32[]{:S(2)}) async-start(), calls=%async_computation.11 | async-start | bytes 1310720 | tf_op jit(solution)/shard_map/all_gather | solution.py:109
  173.7 2.8 %copy-start.2 = (f32[512,512]{0,1:T(8,128)S(1)}, f32[512,512]{0,1:T(8,128)}, u32[]{:S(2)}) copy-start(f32[512,512]{0,1:T(8,128)} %all-gather.25.cloned.1.call-done) | copy-start | bytes 3145732
  179.6 37.5 %collective-permute-start.4 = (f32[512,384]{0,1:T(8,128)S(1)}, f32[512,384]{0,1:T(8,128)S(1)}, u32[]{:S(2)}, u32[]{:S(2)}) collective-permute-start(f32[512,384]{0,1:T(8,128)S(1)} %convolution_subtract_fusion), channel_id=1, source_target_pairs={{0,16},{4,20},{8,24},{12,28},{16,0},{20,4},{24,8},{28,12},{1,17},{... | collective-permute-start | bytes 2359304 | tf_op jit(solution)/shard_map/ppermute | solution.py:12
  219.8 2.8 %copy-start.12 = (f32[512,128]{0,1:T(8,128)S(1)}, f32[512,128]{0,1:T(8,128)}, u32[]{:S(2)}) copy-start(f32[512,128]{0,1:T(8,128)} %get-tuple-element.6) | copy-start | bytes 786436
  (2 other events, 4.3 us)
Sparse Core Ops, SparseCore 0:
  10.1 19.4 all-gather.12
  31.1 16.7 all-gather.10
  49.4 16.7 all-gather.14
  92.6 17.9 all-gather.18
  112.1 16.7 all-gather.16
  130.3 16.7 all-gather.20
  158.2 15.5 all-gather.24
  175.3 16.7 all-gather.22
  193.6 16.7 all-gather.26
  223.5 16.6 all-gather.28
where the time goes:
time: 252 us; the launch traced here: 251 us
  waiting for transfers between devices  162 us (64%)
  matrix products  38.8 us (15%)
  starting transfers between devices  22.5 us (9%)
  between operations  14.6 us (6%)
  local copies, waits for them, and re-layouts  9.24 us (4%)
  other arithmetic  4.07 us (2%)
    ppermute x5, waiting for transfers between devices, passed_along(): return lax.ppermute(value, axis, pairs)  70.9 us
    dot_general x19, matrix products, product(): jnp.dot(left, right, precision=lax.Precision.HIGHEST, preferred_element_t...  38.8 us
    all_gather x3, waiting for transfers between devices, on_device(): lax.all_gather(diag_block, 'az', axis=1, tiled=True)  30.9 us
    all_gather x3, waiting for transfers between devices, on_device(): lax.all_gather(lower_block, 'az', axis=1, tiled=True)  18.5 us
    all_gather x1, waiting for transfers between devices, on_device(): diag_full = lax.all_gather(diag_block, 'az', axis=1, tiled=True)  16.9 us
    all_to_all x1, waiting for transfers between devices, deliver(): lax.all_to_all(send_values.reshape(cycle_size, slot_count, local_width),...  12.3 us
    ppermute x5, starting transfers between devices, passed_along(): return lax.ppermute(value, axis, pairs)  11.1 us
    all_to_all x1, starting transfers between devices, deliver(): lax.all_to_all(row_marks.reshape(cycle_size, slot_count), 'blk', split_ax...  7.28 us
  transfers between devices with their start and end apart: 17, of which 12 were waited for; matrix products, arithmetic and copies ran while one was open for 13% of the time, Pallas kernels for 0%

commit v1 on v0

v1 whole, which is shorter than its diff:
```python
import functools

import jax
import jax.numpy as jnp
from jax import lax
from jax.experimental import pallas as pl
from jax.experimental.pallas import tpu as pltpu
from jax.sharding import PartitionSpec as P

coupling = 0.42
mark_rows = 8
f32 = jnp.float32
bf16 = jnp.bfloat16
in_vmem = pl.BlockSpec(memory_space=pltpu.VMEM)
in_smem = pl.BlockSpec(memory_space=pltpu.SMEM)


def send(value, axis, target_of):
    pairs = [(source, target_of(source)) for source in range(lax.axis_size(axis))]
    return lax.ppermute(value, axis, pairs)


def halves(value):
    high = value.astype(bf16)
    return high, (value - high.astype(f32)).astype(bf16)


def dot(left, right):
    return jnp.dot(left, right, preferred_element_type=f32)


def three_pass(left_high, left_low, right):
    high, low = halves(right)
    return dot(left_high[...], high) + (dot(left_high[...], low) + dot(left_low[...], high))


def row_starts(place, shards, width):
    return [pl.multiple_of((place ^ k) * width, width) for k in range(shards)]


def load_rows(ref, starts, width):
    return jnp.concatenate([ref[pl.ds(start, width), :] for start in starts], axis=0)


def store_rows(ref, starts, width, value):
    for k, start in enumerate(starts):
        ref[pl.ds(start, width), :] = value[k * width : (k + 1) * width, :]


def unit(width):
    rows = lax.broadcasted_iota(jnp.int32, (width, width), 0)
    cols = lax.broadcasted_iota(jnp.int32, (width, width), 1)
    return (rows == cols).astype(f32)


def assemble(high, low, shard_of, starts, width, shift):
    for k in range(len(starts)):
        for g, start in enumerate(starts):
            piece = shard_of(k, start)
            if shift and g == k:
                piece = piece - shift * unit(width)
            at = (slice(g * width, (g + 1) * width), slice(k * width, (k + 1) * width))
            high[at], low[at] = halves(piece)


def shifted(value, width, shift):
    if not shift:
        return value
    return jnp.concatenate([value[:width] - shift * unit(width), value[width:]], axis=0)


def apply_kernel(shards, shift, swap, place, *refs):
    n_refs, v_refs = refs[:shards], refs[shards:-3]
    count = len(v_refs) // 2
    v_refs, o_refs = v_refs[:count], v_refs[count:]
    high, low = refs[-3:-1]
    width = v_refs[0].shape[1]
    starts = row_starts(place[0], shards, width)
    assemble(high, low, lambda k, s: n_refs[k][pl.ds(s, width), :], starts, width, 0)
    values = [shifted(load_rows(ref, starts, width), width, shift) for ref in v_refs]
    if swap:
        even = place[1] == 0
        values = [jnp.where(even, values[0], values[1]), jnp.where(even, values[1], values[0])]
    value = jnp.concatenate(values, axis=1)
    second = value + three_pass(high, low, three_pass(high, low, value))
    result = second - three_pass(high, low, second)
    for k, ref in enumerate(o_refs):
        store_rows(ref, starts, width, result[:, k * width : (k + 1) * width])


def compiler_params(megabytes):
    return pltpu.CompilerParams(vmem_limit_bytes=megabytes * 2**20)


def inverse_apply(place, n_shards, values, shift=0, swap=False):
    order, width = values[0].shape
    shards = len(n_shards)
    columns = width * len(values)
    return pl.pallas_call(
        functools.partial(apply_kernel, shards, shift, swap),
        out_shape=[jax.ShapeDtypeStruct((order, width), f32)] * len(values),
        in_specs=[in_smem] + [in_vmem] * (shards + len(values)),
        out_specs=[in_vmem] * len(values),
        scratch_shapes=[pltpu.VMEM((order, order), bf16)] * 2 + [pltpu.VMEM((8, 128), f32)],
        compiler_params=compiler_params(24),
        cost_estimate=pl.CostEstimate(
            flops=18 * order * order * columns,
            bytes_accessed=4 * order * (order + 2 * columns),
            transcendentals=0,
        ),
    )(place, *n_shards, *values)


def combine_kernel(shards, shift, swap, bases, pairs, singles, place, *refs):
    refs = list(refs)
    take = lambda n: [refs.pop(0) for _ in range(n)]
    one_refs, two_refs = take(shards), take(shards)
    base_refs, pair_refs, single_refs = take(bases), take(2 * pairs), take(2 * singles)
    o_refs = take(pairs + 2 * singles)
    scratch = take(4)
    width = one_refs[0].shape[1]
    starts = row_starts(place[0], shards, width)
    results = []
    for m, (high, low) in enumerate((scratch[:2], scratch[2:])):
        mine, other = (one_refs, two_refs) if m == 0 else (two_refs, one_refs)
        if swap:
            even = place[1] == 0
            shard_of = lambda k, s, mine=mine, other=other: jnp.where(
                even, mine[k][pl.ds(s, width), :], other[k][pl.ds(s, width), :]
            )
        else:
            shard_of = lambda k, s, mine=mine: mine[k][pl.ds(s, width), :]
        assemble(high, low, shard_of, starts, width, shift)
        rights = [load_rows(ref, starts, width) for ref in pair_refs[m::2] + single_refs[m::2]]
        right = jnp.concatenate(rights, axis=1) if len(rights) > 1 else rights[0]
        results.append(three_pass(high, low, right))
    part = lambda m, j: results[m][:, j * width : (j + 1) * width]
    for j in range(pairs):
        base = load_rows(base_refs[j], starts, width)
        store_rows(o_refs[j], starts, width, base - part(0, j) - part(1, j))
    for j in range(singles):
        for m in range(2):
            store_rows(o_refs[pairs + 2 * j + m], starts, width, -part(m, pairs + j))


def combine(place, one_shards, two_shards, base_pairs, single_pairs, shift=0, swap=False):
    order, width = one_shards[0].shape
    shards = len(one_shards)
    bases = [base for base, _, _ in base_pairs]
    rights = [v for _, a, b in base_pairs for v in (a, b)] + [v for pair in single_pairs for v in pair]
    outs = len(base_pairs) + 2 * len(single_pairs)
    return pl.pallas_call(
        functools.partial(
            combine_kernel, shards, shift, swap, len(bases), len(base_pairs), len(single_pairs)
        ),
        out_shape=[jax.ShapeDtypeStruct((order, width), f32)] * outs,
        in_specs=[in_smem] + [in_vmem] * (2 * shards + len(bases) + len(rights)),
        out_specs=[in_vmem] * outs,
        scratch_shapes=[pltpu.VMEM((order, order), bf16)] * 4,
        compiler_params=compiler_params(24),
        cost_estimate=pl.CostEstimate(
            flops=6 * order * order * width * len(rights),
            bytes_accessed=4 * order * (2 * order + 2 * width * len(rights)),
            transcendentals=0,
        ),
    )(place, *one_shards, *two_shards, *bases, *rights)


def slots_kernel(cycle_size, slot_count, counts, owner_row, rows_row, extra, out):
    entries, width = extra.shape
    position = lax.broadcasted_iota(jnp.int32, (1, entries), 1)
    live = position < counts[0]
    owner = jnp.where(live, owner_row[...], cycle_size)
    blocks = lax.broadcasted_iota(jnp.int32, (cycle_size, entries), 0)
    owned = (blocks == owner).astype(f32)
    before = lax.broadcasted_iota(jnp.int32, (entries, entries), 0)
    after = lax.broadcasted_iota(jnp.int32, (entries, entries), 1)
    earlier = dot(owned.astype(bf16), (before < after).astype(f32).astype(bf16))
    rank = jnp.sum(owned * earlier, axis=0, keepdims=True).astype(jnp.int32)
    high, low = halves(extra[...])
    both = jnp.concatenate([high, low], axis=1)
    slots = lax.broadcasted_iota(jnp.int32, (slot_count, entries), 0)
    in_slot = (slots == rank).astype(f32)
    mark_high, mark_low = halves(owned * (rows_row[...] + 1).astype(f32))
    to_slot = lambda mark: lax.dot_general(
        mark, in_slot.astype(bf16), (((1,), (1,)), ((), ())), preferred_element_type=f32
    )
    marks = to_slot(mark_high) + to_slot(mark_low)
    stride = slot_count + mark_rows
    for block in range(cycle_size):
        chosen = jnp.where(owner == block, in_slot, 0.0).astype(bf16)
        found = dot(chosen, both)
        out[block * stride : block * stride + slot_count, :] = found[:, :width] + found[:, width:]
        out[block * stride + slot_count : (block + 1) * stride, :] = jnp.zeros((mark_rows, width), f32)
        out[block * stride + slot_count : block * stride + slot_count + 1, :slot_count] = marks[
            block : block + 1, :
        ]


def load_kernel(cycle_size, slot_count, right_side, got, out):
    order, width = right_side.shape
    stride = slot_count + mark_rows
    total = right_side[...]
    rows = (lax.broadcasted_iota(jnp.int32, (order, slot_count), 0) + 1).astype(f32)
    for block in range(cycle_size):
        high, low = halves(got[block * stride : block * stride + slot_count, :])
        marks = got[block * stride + slot_count : block * stride + slot_count + 1, :slot_count]
        found = dot((rows == marks).astype(f32).astype(bf16), jnp.concatenate([high, low], axis=1))
        total = total + (found[:, :width] + found[:, width:])
    out[...] = total


def deliver(right_side, extra, owners, rows_in, counts):
    cycle_size = lax.axis_size("blk")
    entries, width = extra.shape
    order = right_side.shape[0]
    slot_count = 2 * entries // cycle_size
    stride = slot_count + mark_rows
    sent = pl.pallas_call(
        functools.partial(slots_kernel, cycle_size, slot_count),
        out_shape=jax.ShapeDtypeStruct((cycle_size * stride, width), f32),
        in_specs=[in_smem] + [in_vmem] * 3,
        out_specs=in_vmem,
        compiler_params=compiler_params(24),
    )(counts, owners.reshape(1, entries), rows_in.reshape(1, entries), extra)
    got = lax.all_to_all(
        sent.reshape(cycle_size, stride, width), "blk", split_axis=0, concat_axis=0, tiled=True
    )
    return pl.pallas_call(
        functools.partial(load_kernel, cycle_size, slot_count),
        out_shape=jax.ShapeDtypeStruct((order, width), f32),
        in_specs=[in_vmem] * 2,
        out_specs=in_vmem,
        compiler_params=compiler_params(24),
    )(right_side, got.reshape(cycle_size * stride, width))


def gathered(value):
    bit = lax.axis_size("az") // 2
    shards = {0: value}
    while bit:
        for k in list(shards):
            shards[k | bit] = send(shards[k], "az", lambda source, bit=bit: source ^ bit)
        bit //= 2
    return [shards[k] for k in range(len(shards))]


def on_device(lower_part, diag_part, upper_part, right_side, extra, owners, rows_in, counts):
    cycle_size = lax.axis_size("blk")
    levels = min(4, 3 + cycle_size // 16)
    place = jnp.stack([lax.axis_index("az"), lax.axis_index("blk") % 2]).astype(jnp.int32)
    even = place[1] == 0
    lower, diag, upper = lower_part[0], diag_part[0], upper_part[0]

    n_shards = gathered(diag)
    l_shards, u_shards = gathered(lower), gathered(upper)
    right = deliver(right_side[0], extra, owners, rows_in, counts)

    partner = lambda source: source ^ 1
    onward = lambda source: (source + 2 - 4 * (source % 2)) % cycle_size
    first, second = inverse_apply(place, n_shards, [lower, upper], shift=coupling, swap=True)
    near_first = send(first, "blk", partner)
    near_second = send(second, "blk", partner)
    far_first = send(near_first, "blk", onward)
    (diag,) = combine(
        place, l_shards, u_shards, [(diag, far_first, near_second)], [], shift=coupling, swap=True
    )
    n_next = gathered(diag)
    far_second = send(near_second, "blk", onward)
    one, two = combine(
        place, l_shards, u_shards, [], [(far_second, near_first)], shift=coupling, swap=True
    )
    (solved,) = inverse_apply(place, n_shards, [right])
    near_solved = send(solved, "blk", partner)
    far_solved = send(near_solved, "blk", onward)
    (right,) = combine(
        place, l_shards, u_shards, [(right, far_solved, near_solved)], [], shift=coupling, swap=True
    )
    lower, upper = jnp.where(even, one, two), jnp.where(even, two, one)

    stride = 2
    for level in range(1, levels):
        n_shards = n_next
        l_shards, u_shards = gathered(lower), gathered(upper)
        ahead = lambda source: (source + stride) % cycle_size
        back = lambda source: (source - stride) % cycle_size
        last = level == levels - 1
        p_row, q_row = inverse_apply(place, n_shards, [lower, upper])
        low_q, up_p = send(q_row, "blk", ahead), send(p_row, "blk", back)
        (diag,) = combine(place, l_shards, u_shards, [(diag, low_q, up_p)], [])
        n_next = gathered(diag)
        (solved,) = inverse_apply(place, n_shards, [right])
        if not last:
            low_p, up_q = send(p_row, "blk", ahead), send(q_row, "blk", back)
            lower, upper = combine(place, l_shards, u_shards, [], [(low_p, up_q)])
        low_y = send(solved, "blk", ahead)
        up_y = low_y if 2 * stride == cycle_size else send(solved, "blk", back)
        (right,) = combine(place, l_shards, u_shards, [(right, low_y, up_y)], [])
        stride = 2 * stride
    (result,) = inverse_apply(place, n_next, [right])
    return result[None]


def solution(mesh):
    placed = (
        P("blk", None, "az"),
        P("blk", None, "az"),
        P("blk", None, "az"),
        P("blk", None, "az"),
        P("blk", "az"),
        P("blk", None),
        P("blk"),
        P("blk"),
    )
    return jax.shard_map(
        on_device, mesh=mesh, in_specs=placed, out_specs=P("blk", None, "az"), check_vma=False
    )
```

time: 252 us -> 174 us (0.69)
  waiting for transfers between devices: 162 us -> 78.9 us
  Pallas kernels: 0 us -> 43 us
  matrix products: 38.8 us -> 0 us
  starting transfers between devices: 22.5 us -> 46.4 us
  between operations: 14.6 us -> 1.08 us
  local copies, waits for them, and re-layouts: 9.24 us -> 3.69 us
  other arithmetic: 4.07 us -> 0.11 us
    all_gather x10 -> x0, waiting for transfers between devices: 71.5 us -> none  [the longest x3 30.9 us: on_device(): lax.all_gather(diag_block, 'az', axis=1, tiled=True)]
    pallas_call x0 -> x17, Pallas kernels: none -> 43 us  [the longest x7 23.3 us: inverse_apply(): pl.pallas_call(functools.partial(apply_kernel, shards, shift, swap), out_...]
    dot_general x19 -> x0, matrix products: 38.8 us -> none  [product(): jnp.dot(left, right, precision=lax.Precision.HIGHEST, preferred_element_t...]
    ppermute x5 -> x45, starting transfers between devices: 11.1 us -> 41.4 us  [send(): return lax.ppermute(value, axis, pairs)]
    all_to_all x2 -> x1, waiting for transfers between devices: 15.9 us -> 0.01 us  [deliver(): lax.all_to_all(sent.reshape(cycle_size, stride, width), 'blk', split_axis...]
    ppermute x5 -> x45, waiting for transfers between devices: 70.9 us -> 78.9 us  [send(): return lax.ppermute(value, axis, pairs)]
    scatter x2 -> x0, local copies, waits for them, and re-layouts: 5.87 us -> none  [the longest x1 3 us: deliver(): row_marks = jnp.full((cycle_size * slot_count,), -1.0, jnp.float32).at[ta...]
    all_to_all x2 -> x1, starting transfers between devices: 10.8 us -> 4.95 us  [deliver(): lax.all_to_all(sent.reshape(cycle_size, stride, width), 'blk', split_axis...]
  transfers between devices with their start and end apart: 17 -> 46, of which waited for: 12 -> 15; matrix products, arithmetic and copies ran while one was open for 13% -> 0% of each run, Pallas kernels for 0% -> 23%
where the time goes in v1:
time: 174 us; the launch traced here: 173 us
  waiting for transfers between devices  78.9 us (45%)
  starting transfers between devices  46.4 us (27%)
  Pallas kernels  43 us (25%)
  local copies, waits for them, and re-layouts  3.69 us (2%)
    ppermute x45, waiting for transfers between devices, send(): return lax.ppermute(value, axis, pairs)  78.9 us
    ppermute x45, starting transfers between devices, send(): return lax.ppermute(value, axis, pairs)  41.4 us
    pallas_call x7, Pallas kernels, inverse_apply(): pl.pallas_call(functools.partial(apply_kernel, shards, shift, swap), out_...  23.3 us
    pallas_call x8, Pallas kernels, combine(): pl.pallas_call(functools.partial(combine_kernel, shards, shift, swap, len...  16.4 us
    all_to_all x1, starting transfers between devices, deliver(): lax.all_to_all(sent.reshape(cycle_size, stride, width), 'blk', split_axis...  4.95 us
    unnamed x54, local copies, waits for them, and re-layouts  3.69 us
  transfers between devices with their start and end apart: 46, of which 15 were waited for; matrix products, arithmetic and copies ran while one was open for 0% of the time, Pallas kernels for 23%

profile of v1, /device:TPU:0, one launch (start us, length us, event | category | flops | bytes accessed | tf_op | source)
XLA Modules:
  0.0 173.2 jit_solution(12846265758322745914)
XLA Ops:
  0.0 2.9 %collective-permute-start.7 = (f32[512,128]{1,0:T(8,128)}, f32[512,128]{1,0:T(8,128)S(1)}, u32[]{:S(2)}, u32[]{:S(2)}) collective-permute-start(f32[512,128]{1,0:T(8,128)} %bitcast.18), channel_id=1, source_target_pairs={{0,2},{1,3},{2,0},{3,1},{4,6},{5,7},{6,4},{7,5},{8,10},{9,11},{10,... | collective-permute-start | bytes 786440 | tf_op jit(solution)/shard_map/ppermute | solution.py:20
  2.9 6.5 %collective-permute-done.7.refs_2_ = f32[512,128]{1,0:T(8,128)S(1)} collective-permute-done((f32[512,128]{1,0:T(8,128)}, f32[512,128]{1,0:T(8,128)S(1)}, u32[]{:S(2)}, u32[]{:S(2)}) %collective-permute-start.7) | collective-permute-done | bytes 262176 | tf_op jit(solution)/shard_map/ppermute | solution.py:20
  13.8 3.4 %shard_map.82 = (f32[512,128]{1,0:T(8,128)S(1)}, f32[512,128]{1,0:T(8,128)S(1)}) custom-call(s32[2]{0:T(128)S(1)} %pad_add_fusion.place, f32[512,128]{1,0:T(8,128)S(1)} %bitcast.20, f32[512,128]{1,0:T(8,128)S(1)} %collective-permute-done.6.refs_1_, f32[512,128]{1,0:T(8,128)S(1)} %collective-permute-done.7.refs_2_, ...), custom_call_target="tpu_custom_call" | custom-call | flops 1207959552 | bytes 2097152 | tf_op jit(solution)/shard_map/pallas_call | solution.py:99
  19.4 4.6 %collective-permute-done.4.refs_6_ = f32[512,128]{1,0:T(8,128)S(1)} collective-permute-done((f32[512,128]{1,0:T(8,128)}, f32[512,128]{1,0:T(8,128)S(1)}, u32[]{:S(2)}, u32[]{:S(2)}) %collective-permute-start.4) | collective-permute-done | bytes 262176 | tf_op jit(solution)/shard_map/ppermute | solution.py:20
  28.3 2.9 %collective-permute-done.9.refs_10_ = f32[512,128]{1,0:T(8,128)S(1)} collective-permute-done((f32[512,128]{1,0:T(8,128)S(1)}, f32[512,128]{1,0:T(8,128)S(1)}, u32[]{:S(2)}, u32[]{:S(2)}) %collective-permute-start.9) | collective-permute-done | bytes 262176 | tf_op jit(solution)/shard_map/ppermute | solution.py:20
  35.9 5.0 %all-to-all-start = ((f32[8,136,128]{2,1,0:T(8,128)}), f32[8,136,128]{2,1,0:T(8,128)}, u32[]{:S(2)}, u32[]{:S(2)}) async-start(f32[8,136,128]{2,1,0:T(8,128)} %bitcast.8), calls=%async_computation | async-start | bytes 1114112 | tf_op jit(solution)/shard_map/all_to_all | solution.py:226
  40.9 2.2 %shard_map.84.refs_0_.refs_8_ = f32[512,128]{1,0:T(8,128)S(1)} custom-call(s32[2]{0:T(128)S(1)} %pad_add_fusion.place, f32[512,128]{1,0:T(8,128)S(1)} %bitcast.14, f32[512,128]{1,0:T(8,128)S(1)} %collective-permute-done.refs_1_, f32[512,128]{1,0:T(8,128)S(1)} %collective-permute-done.1.refs_2_, f32[512,128]{1,0:T(8,128)S(1)} %collective-permute-done.2.refs_3_, ...), custom_call_target="tpu_custom_call" | custom-call | flops 402653184 | bytes 3145728 | tf_op jit(solution)/shard_map/pallas_call | solution.py:152
  44.7 2.2 %shard_map.83 = (f32[512,128]{1,0:T(8,128)S(1)}, f32[512,128]{1,0:T(8,128)S(1)}) custom-call(s32[2]{0:T(128)S(1)} %pad_add_fusion.place, f32[512,128]{1,0:T(8,128)S(1)} %bitcast.15, f32[512,128]{1,0:T(8,128)S(1)} %collective-permute-done.refs_1_, f32[512,128]{1,0:T(8,128)S(1)} %collective-permute-done.1.refs_2_, ...), custom_call_target="tpu_custom_call" | custom-call | flops 402653184 | bytes 3145728 | tf_op jit(solution)/shard_map/pallas_call | solution.py:152
  50.5 5.5 %collective-permute-done.13.refs_2_ = f32[512,128]{1,0:T(8,128)S(1)} collective-permute-done((f32[512,128]{1,0:T(8,128)S(1)}, f32[512,128]{1,0:T(8,128)S(1)}, u32[]{:S(2)}, u32[]{:S(2)}) %collective-permute-start.13) | collective-permute-done | bytes 262176 | tf_op jit(solution)/shard_map/ppermute | solution.py:20
  56.1 5.2 %collective-permute-done.16.refs_6_ = f32[512,128]{1,0:T(8,128)S(1)} collective-permute-done((f32[512,128]{1,0:T(8,128)S(1)}, f32[512,128]{1,0:T(8,128)S(1)}, u32[]{:S(2)}, u32[]{:S(2)}) %collective-permute-start.16) | collective-permute-done | bytes 262176 | tf_op jit(solution)/shard_map/ppermute | solution.py:20
  61.3 3.7 %shard_map.85 = (f32[512,128]{1,0:T(8,128)}, f32[512,128]{1,0:T(8,128)}) custom-call(s32[2]{0:T(128)S(1)} %pad_add_fusion.place, f32[512,128]{1,0:T(8,128)S(1)} %shard_map.84.refs_0_.refs_8_, f32[512,128]{1,0:T(8,128)S(1)} %collective-permute-done.19.refs_1_, f32[512,128]{1,0:T(8,128)S(1)} %collective-permute-done.20.refs_2_, ...), custom_call_target="tpu_custom_call" | custom-call | flops 1207959552 | bytes 2097152 | tf_op jit(solution)/shard_map/pallas_call | solution.py:99
  65.0 2.1 %collective-permute-start.30 = (f32[512,128]{1,0:T(8,128)}, f32[512,128]{1,0:T(8,128)S(1)}, u32[]{:S(2)}, u32[]{:S(2)}) collective-permute-start(f32[512,128]{1,0:T(8,128)} %get-tuple-element.20), channel_id=1, source_target_pairs={{0,8},{4,12},{8,16},{12,20},{16,24},{20,28},{24,0},{28,4},{1,9},{5... | collective-permute-start | bytes 786440 | tf_op jit(solution)/shard_map/ppermute | solution.py:20
  69.1 3.7 %collective-permute-start.23 = (f32[512,128]{1,0:T(8,128)}, f32[512,128]{1,0:T(8,128)}, u32[]{:S(2)}, u32[]{:S(2)}) collective-permute-start(f32[512,128]{1,0:T(8,128)} %get-tuple-element.20), channel_id=1, source_target_pairs={{0,24},{4,28},{8,0},{12,4},{16,8},{20,12},{24,16},{28,20},{1,25},{... | collective-permute-start | bytes 786440 | tf_op jit(solution)/shard_map/ppermute | solution.py:20
  72.8 3.5 %collective-permute-done.30.refs_9_ = f32[512,128]{1,0:T(8,128)S(1)} collective-permute-done((f32[512,128]{1,0:T(8,128)}, f32[512,128]{1,0:T(8,128)S(1)}, u32[]{:S(2)}, u32[]{:S(2)}) %collective-permute-start.30) | collective-permute-done | bytes 262176 | tf_op jit(solution)/shard_map/ppermute | solution.py:20
  76.3 5.6 %collective-permute-done.31.refs_10_ = f32[512,128]{1,0:T(8,128)S(1)} collective-permute-done((f32[512,128]{1,0:T(8,128)}, f32[512,128]{1,0:T(8,128)S(1)}, u32[]{:S(2)}, u32[]{:S(2)}) %collective-permute-start.31) | collective-permute-done | bytes 262176 | tf_op jit(solution)/shard_map/ppermute | solution.py:20
  82.0 2.3 %shard_map.87.refs_0_.refs_8_ = f32[512,128]{1,0:T(8,128)} custom-call(s32[2]{0:T(128)S(1)} %pad_add_fusion.place, f32[512,128]{1,0:T(8,128)S(1)} %get-tuple-element.26.refs_4_.refs_0_, f32[512,128]{1,0:T(8,128)S(1)} %collective-permute-done.12.refs_1_, f32[512,128]{1,0:T(8,128)S(1)} %collective-permute-done.13.refs_2_, ...), custom_call_target="tpu_custom_call" | custom-call | flops 402653184 | bytes 3145728 | tf_op jit(solution)/shard_map/pallas_call | solution.py:152
  88.5 2.9 %shard_map.92 = f32[512,128]{1,0:T(8,128)S(1)} custom-call(s32[2]{0:T(128)S(1)} %pad_add_fusion.place, f32[512,128]{1,0:T(8,128)S(1)} %bitcast.22, f32[512,128]{1,0:T(8,128)S(1)} %copy-done.18, f32[512,128]{1,0:T(8,128)S(1)} %copy-done.16, f32[512,128]{1,0:T(8,128)S(1)} %copy-done.20, f32[512,128]{1,0:T(8,128)S(1)} %shard_map.91.refs_4_.refs_8_), custom_call_target="tpu_custom_call" | custom-call | flops 603979776 | bytes 1572864 | tf_op jit(solution)/shard_map/pallas_call | solution.py:99
  92.8 2.1 %shard_map.86 = (f32[512,128]{1,0:T(8,128)S(1)}, f32[512,128]{1,0:T(8,128)S(1)}) custom-call(s32[2]{0:T(128)S(1)} %pad_add_fusion.place, f32[512,128]{1,0:T(8,128)S(1)} %get-tuple-element.26.refs_4_.refs_0_, f32[512,128]{1,0:T(8,128)S(1)} %collective-permute-done.12.refs_1_, f32[512,128]{1,0:T(8,128)S(1)} %collective-permute-done.13.refs_2_, ...), custom_call_target="tpu_custom_call" | custom-call | flops 402653184 | bytes 3145728 | tf_op jit(solution)/shard_map/pallas_call | solution.py:152
  99.9 4.2 %collective-permute-done.25.refs_2_ = f32[512,128]{1,0:T(8,128)S(1)} collective-permute-done((f32[512,128]{1,0:T(8,128)S(1)}, f32[512,128]{1,0:T(8,128)S(1)}, u32[]{:S(2)}, u32[]{:S(2)}) %collective-permute-start.25) | collective-permute-done | bytes 262176 | tf_op jit(solution)/shard_map/ppermute | solution.py:20
  104.1 5.2 %collective-permute-done.28.refs_6_ = f32[512,128]{1,0:T(8,128)S(1)} collective-permute-done((f32[512,128]{1,0:T(8,128)S(1)}, f32[512,128]{1,0:T(8,128)S(1)}, u32[]{:S(2)}, u32[]{:S(2)}) %collective-permute-start.28) | collective-permute-done | bytes 262176 | tf_op jit(solution)/shard_map/ppermute | solution.py:20
  109.9 3.4 %shard_map.88 = (f32[512,128]{1,0:T(8,128)S(1)}, f32[512,128]{1,0:T(8,128)S(1)}) custom-call(s32[2]{0:T(128)S(1)} %pad_add_fusion.place, f32[512,128]{1,0:T(8,128)} %shard_map.87.refs_0_.refs_8_, f32[512,128]{1,0:T(8,128)S(1)} %collective-permute-done.32.refs_1_, f32[512,128]{1,0:T(8,128)} %collective-permute-done.33.refs_2_, ...), custom_call_target="tpu_custom_call" | custom-call | flops 1207959552 | bytes 2097152 | tf_op jit(solution)/shard_map/pallas_call | solution.py:99
  113.3 2.4 %collective-permute-start.35 = (f32[512,128]{1,0:T(8,128)S(1)}, f32[512,128]{1,0:T(8,128)S(1)}, u32[]{:S(2)}, u32[]{:S(2)}) collective-permute-start(f32[512,128]{1,0:T(8,128)S(1)} %get-tuple-element.23), channel_id=1, source_target_pairs={{0,16},{4,20},{8,24},{12,28},{16,0},{20,4},{24,8},{28,12},{1,17},{... | collective-permute-start | bytes 786440 | tf_op jit(solution)/shard_map/ppermute | solution.py:20
  116.3 2.2 %shard_map.93.refs_4_.refs_8_ = f32[512,128]{1,0:T(8,128)S(1)} custom-call(s32[2]{0:T(128)S(1)} %pad_add_fusion.place, f32[512,128]{1,0:T(8,128)S(1)} %bitcast.16, f32[512,128]{1,0:T(8,128)S(1)} %collective-permute-done.refs_1_, f32[512,128]{1,0:T(8,128)S(1)} %collective-permute-done.1.refs_2_, f32[512,128]{1,0:T(8,128)S(1)} %collective-permute-done.2.refs_3_, ...), custom_call_target="tpu_custom_call" | custom-call | flops 402653184 | bytes 3145728 | tf_op jit(solution)/shard_map/pallas_call | solution.py:152
  118.6 2.9 %shard_map.94 = f32[512,128]{1,0:T(8,128)S(1)} custom-call(s32[2]{0:T(128)S(1)} %pad_add_fusion.place, f32[512,128]{1,0:T(8,128)S(1)} %copy-done.7, f32[512,128]{1,0:T(8,128)S(1)} %copy-done.24, f32[512,128]{1,0:T(8,128)S(1)} %copy-done.22, f32[512,128]{1,0:T(8,128)S(1)} %copy-done.26, f32[512,128]{1,0:T(8,128)S(1)} %shard_map.93.refs_4_.refs_8_), custom_call_target="tpu_custom_call" | custom-call | flops 603979776 | bytes 1572864 | tf_op jit(solution)/shard_map/pallas_call | solution.py:99
  123.0 2.3 %collective-permute-start.43 = (f32[512,128]{1,0:T(8,128)S(1)}, f32[512,128]{1,0:T(8,128)S(1)}, u32[]{:S(2)}, u32[]{:S(2)}) collective-permute-start(f32[512,128]{1,0:T(8,128)S(1)} %shard_map.94), channel_id=1, source_target_pairs={{0,24},{4,28},{8,0},{12,4},{16,8},{20,12},{24,16},{28,20},{1,25},{... | collective-permute-start | bytes 786440 | tf_op jit(solution)/shard_map/ppermute | solution.py:20
  125.4 15.0 %collective-permute-done.35.refs_9_ = f32[512,128]{1,0:T(8,128)S(1)} collective-permute-done((f32[512,128]{1,0:T(8,128)S(1)}, f32[512,128]{1,0:T(8,128)S(1)}, u32[]{:S(2)}, u32[]{:S(2)}) %collective-permute-start.35) | collective-permute-done | bytes 262176 | tf_op jit(solution)/shard_map/ppermute | solution.py:20
  140.3 5.6 %collective-permute-done.36.refs_10_ = f32[512,128]{1,0:T(8,128)S(1)} collective-permute-done((f32[512,128]{1,0:T(8,128)S(1)}, f32[512,128]{1,0:T(8,128)S(1)}, u32[]{:S(2)}, u32[]{:S(2)}) %collective-permute-start.36) | collective-permute-done | bytes 262176 | tf_op jit(solution)/shard_map/ppermute | solution.py:20
  145.9 2.0 %shard_map.89.refs_0_ = f32[512,128]{1,0:T(8,128)S(1)} custom-call(s32[2]{0:T(128)S(1)} %pad_add_fusion.place, f32[512,128]{1,0:T(8,128)S(1)} %get-tuple-element.21.refs_4_.refs_0_, f32[512,128]{1,0:T(8,128)S(1)} %collective-permute-done.24.refs_1_, f32[512,128]{1,0:T(8,128)S(1)} %collective-permute-done.25.refs_2_, ...), custom_call_target="tpu_custom_call" | custom-call | flops 402653184 | bytes 3145728 | tf_op jit(solution)/shard_map/pallas_call | solution.py:152
  150.6 3.4 %shard_map.96 = f32[512,128]{1,0:T(8,128)S(1)} custom-call(s32[2]{0:T(128)S(1)} %pad_add_fusion.place, f32[512,128]{1,0:T(8,128)} %shard_map.87.refs_0_.refs_8_, f32[512,128]{1,0:T(8,128)S(1)} %collective-permute-done.32.refs_1_, f32[512,128]{1,0:T(8,128)} %collective-permute-done.33.refs_2_, f32[512,128]{1,0:T(8,128)S(1)} %collective-permute-done.34.refs_3_, ...), custom_call_target="tpu_custom_call" | custom-call | flops 603979776 | bytes 1572864 | tf_op jit(solution)/shard_map/pallas_call | solution.py:99
  154.0 2.6 %collective-permute-start.44 = (f32[512,128]{1,0:T(8,128)S(1)}, f32[512,128]{1,0:T(8,128)S(1)}, u32[]{:S(2)}, u32[]{:S(2)}) collective-permute-start(f32[512,128]{1,0:T(8,128)S(1)} %shard_map.96), channel_id=1, source_target_pairs={{0,16},{4,20},{8,24},{12,28},{16,0},{20,4},{24,8},{28,12},{1,17},{... | collective-permute-start | bytes 786440 | tf_op jit(solution)/shard_map/ppermute | solution.py:20
  157.2 10.7 %collective-permute-done.44.refs_9_.refs_10_ = f32[512,128]{1,0:T(8,128)S(1)} collective-permute-done((f32[512,128]{1,0:T(8,128)S(1)}, f32[512,128]{1,0:T(8,128)S(1)}, u32[]{:S(2)}, u32[]{:S(2)}) %collective-permute-start.44) | collective-permute-done | bytes 262176 | tf_op jit(solution)/shard_map/ppermute | solution.py:20
  169.6 3.6 %shard_map.98 = f32[512,128]{1,0:T(8,128)} custom-call(s32[2]{0:T(128)S(1)} %pad_add_fusion.place, f32[512,128]{1,0:T(8,128)S(1)} %shard_map.89.refs_0_, f32[512,128]{1,0:T(8,128)S(1)} %collective-permute-done.37.refs_1_, f32[512,128]{1,0:T(8,128)S(1)} %collective-permute-done.38.refs_2_, f32[512,128]{1,0:T(8,128)S(1)} %collective-permute-done.39.refs_3_, ...), custom_call_target="tpu_custom_call" | custom-call | flops 603979776 | bytes 1572864 | tf_op jit(solution)/shard_map/pallas_call | solution.py:99
  (133 shorter events, 40.1 us)
Async XLA Ops:
  11.2 12.8 %collective-permute-start = (f32[512,128]{1,0:T(8,128)}, f32[512,128]{1,0:T(8,128)S(1)}, u32[]{:S(2)}, u32[]{:S(2)}) collective-permute-start(f32[512,128]{1,0:T(8,128)} %bitcast.12), channel_id=1, source_target_pairs={{0,1},{1,0},{2,3},{3,2},{4,5},{5,4},{6,7},{7,6},{8,9},{9,8},{10,11... | collective-permute-start | bytes 786440 | tf_op jit(solution)/shard_map/ppermute | solution.py:20
  11.4 12.6 %collective-permute-start.4 = (f32[512,128]{1,0:T(8,128)}, f32[512,128]{1,0:T(8,128)S(1)}, u32[]{:S(2)}, u32[]{:S(2)}) collective-permute-start(f32[512,128]{1,0:T(8,128)} %bitcast.3.refs_5_.refs_4_), channel_id=1, source_target_pairs={{0,2},{1,3},{2,0},{3,1},{4,6},{5,7},{6,4},{7,5},{8,10},{9,11},{10,... | collective-permute-start | bytes 786440 | tf_op jit(solution)/shard_map/ppermute | solution.py:20
  19.1 12.1 %collective-permute-start.9 = (f32[512,128]{1,0:T(8,128)S(1)}, f32[512,128]{1,0:T(8,128)S(1)}, u32[]{:S(2)}, u32[]{:S(2)}) collective-permute-start(f32[512,128]{1,0:T(8,128)S(1)} %get-tuple-element.15), channel_id=1, source_target_pairs={{0,4},{4,0},{8,12},{12,8},{16,20},{20,16},{24,28},{28,24},{1,5},{5... | collective-permute-start | bytes 786440 | tf_op jit(solution)/shard_map/ppermute | solution.py:20
  19.4 21.5 %collective-permute-start.3 = (f32[512,128]{1,0:T(8,128)}, f32[512,128]{1,0:T(8,128)S(1)}, u32[]{:S(2)}, u32[]{:S(2)}) collective-permute-start(f32[512,128]{1,0:T(8,128)} %bitcast.3.refs_5_.refs_4_), channel_id=1, source_target_pairs={{0,1},{1,0},{2,3},{3,2},{4,5},{5,4},{6,7},{7,6},{8,9},{9,8},{10,11... | collective-permute-start | bytes 786440 | tf_op jit(solution)/shard_map/ppermute | solution.py:20
  24.0 16.8 %collective-permute-start.2 = (f32[512,128]{1,0:T(8,128)S(1)}, f32[512,128]{1,0:T(8,128)S(1)}, u32[]{:S(2)}, u32[]{:S(2)}) collective-permute-start(f32[512,128]{1,0:T(8,128)S(1)} %collective-permute-done.1.refs_2_), channel_id=1, source_target_pairs={{0,1},{1,0},{2,3},{3,2},{4,5},{5,4},{6,7},{7,6},{8,9},{9,8},{10,11... | collective-permute-start | bytes 786440 | tf_op jit(solution)/shard_map/ppermute | solution.py:20
  24.0 16.8 %collective-permute-start.5 = (f32[512,128]{1,0:T(8,128)S(1)}, f32[512,128]{1,0:T(8,128)S(1)}, u32[]{:S(2)}, u32[]{:S(2)}) collective-permute-start(f32[512,128]{1,0:T(8,128)S(1)} %collective-permute-done.4.refs_6_), channel_id=1, source_target_pairs={{0,1},{1,0},{2,3},{3,2},{4,5},{5,4},{6,7},{7,6},{8,9},{9,8},{10,11... | collective-permute-start | bytes 786440 | tf_op jit(solution)/shard_map/ppermute | solution.py:20
  26.5 14.3 %collective-permute-start.18 = (f32[512,128]{1,0:T(8,128)S(1)}, f32[512,128]{1,0:T(8,128)S(1)}, u32[]{:S(2)}, u32[]{:S(2)}) collective-permute-start(f32[512,128]{1,0:T(8,128)S(1)} %collective-permute-done.11.refs_9_), channel_id=1, source_target_pairs={{0,8},{4,28},{8,16},{12,4},{16,24},{20,12},{24,0},{28,20},{1,9},{5... | collective-permute-start | bytes 786440 | tf_op jit(solution)/shard_map/ppermute | solution.py:20
  31.2 13.5 %collective-permute-start.10 = (f32[512,128]{1,0:T(8,128)S(1)}, f32[512,128]{1,0:T(8,128)S(1)}, u32[]{:S(2)}, u32[]{:S(2)}) collective-permute-start(f32[512,128]{1,0:T(8,128)S(1)} %collective-permute-done.9.refs_10_), channel_id=1, source_target_pairs={{0,8},{4,28},{8,16},{12,4},{16,24},{20,12},{24,0},{28,20},{1,9},{5... | collective-permute-start | bytes 786440 | tf_op jit(solution)/shard_map/ppermute | solution.py:20
  35.9 49.7 %all-to-all-start = ((f32[8,136,128]{2,1,0:T(8,128)}), f32[8,136,128]{2,1,0:T(8,128)}, u32[]{:S(2)}, u32[]{:S(2)}) async-start(f32[8,136,128]{2,1,0:T(8,128)} %bitcast.8), calls=%async_computation | async-start | bytes 1114112 | tf_op jit(solution)/shard_map/all_to_all | solution.py:226
  47.5 13.8 %collective-permute-start.16 = (f32[512,128]{1,0:T(8,128)S(1)}, f32[512,128]{1,0:T(8,128)S(1)}, u32[]{:S(2)}, u32[]{:S(2)}) collective-permute-start(f32[512,128]{1,0:T(8,128)S(1)} %get-tuple-element.25.refs_5_.refs_4_), channel_id=1, source_target_pairs={{0,2},{1,3},{2,0},{3,1},{4,6},{5,7},{6,4},{7,5},{8,10},{9,11},{10,... | collective-permute-start | bytes 786440 | tf_op jit(solution)/shard_map/ppermute | solution.py:20
  50.0 17.1 %collective-permute-start.12 = (f32[512,128]{1,0:T(8,128)S(1)}, f32[512,128]{1,0:T(8,128)S(1)}, u32[]{:S(2)}, u32[]{:S(2)}) collective-permute-start(f32[512,128]{1,0:T(8,128)S(1)} %get-tuple-element.26.refs_4_.refs_0_), channel_id=1, source_target_pairs={{0,1},{1,0},{2,3},{3,2},{4,5},{5,4},{6,7},{7,6},{8,9},{9,8},{10,11... | collective-permute-start | bytes 786440 | tf_op jit(solution)/shard_map/ppermute | solution.py:20
  50.5 18.5 %collective-permute-start.15 = (f32[512,128]{1,0:T(8,128)S(1)}, f32[512,128]{1,0:T(8,128)S(1)}, u32[]{:S(2)}, u32[]{:S(2)}) collective-permute-start(f32[512,128]{1,0:T(8,128)S(1)} %get-tuple-element.25.refs_5_.refs_4_), channel_id=1, source_target_pairs={{0,1},{1,0},{2,3},{3,2},{4,5},{5,4},{6,7},{7,6},{8,9},{9,8},{10,11... | collective-permute-start | bytes 786440 | tf_op jit(solution)/shard_map/ppermute | solution.py:20
  56.1 13.1 %collective-permute-start.14 = (f32[512,128]{1,0:T(8,128)S(1)}, f32[512,128]{1,0:T(8,128)S(1)}, u32[]{:S(2)}, u32[]{:S(2)}) collective-permute-start(f32[512,128]{1,0:T(8,128)S(1)} %collective-permute-done.13.refs_2_), channel_id=1, source_target_pairs={{0,1},{1,0},{2,3},{3,2},{4,5},{5,4},{6,7},{7,6},{8,9},{9,8},{10,11... | collective-permute-start | bytes 786440 | tf_op jit(solution)/shard_map/ppermute | solution.py:20
  61.3 11.5 %collective-permute-start.17 = (f32[512,128]{1,0:T(8,128)S(1)}, f32[512,128]{1,0:T(8,128)S(1)}, u32[]{:S(2)}, u32[]{:S(2)}) collective-permute-start(f32[512,128]{1,0:T(8,128)S(1)} %collective-permute-done.16.refs_6_), channel_id=1, source_target_pairs={{0,1},{1,0},{2,3},{3,2},{4,5},{5,4},{6,7},{7,6},{8,9},{9,8},{10,11... | collective-permute-start | bytes 786440 | tf_op jit(solution)/shard_map/ppermute | solution.py:20
  67.1 14.9 %collective-permute-start.31 = (f32[512,128]{1,0:T(8,128)}, f32[512,128]{1,0:T(8,128)S(1)}, u32[]{:S(2)}, u32[]{:S(2)}) collective-permute-start(f32[512,128]{1,0:T(8,128)} %get-tuple-element.19), channel_id=1, source_target_pairs={{0,24},{4,28},{8,0},{12,4},{16,8},{20,12},{24,16},{28,20},{1,25},{... | collective-permute-start | bytes 786440 | tf_op jit(solution)/shard_map/ppermute | solution.py:20
  69.0 23.8 %collective-permute-start.22 = (f32[512,128]{1,0:T(8,128)}, f32[512,128]{1,0:T(8,128)}, u32[]{:S(2)}, u32[]{:S(2)}) collective-permute-start(f32[512,128]{1,0:T(8,128)} %get-tuple-element.19), channel_id=1, source_target_pairs={{0,8},{4,12},{8,16},{12,20},{16,24},{20,28},{24,0},{28,4},{1,9},{5... | collective-permute-start | bytes 786440 | tf_op jit(solution)/shard_map/ppermute | solution.py:20
  69.1 23.7 %collective-permute-start.23 = (f32[512,128]{1,0:T(8,128)}, f32[512,128]{1,0:T(8,128)}, u32[]{:S(2)}, u32[]{:S(2)}) collective-permute-start(f32[512,128]{1,0:T(8,128)} %get-tuple-element.20), channel_id=1, source_target_pairs={{0,24},{4,28},{8,0},{12,4},{16,8},{20,12},{24,16},{28,20},{1,25},{... | collective-permute-start | bytes 786440 | tf_op jit(solution)/shard_map/ppermute | solution.py:20
  84.3 12.7 %collective-permute-start.33 = (f32[512,128]{1,0:T(8,128)}, f32[512,128]{1,0:T(8,128)}, u32[]{:S(2)}, u32[]{:S(2)}) collective-permute-start(f32[512,128]{1,0:T(8,128)} %shard_map.87.refs_0_.refs_8_), channel_id=1, source_target_pairs={{0,2},{1,3},{2,0},{3,1},{4,6},{5,7},{6,4},{7,5},{8,10},{9,11},{10,... | collective-permute-start | bytes 786440 | tf_op jit(solution)/shard_map/ppermute | solution.py:20
  96.0 13.4 %collective-permute-start.28 = (f32[512,128]{1,0:T(8,128)S(1)}, f32[512,128]{1,0:T(8,128)S(1)}, u32[]{:S(2)}, u32[]{:S(2)}) collective-permute-start(f32[512,128]{1,0:T(8,128)S(1)} %get-tuple-element.22.refs_5_.refs_4_), channel_id=1, source_target_pairs={{0,2},{1,3},{2,0},{3,1},{4,6},{5,7},{6,4},{7,5},{8,10},{9,11},{10,... | collective-permute-start | bytes 786440 | tf_op jit(solution)/shard_map/ppermute | solution.py:20
  97.1 12.3 %collective-permute-start.34 = (f32[512,128]{1,0:T(8,128)}, f32[512,128]{1,0:T(8,128)S(1)}, u32[]{:S(2)}, u32[]{:S(2)}) collective-permute-start(f32[512,128]{1,0:T(8,128)} %collective-permute-done.33.refs_2_), channel_id=1, source_target_pairs={{0,1},{1,0},{2,3},{3,2},{4,5},{5,4},{6,7},{7,6},{8,9},{9,8},{10,11... | collective-permute-start | bytes 786440 | tf_op jit(solution)/shard_map/ppermute | solution.py:20
  98.3 14.9 %collective-permute-start.41 = (f32[512,128]{1,0:T(8,128)S(1)}, f32[512,128]{1,0:T(8,128)S(1)}, u32[]{:S(2)}, u32[]{:S(2)}) collective-permute-start(f32[512,128]{1,0:T(8,128)S(1)} %collective-permute-done.40.refs_10_), channel_id=1, source_target_pairs={{0,8},{4,28},{8,16},{12,4},{16,24},{20,12},{24,0},{28,20},{1,9},{5... | collective-permute-start | bytes 786440 | tf_op jit(solution)/shard_map/ppermute | solution.py:20
  99.9 15.8 %collective-permute-start.24 = (f32[512,128]{1,0:T(8,128)S(1)}, f32[512,128]{1,0:T(8,128)S(1)}, u32[]{:S(2)}, u32[]{:S(2)}) collective-permute-start(f32[512,128]{1,0:T(8,128)S(1)} %get-tuple-element.21.refs_4_.refs_0_), channel_id=1, source_target_pairs={{0,1},{1,0},{2,3},{3,2},{4,5},{5,4},{6,7},{7,6},{8,9},{9,8},{10,11... | collective-permute-start | bytes 786440 | tf_op jit(solution)/shard_map/ppermute | solution.py:20
  104.1 17.4 %collective-permute-start.27 = (f32[512,128]{1,0:T(8,128)S(1)}, f32[512,128]{1,0:T(8,128)S(1)}, u32[]{:S(2)}, u32[]{:S(2)}) collective-permute-start(f32[512,128]{1,0:T(8,128)S(1)} %get-tuple-element.22.refs_5_.refs_4_), channel_id=1, source_target_pairs={{0,1},{1,0},{2,3},{3,2},{4,5},{5,4},{6,7},{7,6},{8,9},{9,8},{10,11... | collective-permute-start | bytes 786440 | tf_op jit(solution)/shard_map/ppermute | solution.py:20
  109.3 13.7 %collective-permute-start.26 = (f32[512,128]{1,0:T(8,128)S(1)}, f32[512,128]{1,0:T(8,128)S(1)}, u32[]{:S(2)}, u32[]{:S(2)}) collective-permute-start(f32[512,128]{1,0:T(8,128)S(1)} %collective-permute-done.25.refs_2_), channel_id=1, source_target_pairs={{0,1},{1,0},{2,3},{3,2},{4,5},{5,4},{6,7},{7,6},{8,9},{9,8},{10,11... | collective-permute-start | bytes 786440 | tf_op jit(solution)/shard_map/ppermute | solution.py:20
  109.4 16.0 %collective-permute-start.29 = (f32[512,128]{1,0:T(8,128)S(1)}, f32[512,128]{1,0:T(8,128)S(1)}, u32[]{:S(2)}, u32[]{:S(2)}) collective-permute-start(f32[512,128]{1,0:T(8,128)S(1)} %collective-permute-done.28.refs_6_), channel_id=1, source_target_pairs={{0,1},{1,0},{2,3},{3,2},{4,5},{5,4},{6,7},{7,6},{8,9},{9,8},{10,11... | collective-permute-start | bytes 786440 | tf_op jit(solution)/shard_map/ppermute | solution.py:20
  113.3 27.1 %collective-permute-start.35 = (f32[512,128]{1,0:T(8,128)S(1)}, f32[512,128]{1,0:T(8,128)S(1)}, u32[]{:S(2)}, u32[]{:S(2)}) collective-permute-start(f32[512,128]{1,0:T(8,128)S(1)} %get-tuple-element.23), channel_id=1, source_target_pairs={{0,16},{4,20},{8,24},{12,28},{16,0},{20,4},{24,8},{28,12},{1,17},{... | collective-permute-start | bytes 786440 | tf_op jit(solution)/shard_map/ppermute | solution.py:20
  115.7 30.2 %collective-permute-start.36 = (f32[512,128]{1,0:T(8,128)S(1)}, f32[512,128]{1,0:T(8,128)S(1)}, u32[]{:S(2)}, u32[]{:S(2)}) collective-permute-start(f32[512,128]{1,0:T(8,128)S(1)} %get-tuple-element.24), channel_id=1, source_target_pairs={{0,16},{4,20},{8,24},{12,28},{16,0},{20,4},{24,8},{28,12},{1,17},{... | collective-permute-start | bytes 786440 | tf_op jit(solution)/shard_map/ppermute | solution.py:20
  121.5 27.5 %collective-permute-start.42 = (f32[512,128]{1,0:T(8,128)S(1)}, f32[512,128]{1,0:T(8,128)S(1)}, u32[]{:S(2)}, u32[]{:S(2)}) collective-permute-start(f32[512,128]{1,0:T(8,128)S(1)} %shard_map.94), channel_id=1, source_target_pairs={{0,8},{4,12},{8,16},{12,20},{16,24},{20,28},{24,0},{28,4},{1,9},{5... | collective-permute-start | bytes 786440 | tf_op jit(solution)/shard_map/ppermute | solution.py:20
  123.0 26.0 %collective-permute-start.43 = (f32[512,128]{1,0:T(8,128)S(1)}, f32[512,128]{1,0:T(8,128)S(1)}, u32[]{:S(2)}, u32[]{:S(2)}) collective-permute-start(f32[512,128]{1,0:T(8,128)S(1)} %shard_map.94), channel_id=1, source_target_pairs={{0,24},{4,28},{8,0},{12,4},{16,8},{20,12},{24,16},{28,20},{1,25},{... | collective-permute-start | bytes 786440 | tf_op jit(solution)/shard_map/ppermute | solution.py:20
  154.0 13.9 %collective-permute-start.44 = (f32[512,128]{1,0:T(8,128)S(1)}, f32[512,128]{1,0:T(8,128)S(1)}, u32[]{:S(2)}, u32[]{:S(2)}) collective-permute-start(f32[512,128]{1,0:T(8,128)S(1)} %shard_map.96), channel_id=1, source_target_pairs={{0,16},{4,20},{8,24},{12,28},{16,0},{20,4},{24,8},{28,12},{1,17},{... | collective-permute-start | bytes 786440 | tf_op jit(solution)/shard_map/ppermute | solution.py:20
  156.7 12.9 %collective-permute-start.37 = (f32[512,128]{1,0:T(8,128)S(1)}, f32[512,128]{1,0:T(8,128)S(1)}, u32[]{:S(2)}, u32[]{:S(2)}) collective-permute-start(f32[512,128]{1,0:T(8,128)S(1)} %shard_map.89.refs_0_), channel_id=1, source_target_pairs={{0,1},{1,0},{2,3},{3,2},{4,5},{5,4},{6,7},{7,6},{8,9},{9,8},{10,11... | collective-permute-start | bytes 786440 | tf_op jit(solution)/shard_map/ppermute | solution.py:20
  156.7 12.9 %collective-permute-start.39 = (f32[512,128]{1,0:T(8,128)S(1)}, f32[512,128]{1,0:T(8,128)S(1)}, u32[]{:S(2)}, u32[]{:S(2)}) collective-permute-start(f32[512,128]{1,0:T(8,128)S(1)} %collective-permute-done.38.refs_2_), channel_id=1, source_target_pairs={{0,1},{1,0},{2,3},{3,2},{4,5},{5,4},{6,7},{7,6},{8,9},{9,8},{10,11... | collective-permute-start | bytes 786440 | tf_op jit(solution)/shard_map/ppermute | solution.py:20
  (41 other events, 293.8 us)

commit v2 on v1

v2 whole, which is shorter than its diff:
```python
import functools

import jax
import jax.numpy as jnp
from jax import lax
from jax.experimental import pallas as pl
from jax.experimental.pallas import tpu as pltpu
from jax.sharding import PartitionSpec as P

coupling = 0.42
mark_rows = 8
f32 = jnp.float32
bf16 = jnp.bfloat16
in_vmem = pl.BlockSpec(memory_space=pltpu.VMEM)
in_smem = pl.BlockSpec(memory_space=pltpu.SMEM)


def send(value, axis, target_of):
    pairs = [(source, target_of(source)) for source in range(lax.axis_size(axis))]
    return lax.ppermute(value, axis, pairs)


def halves(value):
    high = value.astype(bf16)
    return high, (value - high.astype(f32)).astype(bf16)


def dot(left, right):
    return jnp.dot(left, right, preferred_element_type=f32)


def three_pass(left_high, left_low, right):
    high, low = halves(right)
    both = jnp.concatenate([high, low], axis=1)
    order, columns = left_high.shape[0], right.shape[1]
    found = []
    for rows in (slice(0, order // 2), slice(order // 2, order)):
        wide = dot(left_high[rows, :], both)
        found.append(wide[:, :columns] + wide[:, columns:] + dot(left_low[rows, :], high))
    return jnp.concatenate(found, axis=0)


def row_starts(place, shards, width):
    return [pl.multiple_of((place ^ k) * width, width) for k in range(shards)]


def load_rows(ref, starts, width, base=0):
    return jnp.concatenate([ref[pl.ds(base + start, width), :] for start in starts], axis=0)


def store_rows(ref, starts, width, value, base=0):
    for k, start in enumerate(starts):
        ref[pl.ds(base + start, width), :] = value[k * width : (k + 1) * width, :]


def assemble(high, low, refs, starts, width, base=0):
    for k, ref in enumerate(refs):
        for g, start in enumerate(starts):
            at = (slice(g * width, (g + 1) * width), slice(k * width, (k + 1) * width))
            high[at], low[at] = halves(ref[pl.ds(base + start, width), :])


def polynomial(high, low, value):
    second = value + three_pass(high, low, three_pass(high, low, value))
    return second - three_pass(high, low, second)


def compiler_params(megabytes):
    return pltpu.CompilerParams(vmem_limit_bytes=megabytes * 2**20)


def weight(cost):
    return pl.CostEstimate(
        flops=1 + 1_150_000_000 * cost, bytes_accessed=1 + 3_690_000 * cost, transcendentals=0
    )


def kernel_call(body, place, operands, outs, halves_of, after=(), cost=0):
    order = operands[0].shape[1] * lax.axis_size("az")
    width = operands[0].shape[1]
    count = len(operands)
    waited = len(after)

    def kernel(place_ref, *refs):
        starts = row_starts(place_ref[0], order // width, width)
        swapped = pl.multiple_of(place_ref[1] * order, order)
        body(
            starts,
            (swapped, order - swapped),
            refs[:count],
            refs[count + waited : count + waited + len(outs)],
            refs[count + waited + len(outs) :],
        )

    return pl.pallas_call(
        kernel,
        out_shape=[jax.ShapeDtypeStruct((rows, width), f32) for rows in outs],
        in_specs=[in_smem] + [in_vmem] * count + [pl.BlockSpec(memory_space=pl.ANY)] * waited,
        out_specs=[in_vmem] * len(outs),
        scratch_shapes=[pltpu.VMEM((order, order), bf16)] * (2 * halves_of),
        compiler_params=compiler_params(24),
        cost_estimate=weight(cost),
    )(place, *operands, *after)


def couplings(place, lower, upper, after=()):
    order, width = lower.shape

    def body(starts, bases, refs, outs, scratch):
        rows = lax.broadcasted_iota(jnp.int32, (order, width), 0)
        cols = lax.broadcasted_iota(jnp.int32, (order, width), 1)
        diagonal = jnp.where(rows == cols + starts[0], coupling, 0.0)
        outs[0][:order, :] = refs[0][...] - diagonal
        outs[0][order:, :] = refs[1][...] - diagonal

    return kernel_call(body, place, [lower, upper], [2 * order], 0, after)[0]


def normalized(place, n_shards, both, swap=False, join=False, after=()):
    shards, order, width = len(n_shards), both.shape[0] // 2, both.shape[1]

    def body(starts, bases, refs, outs, scratch):
        assemble(*scratch, refs[:shards], starts, width)
        bases = bases if swap else (0, order)
        value = [load_rows(refs[shards], starts, width, base) for base in bases]
        result = polynomial(*scratch, jnp.concatenate(value, axis=1))
        places = ((outs[0], 0), (outs[0], order)) if join else ((outs[0], 0), (outs[1], 0))
        for k, (ref, base) in enumerate(places):
            store_rows(ref, starts, width, result[:, k * width : (k + 1) * width], base)

    return kernel_call(body, place, [*n_shards, both], [2 * order] if join else [order] * 2, 1, after)


def one_column(place, n_shards, value, after=()):
    shards, order, width = len(n_shards), *value.shape

    def body(starts, bases, refs, outs, scratch):
        assemble(*scratch, refs[:shards], starts, width)
        result = polynomial(*scratch, load_rows(refs[shards], starts, width))
        store_rows(outs[0], starts, width, result)

    return kernel_call(body, place, [*n_shards, value], [order], 1, after)[0]


def joined_column(place, n_shards, value, one, two):
    shards, order, width = len(n_shards), *value.shape

    def body(starts, bases, refs, outs, scratch):
        assemble(*scratch, refs[:shards], starts, width)
        result = polynomial(*scratch, load_rows(refs[shards], starts, width))
        for out, top in zip(outs, refs[shards + 1 :]):
            out[:order, :] = top[...]
            store_rows(out, starts, width, result, order)

    return kernel_call(body, place, [*n_shards, value, one, two], [2 * order] * 2, 1)


def coupled_reduced(place, both_shards, base, one, two, after=()):
    shards, order, width = len(both_shards), *base.shape

    def body(starts, bases, refs, outs, scratch):
        total = load_rows(refs[shards], starts, width)
        for m in range(2):
            assemble(*scratch[2 * m : 2 * m + 2], refs[:shards], starts, width, m * order)
            right = [load_rows(refs[shards + 1 + m], starts, width, at) for at in (0, order)]
            found = three_pass(*scratch[2 * m : 2 * m + 2], jnp.concatenate(right, axis=1))
            store_rows(outs[0], starts, width, -found[:, :width], m * order)
            total = total - found[:, width:]
        store_rows(outs[1], starts, width, total)

    return kernel_call(body, place, [*both_shards, base, one, two], [2 * order, order], 2, after)


def reduced(place, both_shards, base, one, two, swap=False, after=(), cost=0):
    shards, order, width = len(both_shards), *base.shape
    joined = one is two

    def body(starts, bases, refs, outs, scratch):
        bases = bases if swap else (0, order)
        total = load_rows(refs[shards], starts, width)
        if joined and one.shape[0] == 2 * order:
            rights = [load_rows(refs[shards + 1], starts, width, at) for at in (order, 0)]
        else:
            rights = [load_rows(ref, starts, width) for ref in refs[shards + 1 :]]
            rights = rights * 2 if joined else rights
        for m in range(2):
            assemble(*scratch[2 * m : 2 * m + 2], refs[:shards], starts, width, bases[m])
            total = total - three_pass(*scratch[2 * m : 2 * m + 2], rights[m])
        store_rows(outs[0], starts, width, total)

    operands = [*both_shards, base, one] if joined else [*both_shards, base, one, two]
    return kernel_call(body, place, operands, [order], 2, after, cost)[0]


def coupled(place, both_shards, one, two, swap=False, after=()):
    shards, order, width = len(both_shards), *one.shape

    def body(starts, bases, refs, outs, scratch):
        bases = bases if swap else (0, order)
        for m in range(2):
            assemble(*scratch[2 * m : 2 * m + 2], refs[:shards], starts, width, bases[m])
            found = three_pass(*scratch[2 * m : 2 * m + 2], load_rows(refs[shards + m], starts, width))
            store_rows(outs[0], starts, width, -found, bases[m])

    return kernel_call(body, place, [*both_shards, one, two], [2 * order], 2, after)[0]


def slots_kernel(cycle_size, slot_count, counts, owner_row, rows_row, extra, out):
    entries, width = extra.shape
    position = lax.broadcasted_iota(jnp.int32, (1, entries), 1)
    live = position < counts[0]
    target = jnp.where(live, owner_row[...], cycle_size)
    blocks = lax.broadcasted_iota(jnp.int32, (cycle_size, entries), 0)
    owned = (blocks == target).astype(f32)
    before = lax.broadcasted_iota(jnp.int32, (entries, entries), 0)
    after = lax.broadcasted_iota(jnp.int32, (entries, entries), 1)
    earlier = dot(owned.astype(bf16), (before < after).astype(f32).astype(bf16))
    rank = jnp.sum(owned * earlier, axis=0, keepdims=True).astype(jnp.int32)
    high, low = halves(extra[...])
    both = jnp.concatenate([high, low], axis=1)
    slots = lax.broadcasted_iota(jnp.int32, (slot_count, entries), 0)
    in_slot = (slots == rank).astype(f32)
    mark_high, mark_low = halves(owned * (rows_row[...] + 1).astype(f32))
    to_slot = lambda mark: lax.dot_general(
        mark, in_slot.astype(bf16), (((1,), (1,)), ((), ())), preferred_element_type=f32
    )
    marks = to_slot(mark_high) + to_slot(mark_low)
    stride = slot_count + mark_rows
    for block in range(cycle_size):
        base = block * stride
        chosen = jnp.where(target == block, in_slot, 0.0).astype(bf16)
        found = dot(chosen, both)
        out[base : base + slot_count, :] = found[:, :width] + found[:, width:]
        out[base + slot_count : base + stride, :] = jnp.zeros((mark_rows, width), f32)
        out[base + slot_count : base + slot_count + 1, :slot_count] = marks[block : block + 1, :]


def load_kernel(cycle_size, slot_count, right_side, got, _, out):
    order, width = right_side.shape
    stride = slot_count + mark_rows
    total = right_side[...]
    rows = (lax.broadcasted_iota(jnp.int32, (order, slot_count), 0) + 1).astype(f32)
    for block in range(cycle_size):
        high, low = halves(got[block * stride : block * stride + slot_count, :])
        marks = got[block * stride + slot_count : block * stride + slot_count + 1, :slot_count]
        chosen = (rows == marks).astype(f32).astype(bf16)
        found = dot(chosen, jnp.concatenate([high, low], axis=1))
        total = total + (found[:, :width] + found[:, width:])
    out[...] = total


def placed_entries(extra, owners, rows_in, counts):
    cycle_size = lax.axis_size("blk")
    entries, width = extra.shape
    slot_count = 2 * entries // cycle_size
    rows = cycle_size * (slot_count + mark_rows)
    return pl.pallas_call(
        functools.partial(slots_kernel, cycle_size, slot_count),
        out_shape=jax.ShapeDtypeStruct((rows, width), f32),
        in_specs=[in_smem] + [in_vmem] * 3,
        out_specs=in_vmem,
        compiler_params=compiler_params(24),
        cost_estimate=weight(0),
    )(counts, owners.reshape(1, entries), rows_in.reshape(1, entries), extra)


def loaded(right_side, got, after):
    cycle_size = lax.axis_size("blk")
    order, width = right_side.shape
    return pl.pallas_call(
        functools.partial(load_kernel, cycle_size, got.shape[1] - mark_rows),
        out_shape=jax.ShapeDtypeStruct((order, width), f32),
        in_specs=[in_vmem] * 2 + [pl.BlockSpec(memory_space=pl.ANY)],
        out_specs=in_vmem,
        compiler_params=compiler_params(24),
        cost_estimate=weight(0),
    )(right_side, got.reshape(-1, width), after)


def across(value):
    bit = lax.axis_size("az") // 2
    return {bit: send(value, "az", lambda source: source ^ bit)}


def gathered(value, far):
    shards = {0: value, **far}
    bit = max(far) // 2
    while bit:
        for k in list(shards):
            shards[k | bit] = send(shards[k], "az", lambda source, bit=bit: source ^ bit)
        bit //= 2
    return [shards[k] for k in range(len(shards))]


def tied(*values):
    return lax.optimization_barrier(values)


def on_device(lower_part, diag_part, upper_part, right_side, extra, owners, rows_in, counts):
    cycle_size = lax.axis_size("blk")
    levels = min(4, 3 + cycle_size // 16)
    blk = lax.axis_index("blk")
    place = jnp.stack([lax.axis_index("az"), blk % 2]).astype(jnp.int32)
    diag = diag_part[0]

    n_far = across(diag)
    slots = placed_entries(extra, owners, rows_in, counts)
    both = couplings(place, lower_part[0], upper_part[0], [slots])
    n_far, both = tied(n_far, both)
    n_shards = gathered(diag, n_far)

    partner = lambda source: source ^ 1
    onward = lambda source: (source + 2 - 4 * (source % 2)) % cycle_size
    got_slots = lax.all_to_all(
        slots.reshape(cycle_size, -1, slots.shape[1]), "blk", split_axis=0, concat_axis=0, tiled=True
    )
    first, second = normalized(place, n_shards, both, swap=True)
    both_shards = gathered(both, across(both))
    near_first = send(first, "blk", partner)
    near_second = send(second, "blk", partner)
    near_first, got_slots = tied(near_first, got_slots)
    far_first = send(near_first, "blk", onward)
    right = loaded(right_side[0], got_slots, first)
    solved = one_column(place, n_shards, right)
    diag = reduced(place, both_shards, diag, far_first, near_second, swap=True, after=[solved])
    n_far = across(diag)
    far_second = send(near_second, "blk", onward)
    both = coupled(place, both_shards, far_second, near_first, swap=True, after=[solved])
    n_far, both = tied(n_far, both)
    n_shards = gathered(diag, n_far)
    near_solved = send(solved, "blk", partner)
    far_solved = send(near_solved, "blk", onward)
    waiting = (both_shards, right, far_solved, near_solved, True)

    stride = 2
    for level in range(1, levels):
        ahead = lambda source: (source + stride) % cycle_size
        back = lambda source: (source - stride) % cycle_size
        both_far = across(both)
        half = max(both_far)
        last = level == levels - 1
        if last and 2 * stride == cycle_size:
            right = reduced(place, *waiting)
            (pair,) = normalized(place, n_shards, both, join=True, after=[right])
            got = send(pair, "blk", ahead)
            both_far[half], got = tied(both_far[half], got)
            both_shards = gathered(both, both_far)
            solved = one_column(place, n_shards, right, after=[pair])
            low_y = up_y = send(solved, "blk", ahead)
            diag = reduced(place, both_shards, diag, got, got, after=[solved])
        else:
            p_row, q_row = normalized(place, n_shards, both)
            low_q, up_p = send(q_row, "blk", ahead), send(p_row, "blk", back)
            both_far[half], low_q, up_p, p_row, q_row = tied(both_far[half], low_q, up_p, p_row, q_row)
            both_shards = gathered(both, both_far)
            right = reduced(place, *waiting, after=[q_row], cost=20)
            diag = reduced(place, both_shards, diag, low_q, up_p, after=[right])
            solved = one_column(place, n_shards, right, after=[diag])
            low_y, up_y = send(solved, "blk", ahead), send(solved, "blk", back)
        n_far = across(diag)
        if last:
            right = reduced(place, both_shards, right, low_y, up_y, after=[diag], cost=20)
            n_far, right = tied(n_far, right)
        else:
            low_p, up_q = send(p_row, "blk", ahead), send(q_row, "blk", back)
            both = coupled(place, both_shards, low_p, up_q, after=[diag])
            n_far, both = tied(n_far, both)
            waiting = (both_shards, right, low_y, up_y, False)
        n_shards = gathered(diag, n_far)
        stride = 2 * stride
    return one_column(place, n_shards, right)[None]


def solution(mesh):
    placed = (
        P("blk", None, "az"),
        P("blk", None, "az"),
        P("blk", None, "az"),
        P("blk", None, "az"),
        P("blk", "az"),
        P("blk", None),
        P("blk"),
        P("blk"),
    )
    return jax.shard_map(
        on_device, mesh=mesh, in_specs=placed, out_specs=P("blk", None, "az"), check_vma=False
    )
```

time: 174 us -> 148 us (0.85)
  Pallas kernels: 43 us -> 29.1 us
  starting transfers between devices: 46.4 us -> 37.5 us
  waiting for transfers between devices: 78.9 us -> 76.2 us
    pallas_call x17 -> x18, Pallas kernels: 43 us -> 29.1 us  [the longest x16 26.9 us: kernel_call(): pl.pallas_call(kernel, out_shape=[jax.ShapeDtypeStruct((rows, width), f32...]
    ppermute x45 -> x35, starting transfers between devices: 41.4 us -> 31.5 us  [send(): return lax.ppermute(value, axis, pairs)]
    ppermute x45 -> x35, waiting for transfers between devices: 78.9 us -> 76.2 us  [send(): return lax.ppermute(value, axis, pairs)]
    unnamed x54 -> x22, local copies, waits for them, and re-layouts: 3.69 us -> 4.26 us
  transfers between devices with their start and end apart: 46 -> 36, of which waited for: 15 -> 19; matrix products, arithmetic and copies ran while one was open for 0% -> 0% of each run, Pallas kernels for 23% -> 18%
where the time goes in v2:
time: 148 us
  waiting for transfers between devices  76.2 us (51%)
  starting transfers between devices  37.5 us (25%)
  Pallas kernels  29.1 us (20%)
  local copies, waits for them, and re-layouts  4.26 us (3%)
    ppermute x35, waiting for transfers between devices, send(): return lax.ppermute(value, axis, pairs)  76.2 us
    ppermute x35, starting transfers between devices, send(): return lax.ppermute(value, axis, pairs)  31.5 us
    pallas_call x16, Pallas kernels, kernel_call(): pl.pallas_call(kernel, out_shape=[jax.ShapeDtypeStruct((rows, width), f32...  26.9 us
    all_to_all x1, starting transfers between devices, on_device(): lax.all_to_all(slots.reshape(cycle_size, -1, slots.shape[1]), 'blk', spli...  5.96 us
    unnamed x22, local copies, waits for them, and re-layouts  4.26 us
  transfers between devices with their start and end apart: 36, of which 19 were waited for; matrix products, arithmetic and copies ran while one was open for 0% of the time, Pallas kernels for 18%

profile of v2, /device:TPU:0, one launch (start us, length us, event | category | flops | bytes accessed | tf_op | source)
XLA Modules:
  0.0 148.0 jit_solution(5561387304474768208)
XLA Ops:
  0.0 2.9 %collective-permute-start = (f32[512,128]{1,0:T(8,128)}, f32[512,128]{1,0:T(8,128)S(1)}, u32[]{:S(2)}, u32[]{:S(2)}) collective-permute-start(f32[512,128]{1,0:T(8,128)} %bitcast.11), channel_id=1, source_target_pairs={{0,2},{1,3},{2,0},{3,1},{4,6},{5,7},{6,4},{7,5},{8,10},{9,11},{10,... | collective-permute-start | bytes 786440 | tf_op jit(solution)/shard_map/ppermute | solution.py:20
  6.7 6.0 %all-to-all-start = ((f32[8,136,128]{2,1,0:T(8,128)}), f32[8,136,128]{2,1,0:T(8,128)S(1)}, u32[]{:S(2)}, u32[]{:S(2)}) async-start(f32[8,136,128]{2,1,0:T(8,128)} %bitcast.7), calls=%async_computation | async-start | bytes 1114112 | tf_op jit(solution)/shard_map/all_to_all | solution.py:314
  15.9 2.9 %shard_map.84 = (f32[512,128]{1,0:T(8,128)S(1)}, f32[512,128]{1,0:T(8,128)}) custom-call(s32[2]{0:T(128)S(1)} %pad_add_fusion.place_ref, f32[512,128]{1,0:T(8,128)S(1)} %bitcast.13, f32[512,128]{1,0:T(8,128)S(1)} %collective-permute-done.4.refs_1_, f32[512,128]{1,0:T(8,128)S(1)} %collective-permute-done.refs_2_, ...), custom_call_target="tpu_custom_call" | custom-call | flops 1 | bytes 1 | tf_op jit(solution)/shard_map/pallas_call | solution.py:95
  18.9 2.0 %collective-permute-start.6 = (f32[512,128]{1,0:T(8,128)S(1)}, f32[512,128]{1,0:T(8,128)}, u32[]{:S(2)}, u32[]{:S(2)}) collective-permute-start(f32[512,128]{1,0:T(8,128)S(1)} %get-tuple-element.28._), channel_id=1, source_target_pairs={{0,4},{4,0},{8,12},{12,8},{16,20},{20,16},{24,28},{28,24},{1,5},{5... | collective-permute-start | bytes 786440 | tf_op jit(solution)/shard_map/ppermute | solution.py:20
  21.6 5.0 %collective-permute-done.2.refs_2_ = f32[1024,128]{1,0:T(8,128)S(1)} collective-permute-done((f32[1024,128]{1,0:T(8,128)S(1)}, f32[1024,128]{1,0:T(8,128)S(1)}, u32[]{:S(2)}, u32[]{:S(2)}) %collective-permute-start.2) | collective-permute-done | bytes 524320 | tf_op jit(solution)/shard_map/ppermute | solution.py:20
  26.6 1.7 %collective-permute-start.8 = (f32[512,128]{1,0:T(8,128)}, f32[512,128]{1,0:T(8,128)}, u32[]{:S(2)}, u32[]{:S(2)}) collective-permute-start(f32[512,128]{1,0:T(8,128)} %get-tuple-element.30), channel_id=1, source_target_pairs={{0,4},{4,0},{8,12},{12,8},{16,20},{20,16},{24,28},{28,24},{1,5},{5... | collective-permute-start | bytes 786440 | tf_op jit(solution)/shard_map/ppermute | solution.py:20
  29.0 1.9 %collective-permute-start.7 = (f32[512,128]{1,0:T(8,128)}, f32[512,128]{1,0:T(8,128)S(1)}, u32[]{:S(2)}, u32[]{:S(2)}) collective-permute-start(f32[512,128]{1,0:T(8,128)} %collective-permute-done.6.refs_5_), channel_id=1, source_target_pairs={{0,8},{4,28},{8,16},{12,4},{16,24},{20,12},{24,0},{28,20},{1,9},{5... | collective-permute-start | bytes 786440 | tf_op jit(solution)/shard_map/ppermute | solution.py:20
  33.5 2.1 %collective-permute-done.8.refs_6_ = f32[512,128]{1,0:T(8,128)} collective-permute-done((f32[512,128]{1,0:T(8,128)}, f32[512,128]{1,0:T(8,128)}, u32[]{:S(2)}, u32[]{:S(2)}) %collective-permute-start.8) | collective-permute-done | bytes 262176 | tf_op jit(solution)/shard_map/ppermute | solution.py:20
  35.6 1.7 %collective-permute-start.10 = (f32[512,128]{1,0:T(8,128)}, f32[512,128]{1,0:T(8,128)S(1)}, u32[]{:S(2)}, u32[]{:S(2)}) collective-permute-start(f32[512,128]{1,0:T(8,128)} %collective-permute-done.8.refs_6_), channel_id=1, source_target_pairs={{0,8},{4,28},{8,16},{12,4},{16,24},{20,12},{24,0},{28,20},{1,9},{5... | collective-permute-start | bytes 786440 | tf_op jit(solution)/shard_map/ppermute | solution.py:20
  37.3 1.7 %shard_map.86.refs_7_.refs_6_ = f32[512,128]{1,0:T(8,128)S(1)} custom-call(s32[2]{0:T(128)S(1)} %pad_add_fusion.place_ref, f32[512,128]{1,0:T(8,128)S(1)} %bitcast.14, f32[512,128]{1,0:T(8,128)S(1)} %collective-permute-done.4.refs_1_, f32[512,128]{1,0:T(8,128)S(1)} %collective-permute-done.refs_2_, f32[512,128]{1,0:T(8,128)S(1)} %copy-done.2, ...), custom_call_target="tpu_custom_call" | custom-call | flops 1 | bytes 1 | tf_op jit(solution)/shard_map/pallas_call | solution.py:95
  39.1 1.7 %shard_map.87.refs_0_.refs_4_ = f32[512,128]{1,0:T(8,128)S(1)} custom-call(s32[2]{0:T(128)S(1)} %pad_add_fusion.place_ref, f32[1024,128]{1,0:T(8,128)S(1)} %shard_map.83.refs_4_.refs_0_, f32[1024,128]{1,0:T(8,128)S(1)} %collective-permute-done.1.refs_1_, f32[1024,128]{1,0:T(8,128)S(1)} %collective-permute-done.2.refs_2_, ...), custom_call_target="tpu_custom_call" | custom-call | flops 1 | bytes 1 | tf_op jit(solution)/shard_map/pallas_call | solution.py:95
  41.9 3.7 %collective-permute-done.10.refs_4_ = f32[512,128]{1,0:T(8,128)S(1)} collective-permute-done((f32[512,128]{1,0:T(8,128)}, f32[512,128]{1,0:T(8,128)S(1)}, u32[]{:S(2)}, u32[]{:S(2)}) %collective-permute-start.10) | collective-permute-done | bytes 262176 | tf_op jit(solution)/shard_map/ppermute | solution.py:20
  45.6 1.7 %shard_map.88.refs_4_.refs_0_ = f32[1024,128]{1,0:T(8,128)S(1)} custom-call(s32[2]{0:T(128)S(1)} %pad_add_fusion.place_ref, f32[1024,128]{1,0:T(8,128)S(1)} %shard_map.83.refs_4_.refs_0_, f32[1024,128]{1,0:T(8,128)S(1)} %collective-permute-done.1.refs_1_, f32[1024,128]{1,0:T(8,128)S(1)} %collective-permute-done.2.refs_2_, ...), custom_call_target="tpu_custom_call" | custom-call | flops 1 | bytes 1 | tf_op jit(solution)/shard_map/pallas_call | solution.py:95
  49.1 3.3 %collective-permute-start.18 = (f32[512,128]{1,0:T(8,128)S(1)}, f32[512,128]{1,0:T(8,128)S(1)}, u32[]{:S(2)}, u32[]{:S(2)}) collective-permute-start(f32[512,128]{1,0:T(8,128)S(1)} %shard_map.86.refs_7_.refs_6_), channel_id=1, source_target_pairs={{0,4},{4,0},{8,12},{12,8},{16,20},{20,16},{24,28},{28,24},{1,5},{5... | collective-permute-start | bytes 786440 | tf_op jit(solution)/shard_map/ppermute | solution.py:20
  52.3 2.3 %shard_map.89 = (f32[512,128]{1,0:T(8,128)S(1)}, f32[512,128]{1,0:T(8,128)S(1)}) custom-call(s32[2]{0:T(128)S(1)} %pad_add_fusion.place_ref, f32[512,128]{1,0:T(8,128)S(1)} %shard_map.87.refs_0_.refs_4_, f32[512,128]{1,0:T(8,128)S(1)} %collective-permute-done.13.refs_1_, f32[512,128]{1,0:T(8,128)S(1)} %collective-permute-done.9.refs_2_, ...), custom_call_target="tpu_custom_call" | custom-call | flops 1 | bytes 1 | tf_op jit(solution)/shard_map/pallas_call | solution.py:95
  54.7 3.8 %collective-permute-start.16 = (f32[512,128]{1,0:T(8,128)S(1)}, f32[512,128]{1,0:T(8,128)S(1)}, u32[]{:S(2)}, u32[]{:S(2)}) collective-permute-start(f32[512,128]{1,0:T(8,128)S(1)} %get-tuple-element.40), channel_id=1, source_target_pairs={{0,24},{4,28},{8,0},{12,4},{16,8},{20,12},{24,16},{28,20},{1,25},{... | collective-permute-start | bytes 786440 | tf_op jit(solution)/shard_map/ppermute | solution.py:20
  59.1 6.5 %collective-permute-done.15.refs_5_ = f32[512,128]{1,0:T(8,128)S(1)} collective-permute-done((f32[512,128]{1,0:T(8,128)S(1)}, f32[512,128]{1,0:T(8,128)S(1)}, u32[]{:S(2)}, u32[]{:S(2)}) %collective-permute-start.15) | collective-permute-done | bytes 262176 | tf_op jit(solution)/shard_map/ppermute | solution.py:20
  65.6 2.9 %collective-permute-done.16.refs_6_ = f32[512,128]{1,0:T(8,128)S(1)} collective-permute-done((f32[512,128]{1,0:T(8,128)S(1)}, f32[512,128]{1,0:T(8,128)S(1)}, u32[]{:S(2)}, u32[]{:S(2)}) %collective-permute-start.16) | collective-permute-done | bytes 262176 | tf_op jit(solution)/shard_map/ppermute | solution.py:20
  69.0 3.3 %collective-permute-start.22 = (f32[512,128]{1,0:T(8,128)S(1)}, f32[512,128]{1,0:T(8,128)S(1)}, u32[]{:S(2)}, u32[]{:S(2)}) collective-permute-start(f32[512,128]{1,0:T(8,128)S(1)} %get-tuple-element.39.refs_7_), channel_id=1, source_target_pairs={{0,24},{4,28},{8,0},{12,4},{16,8},{20,12},{24,16},{28,20},{1,25},{... | collective-permute-start | bytes 786440 | tf_op jit(solution)/shard_map/ppermute | solution.py:20
  72.3 4.7 %collective-permute-done.19.refs_5_ = f32[512,128]{1,0:T(8,128)S(1)} collective-permute-done((f32[512,128]{1,0:T(8,128)S(1)}, f32[512,128]{1,0:T(8,128)S(1)}, u32[]{:S(2)}, u32[]{:S(2)}) %collective-permute-start.19) | collective-permute-done | bytes 262176 | tf_op jit(solution)/shard_map/ppermute | solution.py:20
  81.3 1.7 %shard_map.93 = f32[512,128]{1,0:T(8,128)S(1)} custom-call(s32[2]{0:T(128)S(1)} %pad_add_fusion.place_ref, f32[512,128]{1,0:T(8,128)S(1)} %shard_map.87.refs_0_.refs_4_, f32[512,128]{1,0:T(8,128)S(1)} %collective-permute-done.13.refs_1_, f32[512,128]{1,0:T(8,128)S(1)} %collective-permute-done.9.refs_2_, f32[512,128]{1,0:T(8,128)S(1)} %collective-permute-done.14.refs_3_, ...), custom_call_target="tpu_custom_call" | custom-call | flops 1 | bytes 1 | tf_op jit(solution)/shard_map/pallas_call | solution.py:95
  83.1 2.0 %collective-permute-start.27 = (f32[512,128]{1,0:T(8,128)S(1)}, f32[512,128]{1,0:T(8,128)S(1)}, u32[]{:S(2)}, u32[]{:S(2)}) collective-permute-start(f32[512,128]{1,0:T(8,128)S(1)} %shard_map.93), channel_id=1, source_target_pairs={{0,8},{4,12},{8,16},{12,20},{16,24},{20,28},{24,0},{28,4},{1,9},{5... | collective-permute-start | bytes 786440 | tf_op jit(solution)/shard_map/ppermute | solution.py:20
  85.1 2.3 %collective-permute-done.22.refs_5_ = f32[512,128]{1,0:T(8,128)S(1)} collective-permute-done((f32[512,128]{1,0:T(8,128)S(1)}, f32[512,128]{1,0:T(8,128)S(1)}, u32[]{:S(2)}, u32[]{:S(2)}) %collective-permute-start.22) | collective-permute-done | bytes 262176 | tf_op jit(solution)/shard_map/ppermute | solution.py:20
  88.7 1.6 %collective-permute-start.24 = (f32[1024,128]{1,0:T(8,128)S(1)}, f32[1024,128]{1,0:T(8,128)S(1)}, u32[]{:S(2)}, u32[]{:S(2)}) collective-permute-start(f32[1024,128]{1,0:T(8,128)S(1)} %shard_map.92.refs_4_.refs_0_), channel_id=1, source_target_pairs={{0,2},{1,3},{2,0},{3,1},{4,6},{5,7},{6,4},{7,5},{8,10},{9,11},{10,... | collective-permute-start | bytes 1572872 | tf_op jit(solution)/shard_map/ppermute | solution.py:20
  90.3 3.2 %collective-permute-done.28.refs_6_ = f32[512,128]{1,0:T(8,128)S(1)} collective-permute-done((f32[512,128]{1,0:T(8,128)S(1)}, f32[512,128]{1,0:T(8,128)S(1)}, u32[]{:S(2)}, u32[]{:S(2)}) %collective-permute-start.28) | collective-permute-done | bytes 262176 | tf_op jit(solution)/shard_map/ppermute | solution.py:20
  93.5 5.0 %collective-permute-done.27.refs_5_ = f32[512,128]{1,0:T(8,128)S(1)} collective-permute-done((f32[512,128]{1,0:T(8,128)S(1)}, f32[512,128]{1,0:T(8,128)S(1)}, u32[]{:S(2)}, u32[]{:S(2)}) %collective-permute-start.27) | collective-permute-done | bytes 262176 | tf_op jit(solution)/shard_map/ppermute | solution.py:20
  99.8 2.3 %shard_map.95.refs_5_ = f32[1024,128]{1,0:T(8,128)S(1)} custom-call(s32[2]{0:T(128)S(1)} %pad_add_fusion.place_ref, f32[512,128]{1,0:T(8,128)S(1)} %shard_map.91.refs_6_.refs_5_.refs_0_.refs_4_, f32[512,128]{1,0:T(8,128)S(1)} %collective-permute-done.25.refs_1_, f32[512,128]{1,0:T(8,128)S(1)} %collective-permute-done.20.refs_2_, ...), custom_call_target="tpu_custom_call" | custom-call | flops 1 | bytes 1 | tf_op jit(solution)/shard_map/pallas_call | solution.py:95
  103.1 22.6 %collective-permute-done.29.refs_5_ = f32[1024,128]{1,0:T(8,128)S(1)} collective-permute-done((f32[1024,128]{1,0:T(8,128)S(1)}, f32[1024,128]{1,0:T(8,128)S(1)}, u32[]{:S(2)}, u32[]{:S(2)}) %collective-permute-start.29) | collective-permute-done | bytes 524320 | tf_op jit(solution)/shard_map/ppermute | solution.py:20
  125.7 1.7 %shard_map.96.refs_6_ = f32[512,128]{1,0:T(8,128)S(1)} custom-call(s32[2]{0:T(128)S(1)} %pad_add_fusion.place_ref, f32[512,128]{1,0:T(8,128)S(1)} %shard_map.91.refs_6_.refs_5_.refs_0_.refs_4_, f32[512,128]{1,0:T(8,128)S(1)} %collective-permute-done.25.refs_1_, f32[512,128]{1,0:T(8,128)S(1)} %collective-permute-done.20.refs_2_, ...), custom_call_target="tpu_custom_call" | custom-call | flops 1 | bytes 1 | tf_op jit(solution)/shard_map/pallas_call | solution.py:95
  128.9 1.6 %collective-permute-start.32 = (f32[512,128]{1,0:T(8,128)S(1)}, f32[512,128]{1,0:T(8,128)S(1)}, u32[]{:S(2)}, u32[]{:S(2)}) collective-permute-start(f32[512,128]{1,0:T(8,128)S(1)} %shard_map.97.refs_6_.refs_0_), channel_id=1, source_target_pairs={{0,2},{1,3},{2,0},{3,1},{4,6},{5,7},{6,4},{7,5},{8,10},{9,11},{10,... | collective-permute-start | bytes 786440 | tf_op jit(solution)/shard_map/ppermute | solution.py:20
  130.7 12.0 %collective-permute-done.33.refs_5_ = f32[512,128]{1,0:T(8,128)S(1)} collective-permute-done((f32[512,128]{1,0:T(8,128)S(1)}, f32[512,128]{1,0:T(8,128)S(1)}, u32[]{:S(2)}, u32[]{:S(2)}) %collective-permute-start.33) | collective-permute-done | bytes 262176 | tf_op jit(solution)/shard_map/ppermute | solution.py:20
  145.6 2.4 %shard_map.99 = f32[512,128]{1,0:T(8,128)} custom-call(s32[2]{0:T(128)S(1)} %pad_add_fusion.place_ref, f32[512,128]{1,0:T(8,128)S(1)} %shard_map.97.refs_6_.refs_0_, f32[512,128]{1,0:T(8,128)S(1)} %collective-permute-done.31.refs_1_, f32[512,128]{1,0:T(8,128)S(1)} %collective-permute-done.32.refs_2_, f32[512,128]{1,0:T(8,128)S(1)} %collective-permute-done.34.refs_3_, ...), custom_call_target="tpu_custom_call" | custom-call | flops 1 | bytes 1 | tf_op jit(solution)/shard_map/pallas_call | solution.py:95
  (81 shorter events, 26.9 us)
Async XLA Ops:
  0.0 13.4 %collective-permute-start = (f32[512,128]{1,0:T(8,128)}, f32[512,128]{1,0:T(8,128)S(1)}, u32[]{:S(2)}, u32[]{:S(2)}) collective-permute-start(f32[512,128]{1,0:T(8,128)} %bitcast.11), channel_id=1, source_target_pairs={{0,2},{1,3},{2,0},{3,1},{4,6},{5,7},{6,4},{7,5},{8,10},{9,11},{10,... | collective-permute-start | bytes 786440 | tf_op jit(solution)/shard_map/ppermute | solution.py:20
  6.7 22.3 %all-to-all-start = ((f32[8,136,128]{2,1,0:T(8,128)}), f32[8,136,128]{2,1,0:T(8,128)S(1)}, u32[]{:S(2)}, u32[]{:S(2)}) async-start(f32[8,136,128]{2,1,0:T(8,128)} %bitcast.7), calls=%async_computation | async-start | bytes 1114112 | tf_op jit(solution)/shard_map/all_to_all | solution.py:314
  13.4 13.2 %collective-permute-start.2 = (f32[1024,128]{1,0:T(8,128)S(1)}, f32[1024,128]{1,0:T(8,128)S(1)}, u32[]{:S(2)}, u32[]{:S(2)}) collective-permute-start(f32[1024,128]{1,0:T(8,128)S(1)} %shard_map.83.refs_4_.refs_0_), channel_id=1, source_target_pairs={{0,2},{1,3},{2,0},{3,1},{4,6},{5,7},{6,4},{7,5},{8,10},{9,11},{10,... | collective-permute-start | bytes 1572872 | tf_op jit(solution)/shard_map/ppermute | solution.py:20
  18.9 10.2 %collective-permute-start.6 = (f32[512,128]{1,0:T(8,128)S(1)}, f32[512,128]{1,0:T(8,128)}, u32[]{:S(2)}, u32[]{:S(2)}) collective-permute-start(f32[512,128]{1,0:T(8,128)S(1)} %get-tuple-element.28._), channel_id=1, source_target_pairs={{0,4},{4,0},{8,12},{12,8},{16,20},{20,16},{24,28},{28,24},{1,5},{5... | collective-permute-start | bytes 786440 | tf_op jit(solution)/shard_map/ppermute | solution.py:20
  21.6 17.5 %collective-permute-start.1 = (f32[1024,128]{1,0:T(8,128)S(1)}, f32[1024,128]{1,0:T(8,128)S(1)}, u32[]{:S(2)}, u32[]{:S(2)}) collective-permute-start(f32[1024,128]{1,0:T(8,128)S(1)} %shard_map.83.refs_4_.refs_0_), channel_id=1, source_target_pairs={{0,1},{1,0},{2,3},{3,2},{4,5},{5,4},{6,7},{7,6},{8,9},{9,8},{10,11... | collective-permute-start | bytes 1572872 | tf_op jit(solution)/shard_map/ppermute | solution.py:20
  26.6 12.5 %collective-permute-start.3 = (f32[1024,128]{1,0:T(8,128)S(1)}, f32[1024,128]{1,0:T(8,128)S(1)}, u32[]{:S(2)}, u32[]{:S(2)}) collective-permute-start(f32[1024,128]{1,0:T(8,128)S(1)} %collective-permute-done.2.refs_2_), channel_id=1, source_target_pairs={{0,1},{1,0},{2,3},{3,2},{4,5},{5,4},{6,7},{7,6},{8,9},{9,8},{10,11... | collective-permute-start | bytes 1572872 | tf_op jit(solution)/shard_map/ppermute | solution.py:20
  26.6 9.0 %collective-permute-start.8 = (f32[512,128]{1,0:T(8,128)}, f32[512,128]{1,0:T(8,128)}, u32[]{:S(2)}, u32[]{:S(2)}) collective-permute-start(f32[512,128]{1,0:T(8,128)} %get-tuple-element.30), channel_id=1, source_target_pairs={{0,4},{4,0},{8,12},{12,8},{16,20},{20,16},{24,28},{28,24},{1,5},{5... | collective-permute-start | bytes 786440 | tf_op jit(solution)/shard_map/ppermute | solution.py:20
  29.0 10.1 %collective-permute-start.7 = (f32[512,128]{1,0:T(8,128)}, f32[512,128]{1,0:T(8,128)S(1)}, u32[]{:S(2)}, u32[]{:S(2)}) collective-permute-start(f32[512,128]{1,0:T(8,128)} %collective-permute-done.6.refs_5_), channel_id=1, source_target_pairs={{0,8},{4,28},{8,16},{12,4},{16,24},{20,12},{24,0},{28,20},{1,9},{5... | collective-permute-start | bytes 786440 | tf_op jit(solution)/shard_map/ppermute | solution.py:20
  35.6 9.9 %collective-permute-start.10 = (f32[512,128]{1,0:T(8,128)}, f32[512,128]{1,0:T(8,128)S(1)}, u32[]{:S(2)}, u32[]{:S(2)}) collective-permute-start(f32[512,128]{1,0:T(8,128)} %collective-permute-done.8.refs_6_), channel_id=1, source_target_pairs={{0,8},{4,28},{8,16},{12,4},{16,24},{20,12},{24,0},{28,20},{1,9},{5... | collective-permute-start | bytes 786440 | tf_op jit(solution)/shard_map/ppermute | solution.py:20
  40.8 7.7 %collective-permute-start.9 = (f32[512,128]{1,0:T(8,128)S(1)}, f32[512,128]{1,0:T(8,128)S(1)}, u32[]{:S(2)}, u32[]{:S(2)}) collective-permute-start(f32[512,128]{1,0:T(8,128)S(1)} %shard_map.87.refs_0_.refs_4_), channel_id=1, source_target_pairs={{0,2},{1,3},{2,0},{3,1},{4,6},{5,7},{6,4},{7,5},{8,10},{9,11},{10,... | collective-permute-start | bytes 786440 | tf_op jit(solution)/shard_map/ppermute | solution.py:20
  41.9 10.4 %collective-permute-start.13 = (f32[512,128]{1,0:T(8,128)S(1)}, f32[512,128]{1,0:T(8,128)S(1)}, u32[]{:S(2)}, u32[]{:S(2)}) collective-permute-start(f32[512,128]{1,0:T(8,128)S(1)} %shard_map.87.refs_0_.refs_4_), channel_id=1, source_target_pairs={{0,1},{1,0},{2,3},{3,2},{4,5},{5,4},{6,7},{7,6},{8,9},{9,8},{10,11... | collective-permute-start | bytes 786440 | tf_op jit(solution)/shard_map/ppermute | solution.py:20
  48.5 3.8 %collective-permute-start.14 = (f32[512,128]{1,0:T(8,128)S(1)}, f32[512,128]{1,0:T(8,128)S(1)}, u32[]{:S(2)}, u32[]{:S(2)}) collective-permute-start(f32[512,128]{1,0:T(8,128)S(1)} %collective-permute-done.9.refs_2_), channel_id=1, source_target_pairs={{0,1},{1,0},{2,3},{3,2},{4,5},{5,4},{6,7},{7,6},{8,9},{9,8},{10,11... | collective-permute-start | bytes 786440 | tf_op jit(solution)/shard_map/ppermute | solution.py:20
  48.5 20.0 %collective-permute-start.12 = (f32[1024,128]{1,0:T(8,128)S(1)}, f32[1024,128]{1,0:T(8,128)S(1)}, u32[]{:S(2)}, u32[]{:S(2)}) collective-permute-start(f32[1024,128]{1,0:T(8,128)S(1)} %shard_map.88.refs_4_.refs_0_), channel_id=1, source_target_pairs={{0,2},{1,3},{2,0},{3,1},{4,6},{5,7},{6,4},{7,5},{8,10},{9,11},{10,... | collective-permute-start | bytes 1572872 | tf_op jit(solution)/shard_map/ppermute | solution.py:20
  49.1 9.9 %collective-permute-start.18 = (f32[512,128]{1,0:T(8,128)S(1)}, f32[512,128]{1,0:T(8,128)S(1)}, u32[]{:S(2)}, u32[]{:S(2)}) collective-permute-start(f32[512,128]{1,0:T(8,128)S(1)} %shard_map.86.refs_7_.refs_6_), channel_id=1, source_target_pairs={{0,4},{4,0},{8,12},{12,8},{16,20},{20,16},{24,28},{28,24},{1,5},{5... | collective-permute-start | bytes 786440 | tf_op jit(solution)/shard_map/ppermute | solution.py:20
  54.6 11.0 %collective-permute-start.15 = (f32[512,128]{1,0:T(8,128)S(1)}, f32[512,128]{1,0:T(8,128)S(1)}, u32[]{:S(2)}, u32[]{:S(2)}) collective-permute-start(f32[512,128]{1,0:T(8,128)S(1)} %get-tuple-element.39.refs_7_), channel_id=1, source_target_pairs={{0,8},{4,12},{8,16},{12,20},{16,24},{20,28},{24,0},{28,4},{1,9},{5... | collective-permute-start | bytes 786440 | tf_op jit(solution)/shard_map/ppermute | solution.py:20
  54.7 13.8 %collective-permute-start.16 = (f32[512,128]{1,0:T(8,128)S(1)}, f32[512,128]{1,0:T(8,128)S(1)}, u32[]{:S(2)}, u32[]{:S(2)}) collective-permute-start(f32[512,128]{1,0:T(8,128)S(1)} %get-tuple-element.40), channel_id=1, source_target_pairs={{0,24},{4,28},{8,0},{12,4},{16,8},{20,12},{24,16},{28,20},{1,25},{... | collective-permute-start | bytes 786440 | tf_op jit(solution)/shard_map/ppermute | solution.py:20
  59.0 18.1 %collective-permute-start.19 = (f32[512,128]{1,0:T(8,128)S(1)}, f32[512,128]{1,0:T(8,128)S(1)}, u32[]{:S(2)}, u32[]{:S(2)}) collective-permute-start(f32[512,128]{1,0:T(8,128)S(1)} %collective-permute-done.18.refs_6_), channel_id=1, source_target_pairs={{0,8},{4,28},{8,16},{12,4},{16,24},{20,12},{24,0},{28,20},{1,9},{5... | collective-permute-start | bytes 786440 | tf_op jit(solution)/shard_map/ppermute | solution.py:20
  59.1 19.2 %collective-permute-start.11 = (f32[1024,128]{1,0:T(8,128)S(1)}, f32[1024,128]{1,0:T(8,128)S(1)}, u32[]{:S(2)}, u32[]{:S(2)}) collective-permute-start(f32[1024,128]{1,0:T(8,128)S(1)} %shard_map.88.refs_4_.refs_0_), channel_id=1, source_target_pairs={{0,1},{1,0},{2,3},{3,2},{4,5},{5,4},{6,7},{7,6},{8,9},{9,8},{10,11... | collective-permute-start | bytes 1572872 | tf_op jit(solution)/shard_map/ppermute | solution.py:20
  68.5 16.6 %collective-permute-start.21 = (f32[512,128]{1,0:T(8,128)S(1)}, f32[512,128]{1,0:T(8,128)S(1)}, u32[]{:S(2)}, u32[]{:S(2)}) collective-permute-start(f32[512,128]{1,0:T(8,128)S(1)} %get-tuple-element.40), channel_id=1, source_target_pairs={{0,8},{4,12},{8,16},{12,20},{16,24},{20,28},{24,0},{28,4},{1,9},{5... | collective-permute-start | bytes 786440 | tf_op jit(solution)/shard_map/ppermute | solution.py:20
  69.0 18.3 %collective-permute-start.22 = (f32[512,128]{1,0:T(8,128)S(1)}, f32[512,128]{1,0:T(8,128)S(1)}, u32[]{:S(2)}, u32[]{:S(2)}) collective-permute-start(f32[512,128]{1,0:T(8,128)S(1)} %get-tuple-element.39.refs_7_), channel_id=1, source_target_pairs={{0,24},{4,28},{8,0},{12,4},{16,8},{20,12},{24,16},{28,20},{1,25},{... | collective-permute-start | bytes 786440 | tf_op jit(solution)/shard_map/ppermute | solution.py:20
  72.3 6.0 %collective-permute-start.17 = (f32[1024,128]{1,0:T(8,128)S(1)}, f32[1024,128]{1,0:T(8,128)S(1)}, u32[]{:S(2)}, u32[]{:S(2)}) collective-permute-start(f32[1024,128]{1,0:T(8,128)S(1)} %collective-permute-done.12.refs_2_), channel_id=1, source_target_pairs={{0,1},{1,0},{2,3},{3,2},{4,5},{5,4},{6,7},{7,6},{8,9},{9,8},{10,11... | collective-permute-start | bytes 1572872 | tf_op jit(solution)/shard_map/ppermute | solution.py:20
  79.7 8.9 %collective-permute-start.20 = (f32[512,128]{1,0:T(8,128)S(1)}, f32[512,128]{1,0:T(8,128)S(1)}, u32[]{:S(2)}, u32[]{:S(2)}) collective-permute-start(f32[512,128]{1,0:T(8,128)S(1)} %shard_map.91.refs_6_.refs_5_.refs_0_.refs_4_), channel_id=1, source_target_pairs={{0,2},{1,3},{2,0},{3,1},{4,6},{5,7},{6,4},{7,5},{8,10},{9,11},{10,... | collective-permute-start | bytes 786440 | tf_op jit(solution)/shard_map/ppermute | solution.py:20
  83.0 10.5 %collective-permute-start.28 = (f32[512,128]{1,0:T(8,128)S(1)}, f32[512,128]{1,0:T(8,128)S(1)}, u32[]{:S(2)}, u32[]{:S(2)}) collective-permute-start(f32[512,128]{1,0:T(8,128)S(1)} %shard_map.93), channel_id=1, source_target_pairs={{0,24},{4,28},{8,0},{12,4},{16,8},{20,12},{24,16},{28,20},{1,25},{... | collective-permute-start | bytes 786440 | tf_op jit(solution)/shard_map/ppermute | solution.py:20
  83.1 15.4 %collective-permute-start.27 = (f32[512,128]{1,0:T(8,128)S(1)}, f32[512,128]{1,0:T(8,128)S(1)}, u32[]{:S(2)}, u32[]{:S(2)}) collective-permute-start(f32[512,128]{1,0:T(8,128)S(1)} %shard_map.93), channel_id=1, source_target_pairs={{0,8},{4,12},{8,16},{12,20},{16,24},{20,28},{24,0},{28,4},{1,9},{5... | collective-permute-start | bytes 786440 | tf_op jit(solution)/shard_map/ppermute | solution.py:20
  85.1 14.7 %collective-permute-start.25 = (f32[512,128]{1,0:T(8,128)S(1)}, f32[512,128]{1,0:T(8,128)S(1)}, u32[]{:S(2)}, u32[]{:S(2)}) collective-permute-start(f32[512,128]{1,0:T(8,128)S(1)} %shard_map.91.refs_6_.refs_5_.refs_0_.refs_4_), channel_id=1, source_target_pairs={{0,1},{1,0},{2,3},{3,2},{4,5},{5,4},{6,7},{7,6},{8,9},{9,8},{10,11... | collective-permute-start | bytes 786440 | tf_op jit(solution)/shard_map/ppermute | solution.py:20
  88.7 11.1 %collective-permute-start.26 = (f32[512,128]{1,0:T(8,128)S(1)}, f32[512,128]{1,0:T(8,128)S(1)}, u32[]{:S(2)}, u32[]{:S(2)}) collective-permute-start(f32[512,128]{1,0:T(8,128)S(1)} %collective-permute-done.20.refs_2_), channel_id=1, source_target_pairs={{0,1},{1,0},{2,3},{3,2},{4,5},{5,4},{6,7},{7,6},{8,9},{9,8},{10,11... | collective-permute-start | bytes 786440 | tf_op jit(solution)/shard_map/ppermute | solution.py:20
  88.7 14.3 %collective-permute-start.24 = (f32[1024,128]{1,0:T(8,128)S(1)}, f32[1024,128]{1,0:T(8,128)S(1)}, u32[]{:S(2)}, u32[]{:S(2)}) collective-permute-start(f32[1024,128]{1,0:T(8,128)S(1)} %shard_map.92.refs_4_.refs_0_), channel_id=1, source_target_pairs={{0,2},{1,3},{2,0},{3,1},{4,6},{5,7},{6,4},{7,5},{8,10},{9,11},{10,... | collective-permute-start | bytes 1572872 | tf_op jit(solution)/shard_map/ppermute | solution.py:20
  102.1 23.5 %collective-permute-start.29 = (f32[1024,128]{1,0:T(8,128)S(1)}, f32[1024,128]{1,0:T(8,128)S(1)}, u32[]{:S(2)}, u32[]{:S(2)}) collective-permute-start(f32[1024,128]{1,0:T(8,128)S(1)} %shard_map.95.refs_5_), channel_id=1, source_target_pairs={{0,16},{4,20},{8,24},{12,28},{16,0},{20,4},{24,8},{28,12},{1,17},{... | collective-permute-start | bytes 1572872 | tf_op jit(solution)/shard_map/ppermute | solution.py:20
  102.2 25.3 %collective-permute-start.23 = (f32[1024,128]{1,0:T(8,128)S(1)}, f32[1024,128]{1,0:T(8,128)S(1)}, u32[]{:S(2)}, u32[]{:S(2)}) collective-permute-start(f32[1024,128]{1,0:T(8,128)S(1)} %shard_map.92.refs_4_.refs_0_), channel_id=1, source_target_pairs={{0,1},{1,0},{2,3},{3,2},{4,5},{5,4},{6,7},{7,6},{8,9},{9,8},{10,11... | collective-permute-start | bytes 1572872 | tf_op jit(solution)/shard_map/ppermute | solution.py:20
  127.4 15.3 %collective-permute-start.33 = (f32[512,128]{1,0:T(8,128)S(1)}, f32[512,128]{1,0:T(8,128)S(1)}, u32[]{:S(2)}, u32[]{:S(2)}) collective-permute-start(f32[512,128]{1,0:T(8,128)S(1)} %shard_map.96.refs_6_), channel_id=1, source_target_pairs={{0,16},{4,20},{8,24},{12,28},{16,0},{20,4},{24,8},{28,12},{1,17},{... | collective-permute-start | bytes 786440 | tf_op jit(solution)/shard_map/ppermute | solution.py:20
  128.9 15.1 %collective-permute-start.32 = (f32[512,128]{1,0:T(8,128)S(1)}, f32[512,128]{1,0:T(8,128)S(1)}, u32[]{:S(2)}, u32[]{:S(2)}) collective-permute-start(f32[512,128]{1,0:T(8,128)S(1)} %shard_map.97.refs_6_.refs_0_), channel_id=1, source_target_pairs={{0,2},{1,3},{2,0},{3,1},{4,6},{5,7},{6,4},{7,5},{8,10},{9,11},{10,... | collective-permute-start | bytes 786440 | tf_op jit(solution)/shard_map/ppermute | solution.py:20
  130.5 13.6 %collective-permute-start.31 = (f32[512,128]{1,0:T(8,128)S(1)}, f32[512,128]{1,0:T(8,128)S(1)}, u32[]{:S(2)}, u32[]{:S(2)}) collective-permute-start(f32[512,128]{1,0:T(8,128)S(1)} %shard_map.97.refs_6_.refs_0_), channel_id=1, source_target_pairs={{0,1},{1,0},{2,3},{3,2},{4,5},{5,4},{6,7},{7,6},{8,9},{9,8},{10,11... | collective-permute-start | bytes 786440 | tf_op jit(solution)/shard_map/ppermute | solution.py:20
  (15 other events, 32.7 us)

commit v3 on v2

--- a/solution.py
+++ b/solution.py
@@ -131,18 +131,7 @@
     return kernel_call(body, place, [*n_shards, both], [2 * order] if join else [order] * 2, 1, after)
 
 
-def one_column(place, n_shards, value, after=()):
-    shards, order, width = len(n_shards), *value.shape
-
-    def body(starts, bases, refs, outs, scratch):
-        assemble(*scratch, refs[:shards], starts, width)
-        result = polynomial(*scratch, load_rows(refs[shards], starts, width))
-        store_rows(outs[0], starts, width, result)
-
-    return kernel_call(body, place, [*n_shards, value], [order], 1, after)[0]
-
-
-def joined_column(place, n_shards, value, one, two):
+def joined_column(place, n_shards, value, one, two, after=()):
     shards, order, width = len(n_shards), *value.shape
 
     def body(starts, bases, refs, outs, scratch):
@@ -152,23 +141,43 @@
             out[:order, :] = top[...]
             store_rows(out, starts, width, result, order)
 
-    return kernel_call(body, place, [*n_shards, value, one, two], [2 * order] * 2, 1)
-
-
-def coupled_reduced(place, both_shards, base, one, two, after=()):
+    return kernel_call(body, place, [*n_shards, value, one, two], [2 * order] * 2, 1, after)
+
+
+def one_column(place, n_shards, value, after=()):
+    shards, order, width = len(n_shards), *value.shape
+
+    def body(starts, bases, refs, outs, scratch):
+        assemble(*scratch, refs[:shards], starts, width)
+        result = polynomial(*scratch, load_rows(refs[shards], starts, width))
+        store_rows(outs[0], starts, width, result)
+
+    return kernel_call(body, place, [*n_shards, value], [order], 1, after)[0]
+
+
+def advanced(place, both_shards, n_shards, base, one, two, join, after=()):
     shards, order, width = len(both_shards), *base.shape
 
     def body(starts, bases, refs, outs, scratch):
-        total = load_rows(refs[shards], starts, width)
+        total = load_rows(refs[2 * shards], starts, width)
+        value = []
         for m in range(2):
             assemble(*scratch[2 * m : 2 * m + 2], refs[:shards], starts, width, m * order)
-            right = [load_rows(refs[shards + 1 + m], starts, width, at) for at in (0, order)]
+            right = [load_rows(refs[2 * shards + 1 + m], starts, width, at) for at in (0, order)]
             found = three_pass(*scratch[2 * m : 2 * m + 2], jnp.concatenate(right, axis=1))
             store_rows(outs[0], starts, width, -found[:, :width], m * order)
+            value.append(-found[:, :width])
             total = total - found[:, width:]
         store_rows(outs[1], starts, width, total)
-
-    return kernel_call(body, place, [*both_shards, base, one, two], [2 * order, order], 2, after)
+        assemble(*scratch[4:], refs[shards : 2 * shards], starts, width)
+        result = polynomial(*scratch[4:], jnp.concatenate(value, axis=1))
+        places = ((outs[2], 0), (outs[2], order)) if join else ((outs[2], 0), (outs[3], 0))
+        for k, (ref, at) in enumerate(places):
+            store_rows(ref, starts, width, result[:, k * width : (k + 1) * width], at)
+
+    operands = [*both_shards, *n_shards, base, one, two]
+    outs = [2 * order, order] + ([2 * order] if join else [order] * 2)
+    return kernel_call(body, place, operands, outs, 3, after)
 
 
 def reduced(place, both_shards, base, one, two, swap=False, after=(), cost=0):
@@ -322,51 +331,52 @@
     far_first = send(near_first, "blk", onward)
     right = loaded(right_side[0], got_slots, first)
     solved = one_column(place, n_shards, right)
-    diag = reduced(place, both_shards, diag, far_first, near_second, swap=True, after=[solved])
+    near_second, solved = tied(near_second, solved)
+    diag = reduced(place, both_shards, diag, far_first, near_second, swap=True, cost=20)
     n_far = across(diag)
     far_second = send(near_second, "blk", onward)
-    both = coupled(place, both_shards, far_second, near_first, swap=True, after=[solved])
+    both = coupled(place, both_shards, far_second, near_first, swap=True, after=[diag])
+    near_solved = send(solved, "blk", partner)
     n_far, both = tied(n_far, both)
     n_shards = gathered(diag, n_far)
-    near_solved = send(solved, "blk", partner)
     far_solved = send(near_solved, "blk", onward)
-    waiting = (both_shards, right, far_solved, near_solved, True)
+    right = reduced(place, both_shards, right, far_solved, near_solved, swap=True, cost=20)
 
     stride = 2
+    closing = lambda level, stride: level == levels - 1 and 2 * stride == cycle_size
+    pieces = normalized(place, n_shards, both, join=closing(1, stride))
     for level in range(1, levels):
         ahead = lambda source: (source + stride) % cycle_size
         back = lambda source: (source - stride) % cycle_size
         both_far = across(both)
         half = max(both_far)
-        last = level == levels - 1
-        if last and 2 * stride == cycle_size:
-            right = reduced(place, *waiting)
-            (pair,) = normalized(place, n_shards, both, join=True, after=[right])
+        if closing(level, stride):
+            (pair,) = pieces
             got = send(pair, "blk", ahead)
-            both_far[half], got = tied(both_far[half], got)
+            both_far[half], late = tied(both_far[half], pair)
             both_shards = gathered(both, both_far)
-            solved = one_column(place, n_shards, right, after=[pair])
-            low_y = up_y = send(solved, "blk", ahead)
-            diag = reduced(place, both_shards, diag, got, got, after=[solved])
+            solved = one_column(place, n_shards, right, after=[late])
+            solved, got = tied(solved, got)
+            low_y = send(solved, "blk", ahead)
+            diag = reduced(place, both_shards, diag, got, got)
+            n_far = across(diag)
+            n_far[half], low_y = tied(n_far[half], low_y)
+            right = reduced(place, both_shards, right, low_y, low_y, after=[diag], cost=20)
+            n_shards = gathered(diag, n_far)
         else:
-            p_row, q_row = normalized(place, n_shards, both)
+            p_row, q_row = pieces
             low_q, up_p = send(q_row, "blk", ahead), send(p_row, "blk", back)
-            both_far[half], low_q, up_p, p_row, q_row = tied(both_far[half], low_q, up_p, p_row, q_row)
+            p_solved, q_solved = joined_column(place, n_shards, right, p_row, q_row)
+            both_far[half], low_q, up_p, p_solved, q_solved = tied(
+                both_far[half], low_q, up_p, p_solved, q_solved
+            )
             both_shards = gathered(both, both_far)
-            right = reduced(place, *waiting, after=[q_row], cost=20)
-            diag = reduced(place, both_shards, diag, low_q, up_p, after=[right])
-            solved = one_column(place, n_shards, right, after=[diag])
-            low_y, up_y = send(solved, "blk", ahead), send(solved, "blk", back)
-        n_far = across(diag)
-        if last:
-            right = reduced(place, both_shards, right, low_y, up_y, after=[diag], cost=20)
-            n_far, right = tied(n_far, right)
-        else:
-            low_p, up_q = send(p_row, "blk", ahead), send(q_row, "blk", back)
-            both = coupled(place, both_shards, low_p, up_q, after=[diag])
-            n_far, both = tied(n_far, both)
-            waiting = (both_shards, right, low_y, up_y, False)
-        n_shards = gathered(diag, n_far)
+            diag = reduced(place, both_shards, diag, low_q, up_p)
+            n_shards = gathered(diag, across(diag))
+            low, up = send(p_solved, "blk", ahead), send(q_solved, "blk", back)
+            both, right, *pieces = advanced(
+                place, both_shards, n_shards, right, low, up, closing(level + 1, 2 * stride)
+            )
         stride = 2 * stride
     return one_column(place, n_shards, right)[None]
 

time: 148 us -> 144 us (0.973); the launches traced: 148 us -> 142 us
  starting transfers between devices: 37.5 us -> 34.7 us
  waiting for transfers between devices: 76.2 us -> 74.3 us
    ppermute x35 -> x33, starting transfers between devices: 31.5 us -> 28.8 us  [send(): return lax.ppermute(value, axis, pairs)]
    ppermute x35 -> x33, waiting for transfers between devices: 76.2 us -> 74.3 us  [send(): return lax.ppermute(value, axis, pairs)]
    pallas_call x16 -> x14, Pallas kernels: 26.9 us -> 26.1 us  [kernel_call(): pl.pallas_call(kernel, out_shape=[jax.ShapeDtypeStruct((rows, width), f32...]
    unnamed x22 -> x18, local copies, waits for them, and re-layouts: 4.26 us -> 4.23 us
  transfers between devices with their start and end apart: 36 -> 34, of which waited for: 19 -> 19; matrix products, arithmetic and copies ran while one was open for 0% -> 0% of each run, Pallas kernels for 18% -> 16%
where the time goes in v3:
time: 144 us; the launch traced here: 142 us
  waiting for transfers between devices  74.3 us (52%)
  starting transfers between devices  34.7 us (24%)
  Pallas kernels  28.3 us (20%)
  local copies, waits for them, and re-layouts  4.23 us (3%)
    ppermute x33, waiting for transfers between devices, send(): return lax.ppermute(value, axis, pairs)  74.3 us
    ppermute x33, starting transfers between devices, send(): return lax.ppermute(value, axis, pairs)  28.8 us
    pallas_call x14, Pallas kernels, kernel_call(): pl.pallas_call(kernel, out_shape=[jax.ShapeDtypeStruct((rows, width), f32...  26.1 us
    all_to_all x1, starting transfers between devices, on_device(): lax.all_to_all(slots.reshape(cycle_size, -1, slots.shape[1]), 'blk', spli...  5.96 us
    unnamed x18, local copies, waits for them, and re-layouts  4.23 us
  transfers between devices with their start and end apart: 34, of which 19 were waited for; matrix products, arithmetic and copies ran while one was open for 0% of the time, Pallas kernels for 16%

profile of v3, /device:TPU:0, one launch (start us, length us, event | category | flops | bytes accessed | tf_op | source)
XLA Modules:
  0.0 142.5 jit_solution(7741372943502072321)
XLA Ops:
  0.0 2.9 %collective-permute-start = (f32[512,128]{1,0:T(8,128)}, f32[512,128]{1,0:T(8,128)S(1)}, u32[]{:S(2)}, u32[]{:S(2)}) collective-permute-start(f32[512,128]{1,0:T(8,128)} %bitcast.12), channel_id=1, source_target_pairs={{0,2},{1,3},{2,0},{3,1},{4,6},{5,7},{6,4},{7,5},{8,10},{9,11},{10,... | collective-permute-start | bytes 786440 | tf_op jit(solution)/shard_map/ppermute | solution.py:20
  5.2 1.5 %shard_map.82.refs_2_ = f32[1088,128]{1,0:T(8,128)} custom-call(s32[1]{0:T(128)S(6)} %copy.9.counts, s32[1,512]{1,0:T(1,128)S(1)} %bitcast.20, s32[1,512]{1,0:T(1,128)S(1)} %bitcast.21, f32[512,128]{1,0:T(8,128)S(1)} %copy-done.1), custom_call_target="tpu_custom_call" | custom-call | flops 1 | bytes 1 | tf_op jit(solution)/shard_map/pallas_call | solution.py:266
  6.7 6.0 %all-to-all-start = ((f32[8,136,128]{2,1,0:T(8,128)}), f32[8,136,128]{2,1,0:T(8,128)S(1)}, u32[]{:S(2)}, u32[]{:S(2)}) async-start(f32[8,136,128]{2,1,0:T(8,128)} %bitcast.7), calls=%async_computation | async-start | bytes 1114112 | tf_op jit(solution)/shard_map/all_to_all | solution.py:323
  15.9 2.9 %shard_map.84 = (f32[512,128]{1,0:T(8,128)S(1)}, f32[512,128]{1,0:T(8,128)}) custom-call(s32[2]{0:T(128)S(1)} %pad_add_fusion.place_ref, f32[512,128]{1,0:T(8,128)S(1)} %bitcast.14, f32[512,128]{1,0:T(8,128)S(1)} %collective-permute-done.4.refs_1_, f32[512,128]{1,0:T(8,128)S(1)} %collective-permute-done.refs_2_, ...), custom_call_target="tpu_custom_call" | custom-call | flops 1 | bytes 1 | tf_op jit(solution)/shard_map/pallas_call | solution.py:95
  18.9 2.0 %collective-permute-start.6 = (f32[512,128]{1,0:T(8,128)S(1)}, f32[512,128]{1,0:T(8,128)S(1)}, u32[]{:S(2)}, u32[]{:S(2)}) collective-permute-start(f32[512,128]{1,0:T(8,128)S(1)} %get-tuple-element.35._), channel_id=1, source_target_pairs={{0,4},{4,0},{8,12},{12,8},{16,20},{20,16},{24,28},{28,24},{1,5},{5... | collective-permute-start | bytes 786440 | tf_op jit(solution)/shard_map/ppermute | solution.py:20
  21.6 5.0 %collective-permute-done.2.refs_2_ = f32[1024,128]{1,0:T(8,128)S(1)} collective-permute-done((f32[1024,128]{1,0:T(8,128)S(1)}, f32[1024,128]{1,0:T(8,128)S(1)}, u32[]{:S(2)}, u32[]{:S(2)}) %collective-permute-start.2) | collective-permute-done | bytes 524320 | tf_op jit(solution)/shard_map/ppermute | solution.py:20
  26.6 1.7 %collective-permute-start.8 = (f32[512,128]{1,0:T(8,128)}, f32[512,128]{1,0:T(8,128)}, u32[]{:S(2)}, u32[]{:S(2)}) collective-permute-start(f32[512,128]{1,0:T(8,128)} %get-tuple-element.37), channel_id=1, source_target_pairs={{0,4},{4,0},{8,12},{12,8},{16,20},{20,16},{24,28},{28,24},{1,5},{5... | collective-permute-start | bytes 786440 | tf_op jit(solution)/shard_map/ppermute | solution.py:20
  28.9 1.9 %collective-permute-start.7 = (f32[512,128]{1,0:T(8,128)S(1)}, f32[512,128]{1,0:T(8,128)S(1)}, u32[]{:S(2)}, u32[]{:S(2)}) collective-permute-start(f32[512,128]{1,0:T(8,128)S(1)} %collective-permute-done.6.refs_5_), channel_id=1, source_target_pairs={{0,8},{4,28},{8,16},{12,4},{16,24},{20,12},{24,0},{28,20},{1,9},{5... | collective-permute-start | bytes 786440 | tf_op jit(solution)/shard_map/ppermute | solution.py:20
  33.4 1.7 %shard_map.86 = f32[512,128]{1,0:T(8,128)S(1)} custom-call(s32[2]{0:T(128)S(1)} %pad_add_fusion.place_ref, f32[512,128]{1,0:T(8,128)S(1)} %bitcast.15, f32[512,128]{1,0:T(8,128)S(1)} %collective-permute-done.4.refs_1_, f32[512,128]{1,0:T(8,128)S(1)} %collective-permute-done.refs_2_, f32[512,128]{1,0:T(8,128)S(1)} %collective-permute-done.5.refs_3_, ...), custom_call_target="tpu_custom_call" | custom-call | flops 1 | bytes 1 | tf_op jit(solution)/shard_map/pallas_call | solution.py:95
  35.6 1.7 %collective-permute-start.10 = (f32[512,128]{1,0:T(8,128)}, f32[512,128]{1,0:T(8,128)S(1)}, u32[]{:S(2)}, u32[]{:S(2)}) collective-permute-start(f32[512,128]{1,0:T(8,128)} %collective-permute-done.8.refs_6_), channel_id=1, source_target_pairs={{0,8},{4,28},{8,16},{12,4},{16,24},{20,12},{24,0},{28,20},{1,9},{5... | collective-permute-start | bytes 786440 | tf_op jit(solution)/shard_map/ppermute | solution.py:20
  38.7 1.8 %shard_map.87.refs_6_.refs_0_.refs_4_ = f32[512,128]{1,0:T(8,128)S(1)} custom-call(s32[2]{0:T(128)S(1)} %pad_add_fusion.place_ref, f32[1024,128]{1,0:T(8,128)S(1)} %shard_map.83.refs_4_.refs_0_, f32[1024,128]{1,0:T(8,128)S(1)} %collective-permute-done.1.refs_1_, f32[1024,128]{1,0:T(8,128)S(1)} %collective-permute-done.2.refs_2_, ...), custom_call_target="tpu_custom_call" | custom-call | flops 23000000512 | bytes 73800000 | tf_op jit(solution)/shard_map/pallas_call | solution.py:95
  43.1 2.5 %collective-permute-done.10.refs_4_ = f32[512,128]{1,0:T(8,128)S(1)} collective-permute-done((f32[512,128]{1,0:T(8,128)}, f32[512,128]{1,0:T(8,128)S(1)}, u32[]{:S(2)}, u32[]{:S(2)}) %collective-permute-start.10) | collective-permute-done | bytes 262176 | tf_op jit(solution)/shard_map/ppermute | solution.py:20
  45.6 1.8 %shard_map.88.refs_4_.refs_0_ = f32[1024,128]{1,0:T(8,128)S(1)} custom-call(s32[2]{0:T(128)S(1)} %pad_add_fusion.place_ref, f32[1024,128]{1,0:T(8,128)S(1)} %shard_map.83.refs_4_.refs_0_, f32[1024,128]{1,0:T(8,128)S(1)} %collective-permute-done.1.refs_1_, f32[1024,128]{1,0:T(8,128)S(1)} %collective-permute-done.2.refs_2_, ...), custom_call_target="tpu_custom_call" | custom-call | flops 1 | bytes 1 | tf_op jit(solution)/shard_map/pallas_call | solution.py:95
  50.2 2.3 %shard_map.89 = (f32[512,128]{1,0:T(8,128)S(1)}, f32[512,128]{1,0:T(8,128)S(1)}) custom-call(s32[2]{0:T(128)S(1)} %pad_add_fusion.place_ref, f32[512,128]{1,0:T(8,128)S(1)} %shard_map.87.refs_6_.refs_0_.refs_4_, f32[512,128]{1,0:T(8,128)S(1)} %collective-permute-done.13.refs_1_, f32[512,128]{1,0:T(8,128)S(1)} %collective-permute-done.9.refs_2_, ...), custom_call_target="tpu_custom_call" | custom-call | flops 1 | bytes 1 | tf_op jit(solution)/shard_map/pallas_call | solution.py:95
  52.5 1.5 %collective-permute-start.15 = (f32[512,128]{1,0:T(8,128)S(1)}, f32[512,128]{1,0:T(8,128)S(1)}, u32[]{:S(2)}, u32[]{:S(2)}) collective-permute-start(f32[512,128]{1,0:T(8,128)S(1)} %get-tuple-element.42.refs_6_), channel_id=1, source_target_pairs={{0,8},{4,12},{8,16},{12,20},{16,24},{20,28},{24,0},{28,4},{1,9},{5... | collective-permute-start | bytes 786440 | tf_op jit(solution)/shard_map/ppermute | solution.py:20
  54.0 2.5 %collective-permute-start.16 = (f32[512,128]{1,0:T(8,128)S(1)}, f32[512,128]{1,0:T(8,128)S(1)}, u32[]{:S(2)}, u32[]{:S(2)}) collective-permute-start(f32[512,128]{1,0:T(8,128)S(1)} %get-tuple-element.43.refs_5_), channel_id=1, source_target_pairs={{0,24},{4,28},{8,0},{12,4},{16,8},{20,12},{24,16},{28,20},{1,25},{... | collective-permute-start | bytes 786440 | tf_op jit(solution)/shard_map/ppermute | solution.py:20
  56.5 3.4 %collective-permute-done.18.refs_5_ = f32[512,128]{1,0:T(8,128)S(1)} collective-permute-done((f32[512,128]{1,0:T(8,128)S(1)}, f32[512,128]{1,0:T(8,128)S(1)}, u32[]{:S(2)}, u32[]{:S(2)}) %collective-permute-start.18) | collective-permute-done | bytes 262176 | tf_op jit(solution)/shard_map/ppermute | solution.py:20
  59.9 1.8 %shard_map.90.refs_4_.refs_8_ = f32[512,128]{1,0:T(8,128)S(1)} custom-call(s32[2]{0:T(128)S(1)} %pad_add_fusion.place_ref, f32[1024,128]{1,0:T(8,128)S(1)} %shard_map.83.refs_4_.refs_0_, f32[1024,128]{1,0:T(8,128)S(1)} %collective-permute-done.1.refs_1_, f32[1024,128]{1,0:T(8,128)S(1)} %collective-permute-done.2.refs_2_, ...), custom_call_target="tpu_custom_call" | custom-call | flops 23000000512 | bytes 73800000 | tf_op jit(solution)/shard_map/pallas_call | solution.py:95
  61.8 1.7 %shard_map.91 = (f32[1024,128]{1,0:T(8,128)S(1)}, f32[1024,128]{1,0:T(8,128)S(1)}) custom-call(s32[2]{0:T(128)S(1)} %pad_add_fusion.place_ref, f32[512,128]{1,0:T(8,128)S(1)} %shard_map.87.refs_6_.refs_0_.refs_4_, f32[512,128]{1,0:T(8,128)S(1)} %collective-permute-done.13.refs_1_, f32[512,128]{1,0:T(8,128)S(1)} %collective-permute-done.9.refs_2_, ...), custom_call_target="tpu_custom_call" | custom-call | flops 1 | bytes 1 | tf_op jit(solution)/shard_map/pallas_call | solution.py:95
  63.5 1.9 %collective-permute-done.15.refs_5_ = f32[512,128]{1,0:T(8,128)S(1)} collective-permute-done((f32[512,128]{1,0:T(8,128)S(1)}, f32[512,128]{1,0:T(8,128)S(1)}, u32[]{:S(2)}, u32[]{:S(2)}) %collective-permute-start.15) | collective-permute-done | bytes 262176 | tf_op jit(solution)/shard_map/ppermute | solution.py:20
  65.4 4.1 %collective-permute-done.16.refs_6_ = f32[512,128]{1,0:T(8,128)S(1)} collective-permute-done((f32[512,128]{1,0:T(8,128)S(1)}, f32[512,128]{1,0:T(8,128)S(1)}, u32[]{:S(2)}, u32[]{:S(2)}) %collective-permute-start.16) | collective-permute-done | bytes 262176 | tf_op jit(solution)/shard_map/ppermute | solution.py:20
  70.1 3.2 %collective-permute-start.24 = (f32[1024,128]{1,0:T(8,128)S(1)}, f32[1024,128]{1,0:T(8,128)S(1)}, u32[]{:S(2)}, u32[]{:S(2)}) collective-permute-start(f32[1024,128]{1,0:T(8,128)S(1)} %get-tuple-element.51), channel_id=1, source_target_pairs={{0,24},{4,28},{8,0},{12,4},{16,8},{20,12},{24,16},{28,20},{1,25},{... | collective-permute-start | bytes 1572872 | tf_op jit(solution)/shard_map/ppermute | solution.py:20
  75.9 7.1 %collective-permute-done.21.refs_6_.refs_2_ = f32[512,128]{1,0:T(8,128)S(1)} collective-permute-done((f32[512,128]{1,0:T(8,128)S(1)}, f32[512,128]{1,0:T(8,128)S(1)}, u32[]{:S(2)}, u32[]{:S(2)}) %collective-permute-start.21) | collective-permute-done | bytes 262176 | tf_op jit(solution)/shard_map/ppermute | solution.py:20
  82.9 3.2 %collective-permute-done.23.refs_9_ = f32[1024,128]{1,0:T(8,128)S(1)} collective-permute-done((f32[1024,128]{1,0:T(8,128)S(1)}, f32[1024,128]{1,0:T(8,128)S(1)}, u32[]{:S(2)}, u32[]{:S(2)}) %collective-permute-start.23) | collective-permute-done | bytes 524320 | tf_op jit(solution)/shard_map/ppermute | solution.py:20
  86.1 9.3 %collective-permute-done.24.refs_10_ = f32[1024,128]{1,0:T(8,128)S(1)} collective-permute-done((f32[1024,128]{1,0:T(8,128)S(1)}, f32[1024,128]{1,0:T(8,128)S(1)}, u32[]{:S(2)}, u32[]{:S(2)}) %collective-permute-start.24) | collective-permute-done | bytes 524320 | tf_op jit(solution)/shard_map/ppermute | solution.py:20
  95.4 3.3 %shard_map.93 = (f32[1024,128]{1,0:T(8,128)S(1)}, f32[512,128]{1,0:T(8,128)S(1)}, f32[1024,128]{1,0:T(8,128)S(1)}) custom-call(s32[2]{0:T(128)S(1)} %pad_add_fusion.place_ref, f32[1024,128]{1,0:T(8,128)S(1)} %shard_map.88.refs_4_.refs_0_, f32[1024,128]{1,0:T(8,128)S(1)} %collective-permute-done.11.refs_1_, f32[1024,128]{1,0:T(8,128)S(1)} %collective-permute-done.12.refs_2_, ...), custom_call_target="tpu_custom_call" | custom-call | flops 1 | bytes 1 | tf_op jit(solution)/shard_map/pallas_call | solution.py:95
  99.9 2.1 %collective-permute-start.28 = (f32[1024,128]{1,0:T(8,128)S(1)}, f32[1024,128]{1,0:T(8,128)S(1)}, u32[]{:S(2)}, u32[]{:S(2)}) collective-permute-start(f32[1024,128]{1,0:T(8,128)S(1)} %get-tuple-element.56.refs_5_), channel_id=1, source_target_pairs={{0,16},{4,20},{8,24},{12,28},{16,0},{20,4},{24,8},{28,12},{1,17},{... | collective-permute-start | bytes 1572872 | tf_op jit(solution)/shard_map/ppermute | solution.py:20
  102.0 10.0 %collective-permute-done.26.refs_2_ = f32[1024,128]{1,0:T(8,128)S(1)} collective-permute-done((f32[1024,128]{1,0:T(8,128)S(1)}, f32[1024,128]{1,0:T(8,128)S(1)}, u32[]{:S(2)}, u32[]{:S(2)}) %collective-permute-start.26) | collective-permute-done | bytes 524320 | tf_op jit(solution)/shard_map/ppermute | solution.py:20
  112.0 1.7 %shard_map.94 = f32[512,128]{1,0:T(8,128)S(1)} custom-call(s32[2]{0:T(128)S(1)} %pad_add_fusion.place_ref, f32[512,128]{1,0:T(8,128)S(1)} %shard_map.92.refs_4_.refs_0_, f32[512,128]{1,0:T(8,128)S(1)} %collective-permute-done.20.refs_5_.refs_1_, f32[512,128]{1,0:T(8,128)S(1)} %collective-permute-done.21.refs_6_.refs_2_, ...), custom_call_target="tpu_custom_call" | custom-call | flops 1 | bytes 1 | tf_op jit(solution)/shard_map/pallas_call | solution.py:95
  113.8 11.2 %collective-permute-done.28.refs_5_ = f32[1024,128]{1,0:T(8,128)S(1)} collective-permute-done((f32[1024,128]{1,0:T(8,128)S(1)}, f32[1024,128]{1,0:T(8,128)S(1)}, u32[]{:S(2)}, u32[]{:S(2)}) %collective-permute-start.28) | collective-permute-done | bytes 524320 | tf_op jit(solution)/shard_map/ppermute | solution.py:20
  127.3 11.1 %collective-permute-done.31.refs_5_ = f32[512,128]{1,0:T(8,128)S(1)} collective-permute-done((f32[512,128]{1,0:T(8,128)S(1)}, f32[512,128]{1,0:T(8,128)S(1)}, u32[]{:S(2)}, u32[]{:S(2)}) %collective-permute-start.31) | collective-permute-done | bytes 262176 | tf_op jit(solution)/shard_map/ppermute | solution.py:20
  140.0 2.4 %shard_map.97 = f32[512,128]{1,0:T(8,128)} custom-call(s32[2]{0:T(128)S(1)} %pad_add_fusion.place_ref, f32[512,128]{1,0:T(8,128)S(1)} %shard_map.95.refs_6_.refs_0_, f32[512,128]{1,0:T(8,128)S(1)} %collective-permute-done.29.refs_1_, f32[512,128]{1,0:T(8,128)S(1)} %collective-permute-done.30.refs_2_, f32[512,128]{1,0:T(8,128)S(1)} %collective-permute-done.32.refs_3_, ...), custom_call_target="tpu_custom_call" | custom-call | flops 1 | bytes 1 | tf_op jit(solution)/shard_map/pallas_call | solution.py:95
  (71 shorter events, 24.1 us)
Async XLA Ops:
  0.0 13.4 %collective-permute-start = (f32[512,128]{1,0:T(8,128)}, f32[512,128]{1,0:T(8,128)S(1)}, u32[]{:S(2)}, u32[]{:S(2)}) collective-permute-start(f32[512,128]{1,0:T(8,128)} %bitcast.12), channel_id=1, source_target_pairs={{0,2},{1,3},{2,0},{3,1},{4,6},{5,7},{6,4},{7,5},{8,10},{9,11},{10,... | collective-permute-start | bytes 786440 | tf_op jit(solution)/shard_map/ppermute | solution.py:20
  6.7 22.2 %all-to-all-start = ((f32[8,136,128]{2,1,0:T(8,128)}), f32[8,136,128]{2,1,0:T(8,128)S(1)}, u32[]{:S(2)}, u32[]{:S(2)}) async-start(f32[8,136,128]{2,1,0:T(8,128)} %bitcast.7), calls=%async_computation | async-start | bytes 1114112 | tf_op jit(solution)/shard_map/all_to_all | solution.py:323
  13.4 13.2 %collective-permute-start.2 = (f32[1024,128]{1,0:T(8,128)S(1)}, f32[1024,128]{1,0:T(8,128)S(1)}, u32[]{:S(2)}, u32[]{:S(2)}) collective-permute-start(f32[1024,128]{1,0:T(8,128)S(1)} %shard_map.83.refs_4_.refs_0_), channel_id=1, source_target_pairs={{0,2},{1,3},{2,0},{3,1},{4,6},{5,7},{6,4},{7,5},{8,10},{9,11},{10,... | collective-permute-start | bytes 1572872 | tf_op jit(solution)/shard_map/ppermute | solution.py:20
  14.0 1.9 %collective-permute-start.5 = (f32[512,128]{1,0:T(8,128)S(1)}, f32[512,128]{1,0:T(8,128)S(1)}, u32[]{:S(2)}, u32[]{:S(2)}) collective-permute-start(f32[512,128]{1,0:T(8,128)S(1)} %collective-permute-done.refs_2_), channel_id=1, source_target_pairs={{0,1},{1,0},{2,3},{3,2},{4,5},{5,4},{6,7},{7,6},{8,9},{9,8},{10,11... | collective-permute-start | bytes 786440 | tf_op jit(solution)/shard_map/ppermute | solution.py:20
  18.9 10.1 %collective-permute-start.6 = (f32[512,128]{1,0:T(8,128)S(1)}, f32[512,128]{1,0:T(8,128)S(1)}, u32[]{:S(2)}, u32[]{:S(2)}) collective-permute-start(f32[512,128]{1,0:T(8,128)S(1)} %get-tuple-element.35._), channel_id=1, source_target_pairs={{0,4},{4,0},{8,12},{12,8},{16,20},{20,16},{24,28},{28,24},{1,5},{5... | collective-permute-start | bytes 786440 | tf_op jit(solution)/shard_map/ppermute | solution.py:20
  21.6 15.8 %collective-permute-start.1 = (f32[1024,128]{1,0:T(8,128)S(1)}, f32[1024,128]{1,0:T(8,128)S(1)}, u32[]{:S(2)}, u32[]{:S(2)}) collective-permute-start(f32[1024,128]{1,0:T(8,128)S(1)} %shard_map.83.refs_4_.refs_0_), channel_id=1, source_target_pairs={{0,1},{1,0},{2,3},{3,2},{4,5},{5,4},{6,7},{7,6},{8,9},{9,8},{10,11... | collective-permute-start | bytes 1572872 | tf_op jit(solution)/shard_map/ppermute | solution.py:20
  26.6 12.2 %collective-permute-start.3 = (f32[1024,128]{1,0:T(8,128)S(1)}, f32[1024,128]{1,0:T(8,128)}, u32[]{:S(2)}, u32[]{:S(2)}) collective-permute-start(f32[1024,128]{1,0:T(8,128)S(1)} %collective-permute-done.2.refs_2_), channel_id=1, source_target_pairs={{0,1},{1,0},{2,3},{3,2},{4,5},{5,4},{6,7},{7,6},{8,9},{9,8},{10,11... | collective-permute-start | bytes 1572872 | tf_op jit(solution)/shard_map/ppermute | solution.py:20
  26.6 9.0 %collective-permute-start.8 = (f32[512,128]{1,0:T(8,128)}, f32[512,128]{1,0:T(8,128)}, u32[]{:S(2)}, u32[]{:S(2)}) collective-permute-start(f32[512,128]{1,0:T(8,128)} %get-tuple-element.37), channel_id=1, source_target_pairs={{0,4},{4,0},{8,12},{12,8},{16,20},{20,16},{24,28},{28,24},{1,5},{5... | collective-permute-start | bytes 786440 | tf_op jit(solution)/shard_map/ppermute | solution.py:20
  28.9 9.8 %collective-permute-start.7 = (f32[512,128]{1,0:T(8,128)S(1)}, f32[512,128]{1,0:T(8,128)S(1)}, u32[]{:S(2)}, u32[]{:S(2)}) collective-permute-start(f32[512,128]{1,0:T(8,128)S(1)} %collective-permute-done.6.refs_5_), channel_id=1, source_target_pairs={{0,8},{4,28},{8,16},{12,4},{16,24},{20,12},{24,0},{28,20},{1,9},{5... | collective-permute-start | bytes 786440 | tf_op jit(solution)/shard_map/ppermute | solution.py:20
  35.6 9.9 %collective-permute-start.10 = (f32[512,128]{1,0:T(8,128)}, f32[512,128]{1,0:T(8,128)S(1)}, u32[]{:S(2)}, u32[]{:S(2)}) collective-permute-start(f32[512,128]{1,0:T(8,128)} %collective-permute-done.8.refs_6_), channel_id=1, source_target_pairs={{0,8},{4,28},{8,16},{12,4},{16,24},{20,12},{24,0},{28,20},{1,9},{5... | collective-permute-start | bytes 786440 | tf_op jit(solution)/shard_map/ppermute | solution.py:20
  40.6 7.2 %collective-permute-start.9 = (f32[512,128]{1,0:T(8,128)S(1)}, f32[512,128]{1,0:T(8,128)S(1)}, u32[]{:S(2)}, u32[]{:S(2)}) collective-permute-start(f32[512,128]{1,0:T(8,128)S(1)} %shard_map.87.refs_6_.refs_0_.refs_4_), channel_id=1, source_target_pairs={{0,2},{1,3},{2,0},{3,1},{4,6},{5,7},{6,4},{7,5},{8,10},{9,11},{10,... | collective-permute-start | bytes 786440 | tf_op jit(solution)/shard_map/ppermute | solution.py:20
  41.7 7.0 %collective-permute-start.17 = (f32[512,128]{1,0:T(8,128)S(1)}, f32[512,128]{1,0:T(8,128)S(1)}, u32[]{:S(2)}, u32[]{:S(2)}) collective-permute-start(f32[512,128]{1,0:T(8,128)S(1)} %shard_map.86), channel_id=1, source_target_pairs={{0,4},{4,0},{8,12},{12,8},{16,20},{20,16},{24,28},{28,24},{1,5},{5... | collective-permute-start | bytes 786440 | tf_op jit(solution)/shard_map/ppermute | solution.py:20
  43.1 7.1 %collective-permute-start.13 = (f32[512,128]{1,0:T(8,128)S(1)}, f32[512,128]{1,0:T(8,128)S(1)}, u32[]{:S(2)}, u32[]{:S(2)}) collective-permute-start(f32[512,128]{1,0:T(8,128)S(1)} %shard_map.87.refs_6_.refs_0_.refs_4_), channel_id=1, source_target_pairs={{0,1},{1,0},{2,3},{3,2},{4,5},{5,4},{6,7},{7,6},{8,9},{9,8},{10,11... | collective-permute-start | bytes 786440 | tf_op jit(solution)/shard_map/ppermute | solution.py:20
  47.8 2.5 %collective-permute-start.14 = (f32[512,128]{1,0:T(8,128)S(1)}, f32[512,128]{1,0:T(8,128)S(1)}, u32[]{:S(2)}, u32[]{:S(2)}) collective-permute-start(f32[512,128]{1,0:T(8,128)S(1)} %collective-permute-done.9.refs_2_), channel_id=1, source_target_pairs={{0,1},{1,0},{2,3},{3,2},{4,5},{5,4},{6,7},{7,6},{8,9},{9,8},{10,11... | collective-permute-start | bytes 786440 | tf_op jit(solution)/shard_map/ppermute | solution.py:20
  48.7 11.2 %collective-permute-start.18 = (f32[512,128]{1,0:T(8,128)S(1)}, f32[512,128]{1,0:T(8,128)S(1)}, u32[]{:S(2)}, u32[]{:S(2)}) collective-permute-start(f32[512,128]{1,0:T(8,128)S(1)} %collective-permute-done.17.refs_6_), channel_id=1, source_target_pairs={{0,8},{4,28},{8,16},{12,4},{16,24},{20,12},{24,0},{28,20},{1,9},{5... | collective-permute-start | bytes 786440 | tf_op jit(solution)/shard_map/ppermute | solution.py:20
  48.8 20.7 %collective-permute-start.12 = (f32[1024,128]{1,0:T(8,128)S(1)}, f32[1024,128]{1,0:T(8,128)S(1)}, u32[]{:S(2)}, u32[]{:S(2)}) collective-permute-start(f32[1024,128]{1,0:T(8,128)S(1)} %shard_map.88.refs_4_.refs_0_), channel_id=1, source_target_pairs={{0,2},{1,3},{2,0},{3,1},{4,6},{5,7},{6,4},{7,5},{8,10},{9,11},{10,... | collective-permute-start | bytes 1572872 | tf_op jit(solution)/shard_map/ppermute | solution.py:20
  52.5 12.9 %collective-permute-start.15 = (f32[512,128]{1,0:T(8,128)S(1)}, f32[512,128]{1,0:T(8,128)S(1)}, u32[]{:S(2)}, u32[]{:S(2)}) collective-permute-start(f32[512,128]{1,0:T(8,128)S(1)} %get-tuple-element.42.refs_6_), channel_id=1, source_target_pairs={{0,8},{4,12},{8,16},{12,20},{16,24},{20,28},{24,0},{28,4},{1,9},{5... | collective-permute-start | bytes 786440 | tf_op jit(solution)/shard_map/ppermute | solution.py:20
  54.0 15.6 %collective-permute-start.16 = (f32[512,128]{1,0:T(8,128)S(1)}, f32[512,128]{1,0:T(8,128)S(1)}, u32[]{:S(2)}, u32[]{:S(2)}) collective-permute-start(f32[512,128]{1,0:T(8,128)S(1)} %get-tuple-element.43.refs_5_), channel_id=1, source_target_pairs={{0,24},{4,28},{8,0},{12,4},{16,8},{20,12},{24,16},{28,20},{1,25},{... | collective-permute-start | bytes 786440 | tf_op jit(solution)/shard_map/ppermute | solution.py:20
  61.7 11.7 %collective-permute-start.11 = (f32[1024,128]{1,0:T(8,128)S(1)}, f32[1024,128]{1,0:T(8,128)S(1)}, u32[]{:S(2)}, u32[]{:S(2)}) collective-permute-start(f32[1024,128]{1,0:T(8,128)S(1)} %shard_map.88.refs_4_.refs_0_), channel_id=1, source_target_pairs={{0,1},{1,0},{2,3},{3,2},{4,5},{5,4},{6,7},{7,6},{8,9},{9,8},{10,11... | collective-permute-start | bytes 1572872 | tf_op jit(solution)/shard_map/ppermute | solution.py:20
  69.5 3.8 %collective-permute-start.19 = (f32[1024,128]{1,0:T(8,128)S(1)}, f32[1024,128]{1,0:T(8,128)S(1)}, u32[]{:S(2)}, u32[]{:S(2)}) collective-permute-start(f32[1024,128]{1,0:T(8,128)S(1)} %collective-permute-done.12.refs_2_), channel_id=1, source_target_pairs={{0,1},{1,0},{2,3},{3,2},{4,5},{5,4},{6,7},{7,6},{8,9},{9,8},{10,11... | collective-permute-start | bytes 1572872 | tf_op jit(solution)/shard_map/ppermute | solution.py:20
  69.5 16.6 %collective-permute-start.23 = (f32[1024,128]{1,0:T(8,128)S(1)}, f32[1024,128]{1,0:T(8,128)S(1)}, u32[]{:S(2)}, u32[]{:S(2)}) collective-permute-start(f32[1024,128]{1,0:T(8,128)S(1)} %get-tuple-element.50), channel_id=1, source_target_pairs={{0,8},{4,12},{8,16},{12,20},{16,24},{20,28},{24,0},{28,4},{1,9},{5... | collective-permute-start | bytes 1572872 | tf_op jit(solution)/shard_map/ppermute | solution.py:20
  70.1 25.3 %collective-permute-start.24 = (f32[1024,128]{1,0:T(8,128)S(1)}, f32[1024,128]{1,0:T(8,128)S(1)}, u32[]{:S(2)}, u32[]{:S(2)}) collective-permute-start(f32[1024,128]{1,0:T(8,128)S(1)} %get-tuple-element.51), channel_id=1, source_target_pairs={{0,24},{4,28},{8,0},{12,4},{16,8},{20,12},{24,16},{28,20},{1,25},{... | collective-permute-start | bytes 1572872 | tf_op jit(solution)/shard_map/ppermute | solution.py:20
  74.7 8.2 %collective-permute-start.21 = (f32[512,128]{1,0:T(8,128)S(1)}, f32[512,128]{1,0:T(8,128)S(1)}, u32[]{:S(2)}, u32[]{:S(2)}) collective-permute-start(f32[512,128]{1,0:T(8,128)S(1)} %shard_map.92.refs_4_.refs_0_), channel_id=1, source_target_pairs={{0,2},{1,3},{2,0},{3,1},{4,6},{5,7},{6,4},{7,5},{8,10},{9,11},{10,... | collective-permute-start | bytes 786440 | tf_op jit(solution)/shard_map/ppermute | solution.py:20
  75.9 19.5 %collective-permute-start.20 = (f32[512,128]{1,0:T(8,128)S(1)}, f32[512,128]{1,0:T(8,128)S(1)}, u32[]{:S(2)}, u32[]{:S(2)}) collective-permute-start(f32[512,128]{1,0:T(8,128)S(1)} %shard_map.92.refs_4_.refs_0_), channel_id=1, source_target_pairs={{0,1},{1,0},{2,3},{3,2},{4,5},{5,4},{6,7},{7,6},{8,9},{9,8},{10,11... | collective-permute-start | bytes 786440 | tf_op jit(solution)/shard_map/ppermute | solution.py:20
  82.9 12.5 %collective-permute-start.22 = (f32[512,128]{1,0:T(8,128)S(1)}, f32[512,128]{1,0:T(8,128)S(1)}, u32[]{:S(2)}, u32[]{:S(2)}) collective-permute-start(f32[512,128]{1,0:T(8,128)S(1)} %collective-permute-done.21.refs_6_.refs_2_), channel_id=1, source_target_pairs={{0,1},{1,0},{2,3},{3,2},{4,5},{5,4},{6,7},{7,6},{8,9},{9,8},{10,11... | collective-permute-start | bytes 786440 | tf_op jit(solution)/shard_map/ppermute | solution.py:20
  98.7 13.3 %collective-permute-start.26 = (f32[1024,128]{1,0:T(8,128)S(1)}, f32[1024,128]{1,0:T(8,128)S(1)}, u32[]{:S(2)}, u32[]{:S(2)}) collective-permute-start(f32[1024,128]{1,0:T(8,128)S(1)} %get-tuple-element.52.refs_0_), channel_id=1, source_target_pairs={{0,2},{1,3},{2,0},{3,1},{4,6},{5,7},{6,4},{7,5},{8,10},{9,11},{10,... | collective-permute-start | bytes 1572872 | tf_op jit(solution)/shard_map/ppermute | solution.py:20
  99.9 25.1 %collective-permute-start.28 = (f32[1024,128]{1,0:T(8,128)S(1)}, f32[1024,128]{1,0:T(8,128)S(1)}, u32[]{:S(2)}, u32[]{:S(2)}) collective-permute-start(f32[1024,128]{1,0:T(8,128)S(1)} %get-tuple-element.56.refs_5_), channel_id=1, source_target_pairs={{0,16},{4,20},{8,24},{12,28},{16,0},{20,4},{24,8},{28,12},{1,17},{... | collective-permute-start | bytes 1572872 | tf_op jit(solution)/shard_map/ppermute | solution.py:20
  102.0 23.0 %collective-permute-start.25 = (f32[1024,128]{1,0:T(8,128)S(1)}, f32[1024,128]{1,0:T(8,128)S(1)}, u32[]{:S(2)}, u32[]{:S(2)}) collective-permute-start(f32[1024,128]{1,0:T(8,128)S(1)} %get-tuple-element.52.refs_0_), channel_id=1, source_target_pairs={{0,1},{1,0},{2,3},{3,2},{4,5},{5,4},{6,7},{7,6},{8,9},{9,8},{10,11... | collective-permute-start | bytes 1572872 | tf_op jit(solution)/shard_map/ppermute | solution.py:20
  112.0 13.0 %collective-permute-start.27 = (f32[1024,128]{1,0:T(8,128)S(1)}, f32[1024,128]{1,0:T(8,128)S(1)}, u32[]{:S(2)}, u32[]{:S(2)}) collective-permute-start(f32[1024,128]{1,0:T(8,128)S(1)} %collective-permute-done.26.refs_2_), channel_id=1, source_target_pairs={{0,1},{1,0},{2,3},{3,2},{4,5},{5,4},{6,7},{7,6},{8,9},{9,8},{10,11... | collective-permute-start | bytes 1572872 | tf_op jit(solution)/shard_map/ppermute | solution.py:20
  125.0 13.5 %collective-permute-start.31 = (f32[512,128]{1,0:T(8,128)S(1)}, f32[512,128]{1,0:T(8,128)S(1)}, u32[]{:S(2)}, u32[]{:S(2)}) collective-permute-start(f32[512,128]{1,0:T(8,128)S(1)} %shard_map.94), channel_id=1, source_target_pairs={{0,16},{4,20},{8,24},{12,28},{16,0},{20,4},{24,8},{28,12},{1,17},{... | collective-permute-start | bytes 786440 | tf_op jit(solution)/shard_map/ppermute | solution.py:20
  126.3 12.1 %collective-permute-start.30 = (f32[512,128]{1,0:T(8,128)S(1)}, f32[512,128]{1,0:T(8,128)S(1)}, u32[]{:S(2)}, u32[]{:S(2)}) collective-permute-start(f32[512,128]{1,0:T(8,128)S(1)} %shard_map.95.refs_6_.refs_0_), channel_id=1, source_target_pairs={{0,2},{1,3},{2,0},{3,1},{4,6},{5,7},{6,4},{7,5},{8,10},{9,11},{10,... | collective-permute-start | bytes 786440 | tf_op jit(solution)/shard_map/ppermute | solution.py:20
  127.3 12.5 %collective-permute-start.29 = (f32[512,128]{1,0:T(8,128)S(1)}, f32[512,128]{1,0:T(8,128)S(1)}, u32[]{:S(2)}, u32[]{:S(2)}) collective-permute-start(f32[512,128]{1,0:T(8,128)S(1)} %shard_map.95.refs_6_.refs_0_), channel_id=1, source_target_pairs={{0,1},{1,0},{2,3},{3,2},{4,5},{5,4},{6,7},{7,6},{8,9},{9,8},{10,11... | collective-permute-start | bytes 786440 | tf_op jit(solution)/shard_map/ppermute | solution.py:20
  (11 other events, 21.3 us)

commit v4 on v3

--- a/solution.py
+++ b/solution.py
@@ -314,8 +314,7 @@
 
     n_far = across(diag)
     slots = placed_entries(extra, owners, rows_in, counts)
-    both = couplings(place, lower_part[0], upper_part[0], [slots])
-    n_far, both = tied(n_far, both)
+    both = couplings(place, lower_part[0], upper_part[0], [slots, *n_far.values()])
     n_shards = gathered(diag, n_far)
 
     partner = lambda source: source ^ 1
@@ -353,10 +352,9 @@
         if closing(level, stride):
             (pair,) = pieces
             got = send(pair, "blk", ahead)
-            both_far[half], late = tied(both_far[half], pair)
+            solved = one_column(place, n_shards, right, after=[pair])
+            both_far[half], got, solved = tied(both_far[half], got, solved)
             both_shards = gathered(both, both_far)
-            solved = one_column(place, n_shards, right, after=[late])
-            solved, got = tied(solved, got)
             low_y = send(solved, "blk", ahead)
             diag = reduced(place, both_shards, diag, got, got)
             n_far = across(diag)

time: 144 us -> 144 us (level)
  no operation moved by 1% of the time
where the time goes in v4:
time: 144 us; the launch traced here: 143 us
  waiting for transfers between devices  74.7 us (52%)
  starting transfers between devices  34.9 us (24%)
  Pallas kernels  28.3 us (20%)
  local copies, waits for them, and re-layouts  4.23 us (3%)
    ppermute x33, waiting for transfers between devices, send(): return lax.ppermute(value, axis, pairs)  74.7 us
    ppermute x33, starting transfers between devices, send(): return lax.ppermute(value, axis, pairs)  29 us
    pallas_call x14, Pallas kernels, kernel_call(): pl.pallas_call(kernel, out_shape=[jax.ShapeDtypeStruct((rows, width), f32...  26.1 us
    all_to_all x1, starting transfers between devices, on_device(): lax.all_to_all(slots.reshape(cycle_size, -1, slots.shape[1]), 'blk', spli...  5.96 us
    unnamed x18, local copies, waits for them, and re-layouts  4.23 us
  transfers between devices with their start and end apart: 34, of which 19 were waited for; matrix products, arithmetic and copies ran while one was open for 0% of the time, Pallas kernels for 16%

profile of v4, /device:TPU:0, one launch (start us, length us, event | category | flops | bytes accessed | tf_op | source)
XLA Modules:
  0.0 143.1 jit_solution(11082983249005453833)
XLA Ops:
  0.0 2.9 %collective-permute-start = (f32[512,128]{1,0:T(8,128)}, f32[512,128]{1,0:T(8,128)S(1)}, u32[]{:S(2)}, u32[]{:S(2)}) collective-permute-start(f32[512,128]{1,0:T(8,128)} %bitcast.12), channel_id=1, source_target_pairs={{0,2},{1,3},{2,0},{3,1},{4,6},{5,7},{6,4},{7,5},{8,10},{9,11},{10,... | collective-permute-start | bytes 786440 | tf_op jit(solution)/shard_map/ppermute | solution.py:20
  5.2 1.5 %shard_map.82.refs_2_ = f32[1088,128]{1,0:T(8,128)} custom-call(s32[1]{0:T(128)S(6)} %copy.9.counts, s32[1,512]{1,0:T(1,128)S(1)} %bitcast.20, s32[1,512]{1,0:T(1,128)S(1)} %bitcast.21, f32[512,128]{1,0:T(8,128)S(1)} %copy-done.1), custom_call_target="tpu_custom_call" | custom-call | flops 1 | bytes 1 | tf_op jit(solution)/shard_map/pallas_call | solution.py:266
  6.7 6.0 %all-to-all-start = ((f32[8,136,128]{2,1,0:T(8,128)}), f32[8,136,128]{2,1,0:T(8,128)S(1)}, u32[]{:S(2)}, u32[]{:S(2)}) async-start(f32[8,136,128]{2,1,0:T(8,128)} %bitcast.7), calls=%async_computation | async-start | bytes 1114112 | tf_op jit(solution)/shard_map/all_to_all | solution.py:322
  15.9 2.9 %shard_map.84 = (f32[512,128]{1,0:T(8,128)S(1)}, f32[512,128]{1,0:T(8,128)}) custom-call(s32[2]{0:T(128)S(1)} %pad_add_fusion.place_ref, f32[512,128]{1,0:T(8,128)S(1)} %bitcast.14, f32[512,128]{1,0:T(8,128)S(1)} %collective-permute-done.4.refs_1_, f32[512,128]{1,0:T(8,128)S(1)} %collective-permute-done.refs_3_.refs_2_, ...), custom_call_target="tpu_custom_call" | custom-call | flops 1 | bytes 1 | tf_op jit(solution)/shard_map/pallas_call | solution.py:95
  18.9 2.0 %collective-permute-start.6 = (f32[512,128]{1,0:T(8,128)S(1)}, f32[512,128]{1,0:T(8,128)S(1)}, u32[]{:S(2)}, u32[]{:S(2)}) collective-permute-start(f32[512,128]{1,0:T(8,128)S(1)} %get-tuple-element.30._), channel_id=1, source_target_pairs={{0,4},{4,0},{8,12},{12,8},{16,20},{20,16},{24,28},{28,24},{1,5},{5... | collective-permute-start | bytes 786440 | tf_op jit(solution)/shard_map/ppermute | solution.py:20
  21.6 5.0 %collective-permute-done.2.refs_2_ = f32[1024,128]{1,0:T(8,128)S(1)} collective-permute-done((f32[1024,128]{1,0:T(8,128)S(1)}, f32[1024,128]{1,0:T(8,128)S(1)}, u32[]{:S(2)}, u32[]{:S(2)}) %collective-permute-start.2) | collective-permute-done | bytes 524320 | tf_op jit(solution)/shard_map/ppermute | solution.py:20
  26.6 1.7 %collective-permute-start.8 = (f32[512,128]{1,0:T(8,128)}, f32[512,128]{1,0:T(8,128)}, u32[]{:S(2)}, u32[]{:S(2)}) collective-permute-start(f32[512,128]{1,0:T(8,128)} %get-tuple-element.32), channel_id=1, source_target_pairs={{0,4},{4,0},{8,12},{12,8},{16,20},{20,16},{24,28},{28,24},{1,5},{5... | collective-permute-start | bytes 786440 | tf_op jit(solution)/shard_map/ppermute | solution.py:20
  28.9 1.9 %collective-permute-start.7 = (f32[512,128]{1,0:T(8,128)S(1)}, f32[512,128]{1,0:T(8,128)S(1)}, u32[]{:S(2)}, u32[]{:S(2)}) collective-permute-start(f32[512,128]{1,0:T(8,128)S(1)} %collective-permute-done.6.refs_5_), channel_id=1, source_target_pairs={{0,8},{4,28},{8,16},{12,4},{16,24},{20,12},{24,0},{28,20},{1,9},{5... | collective-permute-start | bytes 786440 | tf_op jit(solution)/shard_map/ppermute | solution.py:20
  33.4 1.7 %shard_map.86 = f32[512,128]{1,0:T(8,128)S(1)} custom-call(s32[2]{0:T(128)S(1)} %pad_add_fusion.place_ref, f32[512,128]{1,0:T(8,128)S(1)} %bitcast.15, f32[512,128]{1,0:T(8,128)S(1)} %collective-permute-done.4.refs_1_, f32[512,128]{1,0:T(8,128)S(1)} %collective-permute-done.refs_3_.refs_2_, f32[512,128]{1,0:T(8,128)S(1)} %collective-permute-done.5.refs_3_, ...), custom_call_target="tpu_custom_call" | custom-call | flops 1 | bytes 1 | tf_op jit(solution)/shard_map/pallas_call | solution.py:95
  35.6 1.7 %collective-permute-start.10 = (f32[512,128]{1,0:T(8,128)}, f32[512,128]{1,0:T(8,128)S(1)}, u32[]{:S(2)}, u32[]{:S(2)}) collective-permute-start(f32[512,128]{1,0:T(8,128)} %collective-permute-done.8.refs_6_), channel_id=1, source_target_pairs={{0,8},{4,28},{8,16},{12,4},{16,24},{20,12},{24,0},{28,20},{1,9},{5... | collective-permute-start | bytes 786440 | tf_op jit(solution)/shard_map/ppermute | solution.py:20
  38.7 1.8 %shard_map.87.refs_6_.refs_0_.refs_4_ = f32[512,128]{1,0:T(8,128)S(1)} custom-call(s32[2]{0:T(128)S(1)} %pad_add_fusion.place_ref, f32[1024,128]{1,0:T(8,128)S(1)} %shard_map.83.refs_4_.refs_0_, f32[1024,128]{1,0:T(8,128)S(1)} %collective-permute-done.1.refs_1_, f32[1024,128]{1,0:T(8,128)S(1)} %collective-permute-done.2.refs_2_, ...), custom_call_target="tpu_custom_call" | custom-call | flops 23000000512 | bytes 73800000 | tf_op jit(solution)/shard_map/pallas_call | solution.py:95
  43.1 2.5 %collective-permute-done.10.refs_4_ = f32[512,128]{1,0:T(8,128)S(1)} collective-permute-done((f32[512,128]{1,0:T(8,128)}, f32[512,128]{1,0:T(8,128)S(1)}, u32[]{:S(2)}, u32[]{:S(2)}) %collective-permute-start.10) | collective-permute-done | bytes 262176 | tf_op jit(solution)/shard_map/ppermute | solution.py:20
  45.6 1.8 %shard_map.88.refs_4_.refs_0_ = f32[1024,128]{1,0:T(8,128)S(1)} custom-call(s32[2]{0:T(128)S(1)} %pad_add_fusion.place_ref, f32[1024,128]{1,0:T(8,128)S(1)} %shard_map.83.refs_4_.refs_0_, f32[1024,128]{1,0:T(8,128)S(1)} %collective-permute-done.1.refs_1_, f32[1024,128]{1,0:T(8,128)S(1)} %collective-permute-done.2.refs_2_, ...), custom_call_target="tpu_custom_call" | custom-call | flops 1 | bytes 1 | tf_op jit(solution)/shard_map/pallas_call | solution.py:95
  50.2 2.3 %shard_map.89 = (f32[512,128]{1,0:T(8,128)S(1)}, f32[512,128]{1,0:T(8,128)S(1)}) custom-call(s32[2]{0:T(128)S(1)} %pad_add_fusion.place_ref, f32[512,128]{1,0:T(8,128)S(1)} %shard_map.87.refs_6_.refs_0_.refs_4_, f32[512,128]{1,0:T(8,128)S(1)} %collective-permute-done.13.refs_1_, f32[512,128]{1,0:T(8,128)S(1)} %collective-permute-done.9.refs_2_, ...), custom_call_target="tpu_custom_call" | custom-call | flops 1 | bytes 1 | tf_op jit(solution)/shard_map/pallas_call | solution.py:95
  52.5 1.5 %collective-permute-start.15 = (f32[512,128]{1,0:T(8,128)S(1)}, f32[512,128]{1,0:T(8,128)S(1)}, u32[]{:S(2)}, u32[]{:S(2)}) collective-permute-start(f32[512,128]{1,0:T(8,128)S(1)} %get-tuple-element.37.refs_6_), channel_id=1, source_target_pairs={{0,8},{4,12},{8,16},{12,20},{16,24},{20,28},{24,0},{28,4},{1,9},{5... | collective-permute-start | bytes 786440 | tf_op jit(solution)/shard_map/ppermute | solution.py:20
  54.0 2.5 %collective-permute-start.16 = (f32[512,128]{1,0:T(8,128)S(1)}, f32[512,128]{1,0:T(8,128)S(1)}, u32[]{:S(2)}, u32[]{:S(2)}) collective-permute-start(f32[512,128]{1,0:T(8,128)S(1)} %get-tuple-element.38.refs_5_), channel_id=1, source_target_pairs={{0,24},{4,28},{8,0},{12,4},{16,8},{20,12},{24,16},{28,20},{1,25},{... | collective-permute-start | bytes 786440 | tf_op jit(solution)/shard_map/ppermute | solution.py:20
  56.5 3.4 %collective-permute-done.18.refs_5_ = f32[512,128]{1,0:T(8,128)S(1)} collective-permute-done((f32[512,128]{1,0:T(8,128)S(1)}, f32[512,128]{1,0:T(8,128)S(1)}, u32[]{:S(2)}, u32[]{:S(2)}) %collective-permute-start.18) | collective-permute-done | bytes 262176 | tf_op jit(solution)/shard_map/ppermute | solution.py:20
  59.9 1.8 %shard_map.90.refs_4_.refs_8_ = f32[512,128]{1,0:T(8,128)S(1)} custom-call(s32[2]{0:T(128)S(1)} %pad_add_fusion.place_ref, f32[1024,128]{1,0:T(8,128)S(1)} %shard_map.83.refs_4_.refs_0_, f32[1024,128]{1,0:T(8,128)S(1)} %collective-permute-done.1.refs_1_, f32[1024,128]{1,0:T(8,128)S(1)} %collective-permute-done.2.refs_2_, ...), custom_call_target="tpu_custom_call" | custom-call | flops 23000000512 | bytes 73800000 | tf_op jit(solution)/shard_map/pallas_call | solution.py:95
  61.8 1.7 %shard_map.91 = (f32[1024,128]{1,0:T(8,128)S(1)}, f32[1024,128]{1,0:T(8,128)S(1)}) custom-call(s32[2]{0:T(128)S(1)} %pad_add_fusion.place_ref, f32[512,128]{1,0:T(8,128)S(1)} %shard_map.87.refs_6_.refs_0_.refs_4_, f32[512,128]{1,0:T(8,128)S(1)} %collective-permute-done.13.refs_1_, f32[512,128]{1,0:T(8,128)S(1)} %collective-permute-done.9.refs_2_, ...), custom_call_target="tpu_custom_call" | custom-call | flops 1 | bytes 1 | tf_op jit(solution)/shard_map/pallas_call | solution.py:95
  63.5 1.9 %collective-permute-done.15.refs_5_ = f32[512,128]{1,0:T(8,128)S(1)} collective-permute-done((f32[512,128]{1,0:T(8,128)S(1)}, f32[512,128]{1,0:T(8,128)S(1)}, u32[]{:S(2)}, u32[]{:S(2)}) %collective-permute-start.15) | collective-permute-done | bytes 262176 | tf_op jit(solution)/shard_map/ppermute | solution.py:20
  65.4 4.1 %collective-permute-done.16.refs_6_ = f32[512,128]{1,0:T(8,128)S(1)} collective-permute-done((f32[512,128]{1,0:T(8,128)S(1)}, f32[512,128]{1,0:T(8,128)S(1)}, u32[]{:S(2)}, u32[]{:S(2)}) %collective-permute-start.16) | collective-permute-done | bytes 262176 | tf_op jit(solution)/shard_map/ppermute | solution.py:20
  70.1 3.2 %collective-permute-start.24 = (f32[1024,128]{1,0:T(8,128)S(1)}, f32[1024,128]{1,0:T(8,128)S(1)}, u32[]{:S(2)}, u32[]{:S(2)}) collective-permute-start(f32[1024,128]{1,0:T(8,128)S(1)} %get-tuple-element.46), channel_id=1, source_target_pairs={{0,24},{4,28},{8,0},{12,4},{16,8},{20,12},{24,16},{28,20},{1,25},{... | collective-permute-start | bytes 1572872 | tf_op jit(solution)/shard_map/ppermute | solution.py:20
  75.8 7.1 %collective-permute-done.21.refs_6_.refs_2_ = f32[512,128]{1,0:T(8,128)S(1)} collective-permute-done((f32[512,128]{1,0:T(8,128)S(1)}, f32[512,128]{1,0:T(8,128)S(1)}, u32[]{:S(2)}, u32[]{:S(2)}) %collective-permute-start.21) | collective-permute-done | bytes 262176 | tf_op jit(solution)/shard_map/ppermute | solution.py:20
  82.9 3.2 %collective-permute-done.23.refs_9_ = f32[1024,128]{1,0:T(8,128)S(1)} collective-permute-done((f32[1024,128]{1,0:T(8,128)S(1)}, f32[1024,128]{1,0:T(8,128)S(1)}, u32[]{:S(2)}, u32[]{:S(2)}) %collective-permute-start.23) | collective-permute-done | bytes 524320 | tf_op jit(solution)/shard_map/ppermute | solution.py:20
  86.1 9.3 %collective-permute-done.24.refs_10_ = f32[1024,128]{1,0:T(8,128)S(1)} collective-permute-done((f32[1024,128]{1,0:T(8,128)S(1)}, f32[1024,128]{1,0:T(8,128)S(1)}, u32[]{:S(2)}, u32[]{:S(2)}) %collective-permute-start.24) | collective-permute-done | bytes 524320 | tf_op jit(solution)/shard_map/ppermute | solution.py:20
  95.4 3.3 %shard_map.93 = (f32[1024,128]{1,0:T(8,128)S(1)}, f32[512,128]{1,0:T(8,128)S(1)}, f32[1024,128]{1,0:T(8,128)S(1)}) custom-call(s32[2]{0:T(128)S(1)} %pad_add_fusion.place_ref, f32[1024,128]{1,0:T(8,128)S(1)} %shard_map.88.refs_4_.refs_0_, f32[1024,128]{1,0:T(8,128)S(1)} %collective-permute-done.11.refs_1_, f32[1024,128]{1,0:T(8,128)S(1)} %collective-permute-done.12.refs_2_, ...), custom_call_target="tpu_custom_call" | custom-call | flops 1 | bytes 1 | tf_op jit(solution)/shard_map/pallas_call | solution.py:95
  98.7 2.2 %collective-permute-start.27 = (f32[1024,128]{1,0:T(8,128)S(1)}, f32[1024,128]{1,0:T(8,128)S(1)}, u32[]{:S(2)}, u32[]{:S(2)}) collective-permute-start(f32[1024,128]{1,0:T(8,128)S(1)} %get-tuple-element.48.refs_5_), channel_id=1, source_target_pairs={{0,16},{4,20},{8,24},{12,28},{16,0},{20,4},{24,8},{28,12},{1,17},{... | collective-permute-start | bytes 1572872 | tf_op jit(solution)/shard_map/ppermute | solution.py:20
  102.0 1.7 %shard_map.94 = f32[512,128]{1,0:T(8,128)S(1)} custom-call(s32[2]{0:T(128)S(1)} %pad_add_fusion.place_ref, f32[512,128]{1,0:T(8,128)S(1)} %shard_map.92.refs_4_.refs_0_, f32[512,128]{1,0:T(8,128)S(1)} %collective-permute-done.20.refs_5_.refs_1_, f32[512,128]{1,0:T(8,128)S(1)} %collective-permute-done.21.refs_6_.refs_2_, ...), custom_call_target="tpu_custom_call" | custom-call | flops 1 | bytes 1 | tf_op jit(solution)/shard_map/pallas_call | solution.py:95
  103.7 20.4 %collective-permute-done.27.refs_5_ = f32[1024,128]{1,0:T(8,128)S(1)} collective-permute-done((f32[1024,128]{1,0:T(8,128)S(1)}, f32[1024,128]{1,0:T(8,128)S(1)}, u32[]{:S(2)}, u32[]{:S(2)}) %collective-permute-start.27) | collective-permute-done | bytes 524320 | tf_op jit(solution)/shard_map/ppermute | solution.py:20
  124.2 1.9 %collective-permute-done.28.refs_3_ = f32[1024,128]{1,0:T(8,128)S(1)} collective-permute-done((f32[1024,128]{1,0:T(8,128)S(1)}, f32[1024,128]{1,0:T(8,128)S(1)}, u32[]{:S(2)}, u32[]{:S(2)}) %collective-permute-start.28) | collective-permute-done | bytes 524320 | tf_op jit(solution)/shard_map/ppermute | solution.py:20
  128.5 10.6 %collective-permute-done.31.refs_5_ = f32[512,128]{1,0:T(8,128)S(1)} collective-permute-done((f32[512,128]{1,0:T(8,128)S(1)}, f32[512,128]{1,0:T(8,128)S(1)}, u32[]{:S(2)}, u32[]{:S(2)}) %collective-permute-start.31) | collective-permute-done | bytes 262176 | tf_op jit(solution)/shard_map/ppermute | solution.py:20
  140.7 2.4 %shard_map.97 = f32[512,128]{1,0:T(8,128)} custom-call(s32[2]{0:T(128)S(1)} %pad_add_fusion.place_ref, f32[512,128]{1,0:T(8,128)S(1)} %shard_map.95.refs_6_.refs_0_, f32[512,128]{1,0:T(8,128)S(1)} %collective-permute-done.29.refs_1_, f32[512,128]{1,0:T(8,128)S(1)} %collective-permute-done.30.refs_2_, f32[512,128]{1,0:T(8,128)S(1)} %collective-permute-done.32.refs_3_, ...), custom_call_target="tpu_custom_call" | custom-call | flops 1 | bytes 1 | tf_op jit(solution)/shard_map/pallas_call | solution.py:95
  (71 shorter events, 24.2 us)
Async XLA Ops:
  0.0 12.8 %collective-permute-start = (f32[512,128]{1,0:T(8,128)}, f32[512,128]{1,0:T(8,128)S(1)}, u32[]{:S(2)}, u32[]{:S(2)}) collective-permute-start(f32[512,128]{1,0:T(8,128)} %bitcast.12), channel_id=1, source_target_pairs={{0,2},{1,3},{2,0},{3,1},{4,6},{5,7},{6,4},{7,5},{8,10},{9,11},{10,... | collective-permute-start | bytes 786440 | tf_op jit(solution)/shard_map/ppermute | solution.py:20
  6.7 22.2 %all-to-all-start = ((f32[8,136,128]{2,1,0:T(8,128)}), f32[8,136,128]{2,1,0:T(8,128)S(1)}, u32[]{:S(2)}, u32[]{:S(2)}) async-start(f32[8,136,128]{2,1,0:T(8,128)} %bitcast.7), calls=%async_computation | async-start | bytes 1114112 | tf_op jit(solution)/shard_map/all_to_all | solution.py:322
  13.4 13.2 %collective-permute-start.2 = (f32[1024,128]{1,0:T(8,128)S(1)}, f32[1024,128]{1,0:T(8,128)S(1)}, u32[]{:S(2)}, u32[]{:S(2)}) collective-permute-start(f32[1024,128]{1,0:T(8,128)S(1)} %shard_map.83.refs_4_.refs_0_), channel_id=1, source_target_pairs={{0,2},{1,3},{2,0},{3,1},{4,6},{5,7},{6,4},{7,5},{8,10},{9,11},{10,... | collective-permute-start | bytes 1572872 | tf_op jit(solution)/shard_map/ppermute | solution.py:20
  14.0 1.9 %collective-permute-start.5 = (f32[512,128]{1,0:T(8,128)S(1)}, f32[512,128]{1,0:T(8,128)S(1)}, u32[]{:S(2)}, u32[]{:S(2)}) collective-permute-start(f32[512,128]{1,0:T(8,128)S(1)} %collective-permute-done.refs_3_.refs_2_), channel_id=1, source_target_pairs={{0,1},{1,0},{2,3},{3,2},{4,5},{5,4},{6,7},{7,6},{8,9},{9,8},{10,11... | collective-permute-start | bytes 786440 | tf_op jit(solution)/shard_map/ppermute | solution.py:20
  18.9 10.0 %collective-permute-start.6 = (f32[512,128]{1,0:T(8,128)S(1)}, f32[512,128]{1,0:T(8,128)S(1)}, u32[]{:S(2)}, u32[]{:S(2)}) collective-permute-start(f32[512,128]{1,0:T(8,128)S(1)} %get-tuple-element.30._), channel_id=1, source_target_pairs={{0,4},{4,0},{8,12},{12,8},{16,20},{20,16},{24,28},{28,24},{1,5},{5... | collective-permute-start | bytes 786440 | tf_op jit(solution)/shard_map/ppermute | solution.py:20
  21.6 15.8 %collective-permute-start.1 = (f32[1024,128]{1,0:T(8,128)S(1)}, f32[1024,128]{1,0:T(8,128)S(1)}, u32[]{:S(2)}, u32[]{:S(2)}) collective-permute-start(f32[1024,128]{1,0:T(8,128)S(1)} %shard_map.83.refs_4_.refs_0_), channel_id=1, source_target_pairs={{0,1},{1,0},{2,3},{3,2},{4,5},{5,4},{6,7},{7,6},{8,9},{9,8},{10,11... | collective-permute-start | bytes 1572872 | tf_op jit(solution)/shard_map/ppermute | solution.py:20
  26.6 12.1 %collective-permute-start.3 = (f32[1024,128]{1,0:T(8,128)S(1)}, f32[1024,128]{1,0:T(8,128)}, u32[]{:S(2)}, u32[]{:S(2)}) collective-permute-start(f32[1024,128]{1,0:T(8,128)S(1)} %collective-permute-done.2.refs_2_), channel_id=1, source_target_pairs={{0,1},{1,0},{2,3},{3,2},{4,5},{5,4},{6,7},{7,6},{8,9},{9,8},{10,11... | collective-permute-start | bytes 1572872 | tf_op jit(solution)/shard_map/ppermute | solution.py:20
  26.6 9.0 %collective-permute-start.8 = (f32[512,128]{1,0:T(8,128)}, f32[512,128]{1,0:T(8,128)}, u32[]{:S(2)}, u32[]{:S(2)}) collective-permute-start(f32[512,128]{1,0:T(8,128)} %get-tuple-element.32), channel_id=1, source_target_pairs={{0,4},{4,0},{8,12},{12,8},{16,20},{20,16},{24,28},{28,24},{1,5},{5... | collective-permute-start | bytes 786440 | tf_op jit(solution)/shard_map/ppermute | solution.py:20
  28.9 9.8 %collective-permute-start.7 = (f32[512,128]{1,0:T(8,128)S(1)}, f32[512,128]{1,0:T(8,128)S(1)}, u32[]{:S(2)}, u32[]{:S(2)}) collective-permute-start(f32[512,128]{1,0:T(8,128)S(1)} %collective-permute-done.6.refs_5_), channel_id=1, source_target_pairs={{0,8},{4,28},{8,16},{12,4},{16,24},{20,12},{24,0},{28,20},{1,9},{5... | collective-permute-start | bytes 786440 | tf_op jit(solution)/shard_map/ppermute | solution.py:20
  35.6 9.9 %collective-permute-start.10 = (f32[512,128]{1,0:T(8,128)}, f32[512,128]{1,0:T(8,128)S(1)}, u32[]{:S(2)}, u32[]{:S(2)}) collective-permute-start(f32[512,128]{1,0:T(8,128)} %collective-permute-done.8.refs_6_), channel_id=1, source_target_pairs={{0,8},{4,28},{8,16},{12,4},{16,24},{20,12},{24,0},{28,20},{1,9},{5... | collective-permute-start | bytes 786440 | tf_op jit(solution)/shard_map/ppermute | solution.py:20
  40.6 7.2 %collective-permute-start.9 = (f32[512,128]{1,0:T(8,128)S(1)}, f32[512,128]{1,0:T(8,128)S(1)}, u32[]{:S(2)}, u32[]{:S(2)}) collective-permute-start(f32[512,128]{1,0:T(8,128)S(1)} %shard_map.87.refs_6_.refs_0_.refs_4_), channel_id=1, source_target_pairs={{0,2},{1,3},{2,0},{3,1},{4,6},{5,7},{6,4},{7,5},{8,10},{9,11},{10,... | collective-permute-start | bytes 786440 | tf_op jit(solution)/shard_map/ppermute | solution.py:20
  41.7 7.0 %collective-permute-start.17 = (f32[512,128]{1,0:T(8,128)S(1)}, f32[512,128]{1,0:T(8,128)S(1)}, u32[]{:S(2)}, u32[]{:S(2)}) collective-permute-start(f32[512,128]{1,0:T(8,128)S(1)} %shard_map.86), channel_id=1, source_target_pairs={{0,4},{4,0},{8,12},{12,8},{16,20},{20,16},{24,28},{28,24},{1,5},{5... | collective-permute-start | bytes 786440 | tf_op jit(solution)/shard_map/ppermute | solution.py:20
  43.1 7.1 %collective-permute-start.13 = (f32[512,128]{1,0:T(8,128)S(1)}, f32[512,128]{1,0:T(8,128)S(1)}, u32[]{:S(2)}, u32[]{:S(2)}) collective-permute-start(f32[512,128]{1,0:T(8,128)S(1)} %shard_map.87.refs_6_.refs_0_.refs_4_), channel_id=1, source_target_pairs={{0,1},{1,0},{2,3},{3,2},{4,5},{5,4},{6,7},{7,6},{8,9},{9,8},{10,11... | collective-permute-start | bytes 786440 | tf_op jit(solution)/shard_map/ppermute | solution.py:20
  47.7 2.5 %collective-permute-start.14 = (f32[512,128]{1,0:T(8,128)S(1)}, f32[512,128]{1,0:T(8,128)S(1)}, u32[]{:S(2)}, u32[]{:S(2)}) collective-permute-start(f32[512,128]{1,0:T(8,128)S(1)} %collective-permute-done.9.refs_2_), channel_id=1, source_target_pairs={{0,1},{1,0},{2,3},{3,2},{4,5},{5,4},{6,7},{7,6},{8,9},{9,8},{10,11... | collective-permute-start | bytes 786440 | tf_op jit(solution)/shard_map/ppermute | solution.py:20
  48.7 11.2 %collective-permute-start.18 = (f32[512,128]{1,0:T(8,128)S(1)}, f32[512,128]{1,0:T(8,128)S(1)}, u32[]{:S(2)}, u32[]{:S(2)}) collective-permute-start(f32[512,128]{1,0:T(8,128)S(1)} %collective-permute-done.17.refs_6_), channel_id=1, source_target_pairs={{0,8},{4,28},{8,16},{12,4},{16,24},{20,12},{24,0},{28,20},{1,9},{5... | collective-permute-start | bytes 786440 | tf_op jit(solution)/shard_map/ppermute | solution.py:20
  48.8 20.7 %collective-permute-start.12 = (f32[1024,128]{1,0:T(8,128)S(1)}, f32[1024,128]{1,0:T(8,128)S(1)}, u32[]{:S(2)}, u32[]{:S(2)}) collective-permute-start(f32[1024,128]{1,0:T(8,128)S(1)} %shard_map.88.refs_4_.refs_0_), channel_id=1, source_target_pairs={{0,2},{1,3},{2,0},{3,1},{4,6},{5,7},{6,4},{7,5},{8,10},{9,11},{10,... | collective-permute-start | bytes 1572872 | tf_op jit(solution)/shard_map/ppermute | solution.py:20
  52.5 12.9 %collective-permute-start.15 = (f32[512,128]{1,0:T(8,128)S(1)}, f32[512,128]{1,0:T(8,128)S(1)}, u32[]{:S(2)}, u32[]{:S(2)}) collective-permute-start(f32[512,128]{1,0:T(8,128)S(1)} %get-tuple-element.37.refs_6_), channel_id=1, source_target_pairs={{0,8},{4,12},{8,16},{12,20},{16,24},{20,28},{24,0},{28,4},{1,9},{5... | collective-permute-start | bytes 786440 | tf_op jit(solution)/shard_map/ppermute | solution.py:20
  54.0 15.5 %collective-permute-start.16 = (f32[512,128]{1,0:T(8,128)S(1)}, f32[512,128]{1,0:T(8,128)S(1)}, u32[]{:S(2)}, u32[]{:S(2)}) collective-permute-start(f32[512,128]{1,0:T(8,128)S(1)} %get-tuple-element.38.refs_5_), channel_id=1, source_target_pairs={{0,24},{4,28},{8,0},{12,4},{16,8},{20,12},{24,16},{28,20},{1,25},{... | collective-permute-start | bytes 786440 | tf_op jit(solution)/shard_map/ppermute | solution.py:20
  61.7 11.6 %collective-permute-start.11 = (f32[1024,128]{1,0:T(8,128)S(1)}, f32[1024,128]{1,0:T(8,128)S(1)}, u32[]{:S(2)}, u32[]{:S(2)}) collective-permute-start(f32[1024,128]{1,0:T(8,128)S(1)} %shard_map.88.refs_4_.refs_0_), channel_id=1, source_target_pairs={{0,1},{1,0},{2,3},{3,2},{4,5},{5,4},{6,7},{7,6},{8,9},{9,8},{10,11... | collective-permute-start | bytes 1572872 | tf_op jit(solution)/shard_map/ppermute | solution.py:20
  69.5 3.8 %collective-permute-start.19 = (f32[1024,128]{1,0:T(8,128)S(1)}, f32[1024,128]{1,0:T(8,128)S(1)}, u32[]{:S(2)}, u32[]{:S(2)}) collective-permute-start(f32[1024,128]{1,0:T(8,128)S(1)} %collective-permute-done.12.refs_2_), channel_id=1, source_target_pairs={{0,1},{1,0},{2,3},{3,2},{4,5},{5,4},{6,7},{7,6},{8,9},{9,8},{10,11... | collective-permute-start | bytes 1572872 | tf_op jit(solution)/shard_map/ppermute | solution.py:20
  69.5 16.6 %collective-permute-start.23 = (f32[1024,128]{1,0:T(8,128)S(1)}, f32[1024,128]{1,0:T(8,128)S(1)}, u32[]{:S(2)}, u32[]{:S(2)}) collective-permute-start(f32[1024,128]{1,0:T(8,128)S(1)} %get-tuple-element.45), channel_id=1, source_target_pairs={{0,8},{4,12},{8,16},{12,20},{16,24},{20,28},{24,0},{28,4},{1,9},{5... | collective-permute-start | bytes 1572872 | tf_op jit(solution)/shard_map/ppermute | solution.py:20
  70.1 25.3 %collective-permute-start.24 = (f32[1024,128]{1,0:T(8,128)S(1)}, f32[1024,128]{1,0:T(8,128)S(1)}, u32[]{:S(2)}, u32[]{:S(2)}) collective-permute-start(f32[1024,128]{1,0:T(8,128)S(1)} %get-tuple-element.46), channel_id=1, source_target_pairs={{0,24},{4,28},{8,0},{12,4},{16,8},{20,12},{24,16},{28,20},{1,25},{... | collective-permute-start | bytes 1572872 | tf_op jit(solution)/shard_map/ppermute | solution.py:20
  74.7 8.2 %collective-permute-start.21 = (f32[512,128]{1,0:T(8,128)S(1)}, f32[512,128]{1,0:T(8,128)S(1)}, u32[]{:S(2)}, u32[]{:S(2)}) collective-permute-start(f32[512,128]{1,0:T(8,128)S(1)} %shard_map.92.refs_4_.refs_0_), channel_id=1, source_target_pairs={{0,2},{1,3},{2,0},{3,1},{4,6},{5,7},{6,4},{7,5},{8,10},{9,11},{10,... | collective-permute-start | bytes 786440 | tf_op jit(solution)/shard_map/ppermute | solution.py:20
  75.8 19.5 %collective-permute-start.20 = (f32[512,128]{1,0:T(8,128)S(1)}, f32[512,128]{1,0:T(8,128)S(1)}, u32[]{:S(2)}, u32[]{:S(2)}) collective-permute-start(f32[512,128]{1,0:T(8,128)S(1)} %shard_map.92.refs_4_.refs_0_), channel_id=1, source_target_pairs={{0,1},{1,0},{2,3},{3,2},{4,5},{5,4},{6,7},{7,6},{8,9},{9,8},{10,11... | collective-permute-start | bytes 786440 | tf_op jit(solution)/shard_map/ppermute | solution.py:20
  82.9 12.5 %collective-permute-start.22 = (f32[512,128]{1,0:T(8,128)S(1)}, f32[512,128]{1,0:T(8,128)S(1)}, u32[]{:S(2)}, u32[]{:S(2)}) collective-permute-start(f32[512,128]{1,0:T(8,128)S(1)} %collective-permute-done.21.refs_6_.refs_2_), channel_id=1, source_target_pairs={{0,1},{1,0},{2,3},{3,2},{4,5},{5,4},{6,7},{7,6},{8,9},{9,8},{10,11... | collective-permute-start | bytes 786440 | tf_op jit(solution)/shard_map/ppermute | solution.py:20
  98.7 25.4 %collective-permute-start.27 = (f32[1024,128]{1,0:T(8,128)S(1)}, f32[1024,128]{1,0:T(8,128)S(1)}, u32[]{:S(2)}, u32[]{:S(2)}) collective-permute-start(f32[1024,128]{1,0:T(8,128)S(1)} %get-tuple-element.48.refs_5_), channel_id=1, source_target_pairs={{0,16},{4,20},{8,24},{12,28},{16,0},{20,4},{24,8},{28,12},{1,17},{... | collective-permute-start | bytes 1572872 | tf_op jit(solution)/shard_map/ppermute | solution.py:20
  100.9 23.2 %collective-permute-start.26 = (f32[1024,128]{1,0:T(8,128)S(1)}, f32[1024,128]{1,0:T(8,128)S(1)}, u32[]{:S(2)}, u32[]{:S(2)}) collective-permute-start(f32[1024,128]{1,0:T(8,128)S(1)} %get-tuple-element.47.refs_0_), channel_id=1, source_target_pairs={{0,2},{1,3},{2,0},{3,1},{4,6},{5,7},{6,4},{7,5},{8,10},{9,11},{10,... | collective-permute-start | bytes 1572872 | tf_op jit(solution)/shard_map/ppermute | solution.py:20
  102.0 22.2 %collective-permute-start.25 = (f32[1024,128]{1,0:T(8,128)S(1)}, f32[1024,128]{1,0:T(8,128)S(1)}, u32[]{:S(2)}, u32[]{:S(2)}) collective-permute-start(f32[1024,128]{1,0:T(8,128)S(1)} %get-tuple-element.47.refs_0_), channel_id=1, source_target_pairs={{0,1},{1,0},{2,3},{3,2},{4,5},{5,4},{6,7},{7,6},{8,9},{9,8},{10,11... | collective-permute-start | bytes 1572872 | tf_op jit(solution)/shard_map/ppermute | solution.py:20
  124.2 1.9 %collective-permute-start.28 = (f32[1024,128]{1,0:T(8,128)S(1)}, f32[1024,128]{1,0:T(8,128)S(1)}, u32[]{:S(2)}, u32[]{:S(2)}) collective-permute-start(f32[1024,128]{1,0:T(8,128)S(1)} %collective-permute-done.26.refs_2_), channel_id=1, source_target_pairs={{0,1},{1,0},{2,3},{3,2},{4,5},{5,4},{6,7},{7,6},{8,9},{9,8},{10,11... | collective-permute-start | bytes 1572872 | tf_op jit(solution)/shard_map/ppermute | solution.py:20
  124.2 15.0 %collective-permute-start.31 = (f32[512,128]{1,0:T(8,128)S(1)}, f32[512,128]{1,0:T(8,128)S(1)}, u32[]{:S(2)}, u32[]{:S(2)}) collective-permute-start(f32[512,128]{1,0:T(8,128)S(1)} %shard_map.94), channel_id=1, source_target_pairs={{0,16},{4,20},{8,24},{12,28},{16,0},{20,4},{24,8},{28,12},{1,17},{... | collective-permute-start | bytes 786440 | tf_op jit(solution)/shard_map/ppermute | solution.py:20
  127.4 11.8 %collective-permute-start.30 = (f32[512,128]{1,0:T(8,128)S(1)}, f32[512,128]{1,0:T(8,128)S(1)}, u32[]{:S(2)}, u32[]{:S(2)}) collective-permute-start(f32[512,128]{1,0:T(8,128)S(1)} %shard_map.95.refs_6_.refs_0_), channel_id=1, source_target_pairs={{0,2},{1,3},{2,0},{3,1},{4,6},{5,7},{6,4},{7,5},{8,10},{9,11},{10,... | collective-permute-start | bytes 786440 | tf_op jit(solution)/shard_map/ppermute | solution.py:20
  128.5 12.0 %collective-permute-start.29 = (f32[512,128]{1,0:T(8,128)S(1)}, f32[512,128]{1,0:T(8,128)S(1)}, u32[]{:S(2)}, u32[]{:S(2)}) collective-permute-start(f32[512,128]{1,0:T(8,128)S(1)} %shard_map.95.refs_6_.refs_0_), channel_id=1, source_target_pairs={{0,1},{1,0},{2,3},{3,2},{4,5},{5,4},{6,7},{7,6},{8,9},{9,8},{10,11... | collective-permute-start | bytes 786440 | tf_op jit(solution)/shard_map/ppermute | solution.py:20
  (11 other events, 21.3 us)

commit v5 on v4

--- a/solution.py
+++ b/solution.py
@@ -214,11 +214,11 @@
     return kernel_call(body, place, [*both_shards, one, two], [2 * order], 2, after)[0]
 
 
-def slots_kernel(cycle_size, slot_count, counts, owner_row, rows_row, extra, out):
+def slots_kernel(cycle_size, slot_count, counts, names, extra, out):
     entries, width = extra.shape
     position = lax.broadcasted_iota(jnp.int32, (1, entries), 1)
     live = position < counts[0]
-    target = jnp.where(live, owner_row[...], cycle_size)
+    target = jnp.where(live, names[:1, :], cycle_size)
     blocks = lax.broadcasted_iota(jnp.int32, (cycle_size, entries), 0)
     owned = (blocks == target).astype(f32)
     before = lax.broadcasted_iota(jnp.int32, (entries, entries), 0)
@@ -229,7 +229,7 @@
     both = jnp.concatenate([high, low], axis=1)
     slots = lax.broadcasted_iota(jnp.int32, (slot_count, entries), 0)
     in_slot = (slots == rank).astype(f32)
-    mark_high, mark_low = halves(owned * (rows_row[...] + 1).astype(f32))
+    mark_high, mark_low = halves(owned * (names[1:2, :] + 1).astype(f32))
     to_slot = lambda mark: lax.dot_general(
         mark, in_slot.astype(bf16), (((1,), (1,)), ((), ())), preferred_element_type=f32
     )
@@ -263,14 +263,15 @@
     entries, width = extra.shape
     slot_count = 2 * entries // cycle_size
     rows = cycle_size * (slot_count + mark_rows)
+    names = jnp.concatenate([owners.reshape(1, entries), rows_in.reshape(1, entries)], axis=0)
     return pl.pallas_call(
         functools.partial(slots_kernel, cycle_size, slot_count),
         out_shape=jax.ShapeDtypeStruct((rows, width), f32),
-        in_specs=[in_smem] + [in_vmem] * 3,
+        in_specs=[in_smem] + [in_vmem] * 2,
         out_specs=in_vmem,
         compiler_params=compiler_params(24),
         cost_estimate=weight(0),
-    )(counts, owners.reshape(1, entries), rows_in.reshape(1, entries), extra)
+    )(counts, names, extra)
 
 
 def loaded(right_side, got, after):

time: 144 us -> 144 us (level)
  no operation moved by 1% of the time
where the time goes in v5:
time: 144 us; the launch traced here: 143 us
  waiting for transfers between devices  74.7 us (52%)
  starting transfers between devices  35 us (24%)
  Pallas kernels  28.3 us (20%)
  local copies, waits for them, and re-layouts  4.23 us (3%)
    ppermute x33, waiting for transfers between devices, send(): return lax.ppermute(value, axis, pairs)  74.7 us
    ppermute x33, starting transfers between devices, send(): return lax.ppermute(value, axis, pairs)  29 us
    pallas_call x14, Pallas kernels, kernel_call(): pl.pallas_call(kernel, out_shape=[jax.ShapeDtypeStruct((rows, width), f32...  26.1 us
    all_to_all x1, starting transfers between devices, on_device(): lax.all_to_all(slots.reshape(cycle_size, -1, slots.shape[1]), 'blk', spli...  5.96 us
    unnamed x18, local copies, waits for them, and re-layouts  4.23 us
  transfers between devices with their start and end apart: 34, of which 19 were waited for; matrix products, arithmetic and copies ran while one was open for 0% of the time, Pallas kernels for 16%

profile of v5, /device:TPU:0, one launch (start us, length us, event | category | flops | bytes accessed | tf_op | source)
XLA Modules:
  0.0 143.1 jit_solution(3106981871997242394)
XLA Ops:
  0.0 2.9 %collective-permute-start = (f32[512,128]{1,0:T(8,128)}, f32[512,128]{1,0:T(8,128)S(1)}, u32[]{:S(2)}, u32[]{:S(2)}) collective-permute-start(f32[512,128]{1,0:T(8,128)} %bitcast.12), channel_id=1, source_target_pairs={{0,2},{1,3},{2,0},{3,1},{4,6},{5,7},{6,4},{7,5},{8,10},{9,11},{10,... | collective-permute-start | bytes 786440 | tf_op jit(solution)/shard_map/ppermute | solution.py:20
  5.2 1.5 %shard_map.82.refs_2_ = f32[1088,128]{1,0:T(8,128)} custom-call(s32[1]{0:T(128)S(6)} %copy.9.counts, s32[2,512]{1,0:T(2,128)S(1)} %pad_add_fusion.names, f32[512,128]{1,0:T(8,128)S(1)} %copy-done.1), custom_call_target="tpu_custom_call" | custom-call | flops 1 | bytes 1 | tf_op jit(solution)/shard_map/pallas_call | solution.py:267
  6.8 6.0 %all-to-all-start = ((f32[8,136,128]{2,1,0:T(8,128)}), f32[8,136,128]{2,1,0:T(8,128)S(1)}, u32[]{:S(2)}, u32[]{:S(2)}) async-start(f32[8,136,128]{2,1,0:T(8,128)} %bitcast.7), calls=%async_computation | async-start | bytes 1114112 | tf_op jit(solution)/shard_map/all_to_all | solution.py:323
  15.9 2.9 %shard_map.84 = (f32[512,128]{1,0:T(8,128)S(1)}, f32[512,128]{1,0:T(8,128)}) custom-call(s32[2]{0:T(128)S(1)} %pad_add_fusion.1.place_ref, f32[512,128]{1,0:T(8,128)S(1)} %bitcast.14, f32[512,128]{1,0:T(8,128)S(1)} %collective-permute-done.4.refs_1_, f32[512,128]{1,0:T(8,128)S(1)} %collective-permute-done.refs_3_.refs_2_, ...), custom_call_target="tpu_custom_call" | custom-call | flops 1 | bytes 1 | tf_op jit(solution)/shard_map/pallas_call | solution.py:95
  18.9 2.0 %collective-permute-start.6 = (f32[512,128]{1,0:T(8,128)S(1)}, f32[512,128]{1,0:T(8,128)S(1)}, u32[]{:S(2)}, u32[]{:S(2)}) collective-permute-start(f32[512,128]{1,0:T(8,128)S(1)} %get-tuple-element.30._), channel_id=1, source_target_pairs={{0,4},{4,0},{8,12},{12,8},{16,20},{20,16},{24,28},{28,24},{1,5},{5... | collective-permute-start | bytes 786440 | tf_op jit(solution)/shard_map/ppermute | solution.py:20
  21.6 5.0 %collective-permute-done.2.refs_2_ = f32[1024,128]{1,0:T(8,128)S(1)} collective-permute-done((f32[1024,128]{1,0:T(8,128)S(1)}, f32[1024,128]{1,0:T(8,128)S(1)}, u32[]{:S(2)}, u32[]{:S(2)}) %collective-permute-start.2) | collective-permute-done | bytes 524320 | tf_op jit(solution)/shard_map/ppermute | solution.py:20
  26.6 1.7 %collective-permute-start.8 = (f32[512,128]{1,0:T(8,128)}, f32[512,128]{1,0:T(8,128)}, u32[]{:S(2)}, u32[]{:S(2)}) collective-permute-start(f32[512,128]{1,0:T(8,128)} %get-tuple-element.32), channel_id=1, source_target_pairs={{0,4},{4,0},{8,12},{12,8},{16,20},{20,16},{24,28},{28,24},{1,5},{5... | collective-permute-start | bytes 786440 | tf_op jit(solution)/shard_map/ppermute | solution.py:20
  28.9 1.9 %collective-permute-start.7 = (f32[512,128]{1,0:T(8,128)S(1)}, f32[512,128]{1,0:T(8,128)S(1)}, u32[]{:S(2)}, u32[]{:S(2)}) collective-permute-start(f32[512,128]{1,0:T(8,128)S(1)} %collective-permute-done.6.refs_5_), channel_id=1, source_target_pairs={{0,8},{4,28},{8,16},{12,4},{16,24},{20,12},{24,0},{28,20},{1,9},{5... | collective-permute-start | bytes 786440 | tf_op jit(solution)/shard_map/ppermute | solution.py:20
  33.4 1.7 %shard_map.86 = f32[512,128]{1,0:T(8,128)S(1)} custom-call(s32[2]{0:T(128)S(1)} %pad_add_fusion.1.place_ref, f32[512,128]{1,0:T(8,128)S(1)} %bitcast.15, f32[512,128]{1,0:T(8,128)S(1)} %collective-permute-done.4.refs_1_, f32[512,128]{1,0:T(8,128)S(1)} %collective-permute-done.refs_3_.refs_2_, f32[512,128]{1,0:T(8,128)S(1)} %collective-permute-done.5.refs_3_, ...), custom_call_target="tpu_custom_call" | custom-call | flops 1 | bytes 1 | tf_op jit(solution)/shard_map/pallas_call | solution.py:95
  35.6 1.7 %collective-permute-start.10 = (f32[512,128]{1,0:T(8,128)}, f32[512,128]{1,0:T(8,128)S(1)}, u32[]{:S(2)}, u32[]{:S(2)}) collective-permute-start(f32[512,128]{1,0:T(8,128)} %collective-permute-done.8.refs_6_), channel_id=1, source_target_pairs={{0,8},{4,28},{8,16},{12,4},{16,24},{20,12},{24,0},{28,20},{1,9},{5... | collective-permute-start | bytes 786440 | tf_op jit(solution)/shard_map/ppermute | solution.py:20
  38.7 1.8 %shard_map.87.refs_6_.refs_0_.refs_4_ = f32[512,128]{1,0:T(8,128)S(1)} custom-call(s32[2]{0:T(128)S(1)} %pad_add_fusion.1.place_ref, f32[1024,128]{1,0:T(8,128)S(1)} %shard_map.83.refs_4_.refs_0_, f32[1024,128]{1,0:T(8,128)S(1)} %collective-permute-done.1.refs_1_, f32[1024,128]{1,0:T(8,128)S(1)} %collective-permute-done.2.refs_2_, ...), custom_call_target="tpu_custom_call" | custom-call | flops 23000000512 | bytes 73800000 | tf_op jit(solution)/shard_map/pallas_call | solution.py:95
  43.1 2.5 %collective-permute-done.10.refs_4_ = f32[512,128]{1,0:T(8,128)S(1)} collective-permute-done((f32[512,128]{1,0:T(8,128)}, f32[512,128]{1,0:T(8,128)S(1)}, u32[]{:S(2)}, u32[]{:S(2)}) %collective-permute-start.10) | collective-permute-done | bytes 262176 | tf_op jit(solution)/shard_map/ppermute | solution.py:20
  45.6 1.8 %shard_map.88.refs_4_.refs_0_ = f32[1024,128]{1,0:T(8,128)S(1)} custom-call(s32[2]{0:T(128)S(1)} %pad_add_fusion.1.place_ref, f32[1024,128]{1,0:T(8,128)S(1)} %shard_map.83.refs_4_.refs_0_, f32[1024,128]{1,0:T(8,128)S(1)} %collective-permute-done.1.refs_1_, f32[1024,128]{1,0:T(8,128)S(1)} %collective-permute-done.2.refs_2_, ...), custom_call_target="tpu_custom_call" | custom-call | flops 1 | bytes 1 | tf_op jit(solution)/shard_map/pallas_call | solution.py:95
  50.2 2.3 %shard_map.89 = (f32[512,128]{1,0:T(8,128)S(1)}, f32[512,128]{1,0:T(8,128)S(1)}) custom-call(s32[2]{0:T(128)S(1)} %pad_add_fusion.1.place_ref, f32[512,128]{1,0:T(8,128)S(1)} %shard_map.87.refs_6_.refs_0_.refs_4_, f32[512,128]{1,0:T(8,128)S(1)} %collective-permute-done.13.refs_1_, f32[512,128]{1,0:T(8,128)S(1)} %collective-permute-done.9.refs_2_, ...), custom_call_target="tpu_custom_call" | custom-call | flops 1 | bytes 1 | tf_op jit(solution)/shard_map/pallas_call | solution.py:95
  52.5 1.5 %collective-permute-start.15 = (f32[512,128]{1,0:T(8,128)S(1)}, f32[512,128]{1,0:T(8,128)S(1)}, u32[]{:S(2)}, u32[]{:S(2)}) collective-permute-start(f32[512,128]{1,0:T(8,128)S(1)} %get-tuple-element.37.refs_6_), channel_id=1, source_target_pairs={{0,8},{4,12},{8,16},{12,20},{16,24},{20,28},{24,0},{28,4},{1,9},{5... | collective-permute-start | bytes 786440 | tf_op jit(solution)/shard_map/ppermute | solution.py:20
  54.0 2.5 %collective-permute-start.16 = (f32[512,128]{1,0:T(8,128)S(1)}, f32[512,128]{1,0:T(8,128)S(1)}, u32[]{:S(2)}, u32[]{:S(2)}) collective-permute-start(f32[512,128]{1,0:T(8,128)S(1)} %get-tuple-element.38.refs_5_), channel_id=1, source_target_pairs={{0,24},{4,28},{8,0},{12,4},{16,8},{20,12},{24,16},{28,20},{1,25},{... | collective-permute-start | bytes 786440 | tf_op jit(solution)/shard_map/ppermute | solution.py:20
  56.5 3.4 %collective-permute-done.18.refs_5_ = f32[512,128]{1,0:T(8,128)S(1)} collective-permute-done((f32[512,128]{1,0:T(8,128)S(1)}, f32[512,128]{1,0:T(8,128)S(1)}, u32[]{:S(2)}, u32[]{:S(2)}) %collective-permute-start.18) | collective-permute-done | bytes 262176 | tf_op jit(solution)/shard_map/ppermute | solution.py:20
  59.9 1.8 %shard_map.90.refs_4_.refs_8_ = f32[512,128]{1,0:T(8,128)S(1)} custom-call(s32[2]{0:T(128)S(1)} %pad_add_fusion.1.place_ref, f32[1024,128]{1,0:T(8,128)S(1)} %shard_map.83.refs_4_.refs_0_, f32[1024,128]{1,0:T(8,128)S(1)} %collective-permute-done.1.refs_1_, f32[1024,128]{1,0:T(8,128)S(1)} %collective-permute-done.2.refs_2_, ...), custom_call_target="tpu_custom_call" | custom-call | flops 23000000512 | bytes 73800000 | tf_op jit(solution)/shard_map/pallas_call | solution.py:95
  61.8 1.7 %shard_map.91 = (f32[1024,128]{1,0:T(8,128)S(1)}, f32[1024,128]{1,0:T(8,128)S(1)}) custom-call(s32[2]{0:T(128)S(1)} %pad_add_fusion.1.place_ref, f32[512,128]{1,0:T(8,128)S(1)} %shard_map.87.refs_6_.refs_0_.refs_4_, f32[512,128]{1,0:T(8,128)S(1)} %collective-permute-done.13.refs_1_, f32[512,128]{1,0:T(8,128)S(1)} %collective-permute-done.9.refs_2_, ...), custom_call_target="tpu_custom_call" | custom-call | flops 1 | bytes 1 | tf_op jit(solution)/shard_map/pallas_call | solution.py:95
  63.5 1.9 %collective-permute-done.15.refs_5_ = f32[512,128]{1,0:T(8,128)S(1)} collective-permute-done((f32[512,128]{1,0:T(8,128)S(1)}, f32[512,128]{1,0:T(8,128)S(1)}, u32[]{:S(2)}, u32[]{:S(2)}) %collective-permute-start.15) | collective-permute-done | bytes 262176 | tf_op jit(solution)/shard_map/ppermute | solution.py:20
  65.4 4.1 %collective-permute-done.16.refs_6_ = f32[512,128]{1,0:T(8,128)S(1)} collective-permute-done((f32[512,128]{1,0:T(8,128)S(1)}, f32[512,128]{1,0:T(8,128)S(1)}, u32[]{:S(2)}, u32[]{:S(2)}) %collective-permute-start.16) | collective-permute-done | bytes 262176 | tf_op jit(solution)/shard_map/ppermute | solution.py:20
  70.1 3.2 %collective-permute-start.24 = (f32[1024,128]{1,0:T(8,128)S(1)}, f32[1024,128]{1,0:T(8,128)S(1)}, u32[]{:S(2)}, u32[]{:S(2)}) collective-permute-start(f32[1024,128]{1,0:T(8,128)S(1)} %get-tuple-element.46), channel_id=1, source_target_pairs={{0,24},{4,28},{8,0},{12,4},{16,8},{20,12},{24,16},{28,20},{1,25},{... | collective-permute-start | bytes 1572872 | tf_op jit(solution)/shard_map/ppermute | solution.py:20
  75.9 7.0 %collective-permute-done.21.refs_6_.refs_2_ = f32[512,128]{1,0:T(8,128)S(1)} collective-permute-done((f32[512,128]{1,0:T(8,128)S(1)}, f32[512,128]{1,0:T(8,128)S(1)}, u32[]{:S(2)}, u32[]{:S(2)}) %collective-permute-start.21) | collective-permute-done | bytes 262176 | tf_op jit(solution)/shard_map/ppermute | solution.py:20
  82.9 3.2 %collective-permute-done.23.refs_9_ = f32[1024,128]{1,0:T(8,128)S(1)} collective-permute-done((f32[1024,128]{1,0:T(8,128)S(1)}, f32[1024,128]{1,0:T(8,128)S(1)}, u32[]{:S(2)}, u32[]{:S(2)}) %collective-permute-start.23) | collective-permute-done | bytes 524320 | tf_op jit(solution)/shard_map/ppermute | solution.py:20
  86.1 9.3 %collective-permute-done.24.refs_10_ = f32[1024,128]{1,0:T(8,128)S(1)} collective-permute-done((f32[1024,128]{1,0:T(8,128)S(1)}, f32[1024,128]{1,0:T(8,128)S(1)}, u32[]{:S(2)}, u32[]{:S(2)}) %collective-permute-start.24) | collective-permute-done | bytes 524320 | tf_op jit(solution)/shard_map/ppermute | solution.py:20
  95.4 3.3 %shard_map.93 = (f32[1024,128]{1,0:T(8,128)S(1)}, f32[512,128]{1,0:T(8,128)S(1)}, f32[1024,128]{1,0:T(8,128)S(1)}) custom-call(s32[2]{0:T(128)S(1)} %pad_add_fusion.1.place_ref, f32[1024,128]{1,0:T(8,128)S(1)} %shard_map.88.refs_4_.refs_0_, f32[1024,128]{1,0:T(8,128)S(1)} %collective-permute-done.11.refs_1_, ...), custom_call_target="tpu_custom_call" | custom-call | flops 1 | bytes 1 | tf_op jit(solution)/shard_map/pallas_call | solution.py:95
  98.7 2.2 %collective-permute-start.27 = (f32[1024,128]{1,0:T(8,128)S(1)}, f32[1024,128]{1,0:T(8,128)S(1)}, u32[]{:S(2)}, u32[]{:S(2)}) collective-permute-start(f32[1024,128]{1,0:T(8,128)S(1)} %get-tuple-element.48.refs_5_), channel_id=1, source_target_pairs={{0,16},{4,20},{8,24},{12,28},{16,0},{20,4},{24,8},{28,12},{1,17},{... | collective-permute-start | bytes 1572872 | tf_op jit(solution)/shard_map/ppermute | solution.py:20
  102.0 1.7 %shard_map.94 = f32[512,128]{1,0:T(8,128)S(1)} custom-call(s32[2]{0:T(128)S(1)} %pad_add_fusion.1.place_ref, f32[512,128]{1,0:T(8,128)S(1)} %shard_map.92.refs_4_.refs_0_, f32[512,128]{1,0:T(8,128)S(1)} %collective-permute-done.20.refs_5_.refs_1_, f32[512,128]{1,0:T(8,128)S(1)} %collective-permute-done.21.refs_6_.refs_2_, ...), custom_call_target="tpu_custom_call" | custom-call | flops 1 | bytes 1 | tf_op jit(solution)/shard_map/pallas_call | solution.py:95
  103.8 20.4 %collective-permute-done.27.refs_5_ = f32[1024,128]{1,0:T(8,128)S(1)} collective-permute-done((f32[1024,128]{1,0:T(8,128)S(1)}, f32[1024,128]{1,0:T(8,128)S(1)}, u32[]{:S(2)}, u32[]{:S(2)}) %collective-permute-start.27) | collective-permute-done | bytes 524320 | tf_op jit(solution)/shard_map/ppermute | solution.py:20
  124.2 1.9 %collective-permute-done.28.refs_3_ = f32[1024,128]{1,0:T(8,128)S(1)} collective-permute-done((f32[1024,128]{1,0:T(8,128)S(1)}, f32[1024,128]{1,0:T(8,128)S(1)}, u32[]{:S(2)}, u32[]{:S(2)}) %collective-permute-start.28) | collective-permute-done | bytes 524320 | tf_op jit(solution)/shard_map/ppermute | solution.py:20
  128.6 10.6 %collective-permute-done.31.refs_5_ = f32[512,128]{1,0:T(8,128)S(1)} collective-permute-done((f32[512,128]{1,0:T(8,128)S(1)}, f32[512,128]{1,0:T(8,128)S(1)}, u32[]{:S(2)}, u32[]{:S(2)}) %collective-permute-start.31) | collective-permute-done | bytes 262176 | tf_op jit(solution)/shard_map/ppermute | solution.py:20
  140.7 2.4 %shard_map.97 = f32[512,128]{1,0:T(8,128)} custom-call(s32[2]{0:T(128)S(1)} %pad_add_fusion.1.place_ref, f32[512,128]{1,0:T(8,128)S(1)} %shard_map.95.refs_6_.refs_0_, f32[512,128]{1,0:T(8,128)S(1)} %collective-permute-done.29.refs_1_, f32[512,128]{1,0:T(8,128)S(1)} %collective-permute-done.30.refs_2_, f32[512,128]{1,0:T(8,128)S(1)} %collective-permute-done.32.refs_3_, ...), custom_call_target="tpu_custom_call" | custom-call | flops 1 | bytes 1 | tf_op jit(solution)/shard_map/pallas_call | solution.py:95
  (72 shorter events, 24.3 us)
Async XLA Ops:
  0.0 12.8 %collective-permute-start = (f32[512,128]{1,0:T(8,128)}, f32[512,128]{1,0:T(8,128)S(1)}, u32[]{:S(2)}, u32[]{:S(2)}) collective-permute-start(f32[512,128]{1,0:T(8,128)} %bitcast.12), channel_id=1, source_target_pairs={{0,2},{1,3},{2,0},{3,1},{4,6},{5,7},{6,4},{7,5},{8,10},{9,11},{10,... | collective-permute-start | bytes 786440 | tf_op jit(solution)/shard_map/ppermute | solution.py:20
  6.8 22.2 %all-to-all-start = ((f32[8,136,128]{2,1,0:T(8,128)}), f32[8,136,128]{2,1,0:T(8,128)S(1)}, u32[]{:S(2)}, u32[]{:S(2)}) async-start(f32[8,136,128]{2,1,0:T(8,128)} %bitcast.7), calls=%async_computation | async-start | bytes 1114112 | tf_op jit(solution)/shard_map/all_to_all | solution.py:323
  13.4 13.2 %collective-permute-start.2 = (f32[1024,128]{1,0:T(8,128)S(1)}, f32[1024,128]{1,0:T(8,128)S(1)}, u32[]{:S(2)}, u32[]{:S(2)}) collective-permute-start(f32[1024,128]{1,0:T(8,128)S(1)} %shard_map.83.refs_4_.refs_0_), channel_id=1, source_target_pairs={{0,2},{1,3},{2,0},{3,1},{4,6},{5,7},{6,4},{7,5},{8,10},{9,11},{10,... | collective-permute-start | bytes 1572872 | tf_op jit(solution)/shard_map/ppermute | solution.py:20
  14.0 1.9 %collective-permute-start.5 = (f32[512,128]{1,0:T(8,128)S(1)}, f32[512,128]{1,0:T(8,128)S(1)}, u32[]{:S(2)}, u32[]{:S(2)}) collective-permute-start(f32[512,128]{1,0:T(8,128)S(1)} %collective-permute-done.refs_3_.refs_2_), channel_id=1, source_target_pairs={{0,1},{1,0},{2,3},{3,2},{4,5},{5,4},{6,7},{7,6},{8,9},{9,8},{10,11... | collective-permute-start | bytes 786440 | tf_op jit(solution)/shard_map/ppermute | solution.py:20
  18.9 10.0 %collective-permute-start.6 = (f32[512,128]{1,0:T(8,128)S(1)}, f32[512,128]{1,0:T(8,128)S(1)}, u32[]{:S(2)}, u32[]{:S(2)}) collective-permute-start(f32[512,128]{1,0:T(8,128)S(1)} %get-tuple-element.30._), channel_id=1, source_target_pairs={{0,4},{4,0},{8,12},{12,8},{16,20},{20,16},{24,28},{28,24},{1,5},{5... | collective-permute-start | bytes 786440 | tf_op jit(solution)/shard_map/ppermute | solution.py:20
  21.6 15.8 %collective-permute-start.1 = (f32[1024,128]{1,0:T(8,128)S(1)}, f32[1024,128]{1,0:T(8,128)S(1)}, u32[]{:S(2)}, u32[]{:S(2)}) collective-permute-start(f32[1024,128]{1,0:T(8,128)S(1)} %shard_map.83.refs_4_.refs_0_), channel_id=1, source_target_pairs={{0,1},{1,0},{2,3},{3,2},{4,5},{5,4},{6,7},{7,6},{8,9},{9,8},{10,11... | collective-permute-start | bytes 1572872 | tf_op jit(solution)/shard_map/ppermute | solution.py:20
  26.6 12.1 %collective-permute-start.3 = (f32[1024,128]{1,0:T(8,128)S(1)}, f32[1024,128]{1,0:T(8,128)}, u32[]{:S(2)}, u32[]{:S(2)}) collective-permute-start(f32[1024,128]{1,0:T(8,128)S(1)} %collective-permute-done.2.refs_2_), channel_id=1, source_target_pairs={{0,1},{1,0},{2,3},{3,2},{4,5},{5,4},{6,7},{7,6},{8,9},{9,8},{10,11... | collective-permute-start | bytes 1572872 | tf_op jit(solution)/shard_map/ppermute | solution.py:20
  26.6 9.0 %collective-permute-start.8 = (f32[512,128]{1,0:T(8,128)}, f32[512,128]{1,0:T(8,128)}, u32[]{:S(2)}, u32[]{:S(2)}) collective-permute-start(f32[512,128]{1,0:T(8,128)} %get-tuple-element.32), channel_id=1, source_target_pairs={{0,4},{4,0},{8,12},{12,8},{16,20},{20,16},{24,28},{28,24},{1,5},{5... | collective-permute-start | bytes 786440 | tf_op jit(solution)/shard_map/ppermute | solution.py:20
  28.9 9.8 %collective-permute-start.7 = (f32[512,128]{1,0:T(8,128)S(1)}, f32[512,128]{1,0:T(8,128)S(1)}, u32[]{:S(2)}, u32[]{:S(2)}) collective-permute-start(f32[512,128]{1,0:T(8,128)S(1)} %collective-permute-done.6.refs_5_), channel_id=1, source_target_pairs={{0,8},{4,28},{8,16},{12,4},{16,24},{20,12},{24,0},{28,20},{1,9},{5... | collective-permute-start | bytes 786440 | tf_op jit(solution)/shard_map/ppermute | solution.py:20
  35.6 9.9 %collective-permute-start.10 = (f32[512,128]{1,0:T(8,128)}, f32[512,128]{1,0:T(8,128)S(1)}, u32[]{:S(2)}, u32[]{:S(2)}) collective-permute-start(f32[512,128]{1,0:T(8,128)} %collective-permute-done.8.refs_6_), channel_id=1, source_target_pairs={{0,8},{4,28},{8,16},{12,4},{16,24},{20,12},{24,0},{28,20},{1,9},{5... | collective-permute-start | bytes 786440 | tf_op jit(solution)/shard_map/ppermute | solution.py:20
  40.6 7.2 %collective-permute-start.9 = (f32[512,128]{1,0:T(8,128)S(1)}, f32[512,128]{1,0:T(8,128)S(1)}, u32[]{:S(2)}, u32[]{:S(2)}) collective-permute-start(f32[512,128]{1,0:T(8,128)S(1)} %shard_map.87.refs_6_.refs_0_.refs_4_), channel_id=1, source_target_pairs={{0,2},{1,3},{2,0},{3,1},{4,6},{5,7},{6,4},{7,5},{8,10},{9,11},{10,... | collective-permute-start | bytes 786440 | tf_op jit(solution)/shard_map/ppermute | solution.py:20
  41.7 7.0 %collective-permute-start.17 = (f32[512,128]{1,0:T(8,128)S(1)}, f32[512,128]{1,0:T(8,128)S(1)}, u32[]{:S(2)}, u32[]{:S(2)}) collective-permute-start(f32[512,128]{1,0:T(8,128)S(1)} %shard_map.86), channel_id=1, source_target_pairs={{0,4},{4,0},{8,12},{12,8},{16,20},{20,16},{24,28},{28,24},{1,5},{5... | collective-permute-start | bytes 786440 | tf_op jit(solution)/shard_map/ppermute | solution.py:20
  43.1 7.1 %collective-permute-start.13 = (f32[512,128]{1,0:T(8,128)S(1)}, f32[512,128]{1,0:T(8,128)S(1)}, u32[]{:S(2)}, u32[]{:S(2)}) collective-permute-start(f32[512,128]{1,0:T(8,128)S(1)} %shard_map.87.refs_6_.refs_0_.refs_4_), channel_id=1, source_target_pairs={{0,1},{1,0},{2,3},{3,2},{4,5},{5,4},{6,7},{7,6},{8,9},{9,8},{10,11... | collective-permute-start | bytes 786440 | tf_op jit(solution)/shard_map/ppermute | solution.py:20
  47.8 2.5 %collective-permute-start.14 = (f32[512,128]{1,0:T(8,128)S(1)}, f32[512,128]{1,0:T(8,128)S(1)}, u32[]{:S(2)}, u32[]{:S(2)}) collective-permute-start(f32[512,128]{1,0:T(8,128)S(1)} %collective-permute-done.9.refs_2_), channel_id=1, source_target_pairs={{0,1},{1,0},{2,3},{3,2},{4,5},{5,4},{6,7},{7,6},{8,9},{9,8},{10,11... | collective-permute-start | bytes 786440 | tf_op jit(solution)/shard_map/ppermute | solution.py:20
  48.7 11.2 %collective-permute-start.18 = (f32[512,128]{1,0:T(8,128)S(1)}, f32[512,128]{1,0:T(8,128)S(1)}, u32[]{:S(2)}, u32[]{:S(2)}) collective-permute-start(f32[512,128]{1,0:T(8,128)S(1)} %collective-permute-done.17.refs_6_), channel_id=1, source_target_pairs={{0,8},{4,28},{8,16},{12,4},{16,24},{20,12},{24,0},{28,20},{1,9},{5... | collective-permute-start | bytes 786440 | tf_op jit(solution)/shard_map/ppermute | solution.py:20
  48.8 20.7 %collective-permute-start.12 = (f32[1024,128]{1,0:T(8,128)S(1)}, f32[1024,128]{1,0:T(8,128)S(1)}, u32[]{:S(2)}, u32[]{:S(2)}) collective-permute-start(f32[1024,128]{1,0:T(8,128)S(1)} %shard_map.88.refs_4_.refs_0_), channel_id=1, source_target_pairs={{0,2},{1,3},{2,0},{3,1},{4,6},{5,7},{6,4},{7,5},{8,10},{9,11},{10,... | collective-permute-start | bytes 1572872 | tf_op jit(solution)/shard_map/ppermute | solution.py:20
  52.5 12.9 %collective-permute-start.15 = (f32[512,128]{1,0:T(8,128)S(1)}, f32[512,128]{1,0:T(8,128)S(1)}, u32[]{:S(2)}, u32[]{:S(2)}) collective-permute-start(f32[512,128]{1,0:T(8,128)S(1)} %get-tuple-element.37.refs_6_), channel_id=1, source_target_pairs={{0,8},{4,12},{8,16},{12,20},{16,24},{20,28},{24,0},{28,4},{1,9},{5... | collective-permute-start | bytes 786440 | tf_op jit(solution)/shard_map/ppermute | solution.py:20
  54.0 15.5 %collective-permute-start.16 = (f32[512,128]{1,0:T(8,128)S(1)}, f32[512,128]{1,0:T(8,128)S(1)}, u32[]{:S(2)}, u32[]{:S(2)}) collective-permute-start(f32[512,128]{1,0:T(8,128)S(1)} %get-tuple-element.38.refs_5_), channel_id=1, source_target_pairs={{0,24},{4,28},{8,0},{12,4},{16,8},{20,12},{24,16},{28,20},{1,25},{... | collective-permute-start | bytes 786440 | tf_op jit(solution)/shard_map/ppermute | solution.py:20
  61.7 11.6 %collective-permute-start.11 = (f32[1024,128]{1,0:T(8,128)S(1)}, f32[1024,128]{1,0:T(8,128)S(1)}, u32[]{:S(2)}, u32[]{:S(2)}) collective-permute-start(f32[1024,128]{1,0:T(8,128)S(1)} %shard_map.88.refs_4_.refs_0_), channel_id=1, source_target_pairs={{0,1},{1,0},{2,3},{3,2},{4,5},{5,4},{6,7},{7,6},{8,9},{9,8},{10,11... | collective-permute-start | bytes 1572872 | tf_op jit(solution)/shard_map/ppermute | solution.py:20
  69.5 3.8 %collective-permute-start.19 = (f32[1024,128]{1,0:T(8,128)S(1)}, f32[1024,128]{1,0:T(8,128)S(1)}, u32[]{:S(2)}, u32[]{:S(2)}) collective-permute-start(f32[1024,128]{1,0:T(8,128)S(1)} %collective-permute-done.12.refs_2_), channel_id=1, source_target_pairs={{0,1},{1,0},{2,3},{3,2},{4,5},{5,4},{6,7},{7,6},{8,9},{9,8},{10,11... | collective-permute-start | bytes 1572872 | tf_op jit(solution)/shard_map/ppermute | solution.py:20
  69.5 16.6 %collective-permute-start.23 = (f32[1024,128]{1,0:T(8,128)S(1)}, f32[1024,128]{1,0:T(8,128)S(1)}, u32[]{:S(2)}, u32[]{:S(2)}) collective-permute-start(f32[1024,128]{1,0:T(8,128)S(1)} %get-tuple-element.45), channel_id=1, source_target_pairs={{0,8},{4,12},{8,16},{12,20},{16,24},{20,28},{24,0},{28,4},{1,9},{5... | collective-permute-start | bytes 1572872 | tf_op jit(solution)/shard_map/ppermute | solution.py:20
  70.1 25.3 %collective-permute-start.24 = (f32[1024,128]{1,0:T(8,128)S(1)}, f32[1024,128]{1,0:T(8,128)S(1)}, u32[]{:S(2)}, u32[]{:S(2)}) collective-permute-start(f32[1024,128]{1,0:T(8,128)S(1)} %get-tuple-element.46), channel_id=1, source_target_pairs={{0,24},{4,28},{8,0},{12,4},{16,8},{20,12},{24,16},{28,20},{1,25},{... | collective-permute-start | bytes 1572872 | tf_op jit(solution)/shard_map/ppermute | solution.py:20
  74.7 8.2 %collective-permute-start.21 = (f32[512,128]{1,0:T(8,128)S(1)}, f32[512,128]{1,0:T(8,128)S(1)}, u32[]{:S(2)}, u32[]{:S(2)}) collective-permute-start(f32[512,128]{1,0:T(8,128)S(1)} %shard_map.92.refs_4_.refs_0_), channel_id=1, source_target_pairs={{0,2},{1,3},{2,0},{3,1},{4,6},{5,7},{6,4},{7,5},{8,10},{9,11},{10,... | collective-permute-start | bytes 786440 | tf_op jit(solution)/shard_map/ppermute | solution.py:20
  75.9 19.5 %collective-permute-start.20 = (f32[512,128]{1,0:T(8,128)S(1)}, f32[512,128]{1,0:T(8,128)S(1)}, u32[]{:S(2)}, u32[]{:S(2)}) collective-permute-start(f32[512,128]{1,0:T(8,128)S(1)} %shard_map.92.refs_4_.refs_0_), channel_id=1, source_target_pairs={{0,1},{1,0},{2,3},{3,2},{4,5},{5,4},{6,7},{7,6},{8,9},{9,8},{10,11... | collective-permute-start | bytes 786440 | tf_op jit(solution)/shard_map/ppermute | solution.py:20
  82.9 12.5 %collective-permute-start.22 = (f32[512,128]{1,0:T(8,128)S(1)}, f32[512,128]{1,0:T(8,128)S(1)}, u32[]{:S(2)}, u32[]{:S(2)}) collective-permute-start(f32[512,128]{1,0:T(8,128)S(1)} %collective-permute-done.21.refs_6_.refs_2_), channel_id=1, source_target_pairs={{0,1},{1,0},{2,3},{3,2},{4,5},{5,4},{6,7},{7,6},{8,9},{9,8},{10,11... | collective-permute-start | bytes 786440 | tf_op jit(solution)/shard_map/ppermute | solution.py:20
  98.7 25.4 %collective-permute-start.27 = (f32[1024,128]{1,0:T(8,128)S(1)}, f32[1024,128]{1,0:T(8,128)S(1)}, u32[]{:S(2)}, u32[]{:S(2)}) collective-permute-start(f32[1024,128]{1,0:T(8,128)S(1)} %get-tuple-element.48.refs_5_), channel_id=1, source_target_pairs={{0,16},{4,20},{8,24},{12,28},{16,0},{20,4},{24,8},{28,12},{1,17},{... | collective-permute-start | bytes 1572872 | tf_op jit(solution)/shard_map/ppermute | solution.py:20
  100.9 23.2 %collective-permute-start.26 = (f32[1024,128]{1,0:T(8,128)S(1)}, f32[1024,128]{1,0:T(8,128)S(1)}, u32[]{:S(2)}, u32[]{:S(2)}) collective-permute-start(f32[1024,128]{1,0:T(8,128)S(1)} %get-tuple-element.47.refs_0_), channel_id=1, source_target_pairs={{0,2},{1,3},{2,0},{3,1},{4,6},{5,7},{6,4},{7,5},{8,10},{9,11},{10,... | collective-permute-start | bytes 1572872 | tf_op jit(solution)/shard_map/ppermute | solution.py:20
  102.0 22.2 %collective-permute-start.25 = (f32[1024,128]{1,0:T(8,128)S(1)}, f32[1024,128]{1,0:T(8,128)S(1)}, u32[]{:S(2)}, u32[]{:S(2)}) collective-permute-start(f32[1024,128]{1,0:T(8,128)S(1)} %get-tuple-element.47.refs_0_), channel_id=1, source_target_pairs={{0,1},{1,0},{2,3},{3,2},{4,5},{5,4},{6,7},{7,6},{8,9},{9,8},{10,11... | collective-permute-start | bytes 1572872 | tf_op jit(solution)/shard_map/ppermute | solution.py:20
  124.2 1.9 %collective-permute-start.28 = (f32[1024,128]{1,0:T(8,128)S(1)}, f32[1024,128]{1,0:T(8,128)S(1)}, u32[]{:S(2)}, u32[]{:S(2)}) collective-permute-start(f32[1024,128]{1,0:T(8,128)S(1)} %collective-permute-done.26.refs_2_), channel_id=1, source_target_pairs={{0,1},{1,0},{2,3},{3,2},{4,5},{5,4},{6,7},{7,6},{8,9},{9,8},{10,11... | collective-permute-start | bytes 1572872 | tf_op jit(solution)/shard_map/ppermute | solution.py:20
  124.2 15.0 %collective-permute-start.31 = (f32[512,128]{1,0:T(8,128)S(1)}, f32[512,128]{1,0:T(8,128)S(1)}, u32[]{:S(2)}, u32[]{:S(2)}) collective-permute-start(f32[512,128]{1,0:T(8,128)S(1)} %shard_map.94), channel_id=1, source_target_pairs={{0,16},{4,20},{8,24},{12,28},{16,0},{20,4},{24,8},{28,12},{1,17},{... | collective-permute-start | bytes 786440 | tf_op jit(solution)/shard_map/ppermute | solution.py:20
  127.4 11.8 %collective-permute-start.30 = (f32[512,128]{1,0:T(8,128)S(1)}, f32[512,128]{1,0:T(8,128)S(1)}, u32[]{:S(2)}, u32[]{:S(2)}) collective-permute-start(f32[512,128]{1,0:T(8,128)S(1)} %shard_map.95.refs_6_.refs_0_), channel_id=1, source_target_pairs={{0,2},{1,3},{2,0},{3,1},{4,6},{5,7},{6,4},{7,5},{8,10},{9,11},{10,... | collective-permute-start | bytes 786440 | tf_op jit(solution)/shard_map/ppermute | solution.py:20
  128.6 12.0 %collective-permute-start.29 = (f32[512,128]{1,0:T(8,128)S(1)}, f32[512,128]{1,0:T(8,128)S(1)}, u32[]{:S(2)}, u32[]{:S(2)}) collective-permute-start(f32[512,128]{1,0:T(8,128)S(1)} %shard_map.95.refs_6_.refs_0_), channel_id=1, source_target_pairs={{0,1},{1,0},{2,3},{3,2},{4,5},{5,4},{6,7},{7,6},{8,9},{9,8},{10,11... | collective-permute-start | bytes 786440 | tf_op jit(solution)/shard_map/ppermute | solution.py:20
  (11 other events, 21.3 us)
